TPU v7x, 32 devices: a whole 2x2x4 slice. The times are simulated.
32 devices in a mesh: pipe: 4 (over y, x), expert: 8 (over z, core).
Axes of the slice: x: 2, y: 2, z: 4, core: 2. Of those that a mesh axis runs over, the one named last changes fastest.
Arguments:
- hidden_in: bfloat16 [4, 1024, 4096], P('pipe', 'expert'), may hold values from -90 to 90
- out_grad: bfloat16 [4, 1024, 4096], P('pipe', 'expert'), may hold values from -6 to 6
- expert_ids: int32 [4, 1024, 8], P('pipe', 'expert'), may hold values from 0 to 127, as said below
- route_weight: bfloat16 [4, 1024, 8], P('pipe', 'expert'), may hold values from 0.25 to 1
- norm_gain: float32 [4, 4096], P('pipe'), may hold values from 0.25 to 1.75
- w_gate_up: bfloat16 [4, 8, 2, 192, 4096], P('pipe', 'expert'), may hold values from -0.09375 to 0.09375
- w_down: bfloat16 [4, 8, 192, 4096], P('pipe', 'expert'), may hold values from -0.15625 to 0.15625
Outputs:
- handed_grad: bfloat16 [4, 1024, 4096], P('pipe', 'expert')
- grad_gate_up: bfloat16 [4, 8, 2, 192, 4096], P('pipe', 'expert')
- grad_down: bfloat16 [4, 8, 192, 4096], P('pipe', 'expert')
- grad_combine: float32 [4, 1024, 8], P('pipe', 'expert')
Inputs may be any that keep to these rules, and one draw needn't show every extreme that they name: `expert_ids`: each token names 8 different experts. In each layer, at most 8 tokens of one aligned block of 128 tokens name any one of the experts 0 to 0, and one of these experts is named by exactly 8 tokens of every block.
All inputs are finite; a program needn't handle non-finite values.
Results may differ from a plain program's by a relative error of at most 0.008.
Values may be sent and summed in bfloat16 or wider, within the bound.
No kernel may reach another device: no remote copies, remote signals or barrier semaphores. Data moves between devices by JAX's collectives and lax.ppermute only.
A program may use at most 128 MiB of HBM per device.

v0:
```python
import jax
import jax.numpy as jnp
from jax import lax
from jax.sharding import PartitionSpec as P

SPLIT = 8
SPECIALIST_CAP = 8


def shifted(block, axis, distance):
    devices = range(lax.axis_size(axis))
    route = [((i - distance) % len(devices), i) for i in devices]
    return lax.ppermute(block, axis, route)


def rows_product(left_rows, right_rows):
    return lax.dot_general(
        left_rows, right_rows, (((1,), (1,)), ((), ())), preferred_element_type=jnp.float32
    )


def column_product(left_rows, right_rows):
    return lax.dot_general(
        left_rows, right_rows, (((0,), (0,)), ((), ())), preferred_element_type=jnp.float32
    )


def on_device(hidden_in, out_grad, expert_ids, route_weight, norm_gain, w_gate_up, w_down):
    tokens_in = hidden_in[0]
    grad_out = out_grad[0]
    chosen = expert_ids[0]
    weights_in = route_weight[0]
    gain_row = norm_gain[0]
    slab_gate_up = w_gate_up[0, 0]
    slab_down = w_down[0, 0]
    devices = lax.axis_size("expert")
    specialist_span = devices // SPLIT
    model_width = tokens_in.shape[1]
    hidden_slab = slab_down.shape[0]
    capacity = SPECIALIST_CAP
    tokens_f = tokens_in.astype(jnp.float32)
    rms_value = jnp.sqrt(jnp.mean(tokens_f * tokens_f, axis=-1, keepdims=True) + 1e-06)
    normed = tokens_f / rms_value
    normed_in = (normed * gain_row).astype(jnp.bfloat16)
    expert_range = jnp.arange(specialist_span, dtype=jnp.int32)
    picked = chosen[:, :, None] == expert_range[None, None, :]
    member = jnp.any(picked, axis=1).astype(jnp.int32)
    weight_te = jnp.sum(jnp.where(picked, weights_in.astype(jnp.float32)[:, :, None], 0.0), axis=1)
    position = jnp.cumsum(member, axis=0) - member
    slot_range = jnp.arange(capacity, dtype=jnp.int32)
    placing = (position.T[:, None, :] == slot_range[None, :, None]) & (member.T[:, None, :] == 1)
    place_bf = placing.astype(jnp.bfloat16)
    place_f = placing.astype(jnp.float32)
    sent_in = jnp.einsum(
        "wst,td->wsd", place_bf, normed_in, preferred_element_type=jnp.float32
    ).astype(jnp.bfloat16)
    sent_grad = jnp.einsum(
        "wst,td->wsd", place_bf, grad_out, preferred_element_type=jnp.float32
    ).astype(jnp.bfloat16)
    sent_weight = jnp.sum(place_f * weight_te.T[:, None, :], axis=-1).astype(jnp.bfloat16)
    rows_in, rows_grad, rows_weight = (
        lax.all_to_all(
            jnp.repeat(sent_in, SPLIT, axis=0), "expert", split_axis=0, concat_axis=0, tiled=True
        ),
        lax.all_to_all(
            jnp.repeat(sent_grad, SPLIT, axis=0), "expert", split_axis=0, concat_axis=0, tiled=True
        ),
        lax.all_to_all(
            jnp.repeat(sent_weight, SPLIT, axis=0),
            "expert",
            split_axis=0,
            concat_axis=0,
            tiled=True,
        ),
    )
    total_rows = devices * capacity
    flat_in = rows_in.reshape(total_rows, model_width)
    flat_grad = rows_grad.reshape(total_rows, model_width)
    flat_weight = rows_weight.reshape(total_rows, 1).astype(jnp.float32)
    joined_slab = slab_gate_up.reshape(2 * hidden_slab, model_width)
    projected = rows_product(flat_in, joined_slab)
    gate_pre = projected[:, :hidden_slab]
    up_pre = projected[:, hidden_slab:]
    sigmoid_gate = jax.nn.sigmoid(gate_pre)
    active = gate_pre * sigmoid_gate
    hidden_act = active * up_pre
    scaled_hidden = (flat_weight * hidden_act).astype(jnp.bfloat16)
    back_proj = rows_product(flat_grad, slab_down)
    grad_hidden = flat_weight * back_proj
    grad_gate = (
        grad_hidden * up_pre * sigmoid_gate * (1.0 + gate_pre * (1.0 - sigmoid_gate))
    ).astype(jnp.bfloat16)
    grad_up = (grad_hidden * active).astype(jnp.bfloat16)
    grad_both = jnp.concatenate([grad_gate, grad_up], axis=1)
    weight_grad = column_product(grad_both, flat_in)
    down_grad = column_product(scaled_hidden, flat_grad)
    input_part = (
        jnp.dot(grad_both, joined_slab, preferred_element_type=jnp.float32)
        .astype(jnp.bfloat16)
        .reshape(devices, capacity, model_width)
    )
    combine_part = (
        jnp.sum(hidden_act * back_proj, axis=-1).astype(jnp.bfloat16).reshape(devices, capacity)
    )
    returned_in, returned_comb = (
        lax.all_to_all(input_part, "expert", split_axis=0, concat_axis=0, tiled=True),
        lax.all_to_all(combine_part, "expert", split_axis=0, concat_axis=0, tiled=True),
    )
    summed_in = jnp.sum(
        returned_in.reshape(specialist_span, SPLIT, capacity, model_width).astype(jnp.float32),
        axis=1,
    )
    summed_comb = jnp.sum(
        returned_comb.reshape(specialist_span, SPLIT, capacity).astype(jnp.float32), axis=1
    )
    grad_normed = jnp.einsum("wst,wsd->td", place_f, summed_in, precision=lax.Precision.HIGHEST)
    comb_te = jnp.sum(place_f * summed_comb[:, :, None], axis=1)
    grad_combine = jnp.sum(jnp.where(picked, comb_te.T[:, None, :], 0.0), axis=-1)
    scaled = grad_normed * gain_row
    inner_mean = jnp.mean(scaled * normed, axis=-1, keepdims=True)
    grad_tokens = (
        grad_out.astype(jnp.float32) + (scaled - normed * inner_mean) / rms_value
    ).astype(jnp.bfloat16)
    handed = shifted(grad_tokens, "pipe", -1)
    gate_up_out = weight_grad.reshape(2, hidden_slab, model_width).astype(jnp.bfloat16)
    return (
        handed[None],
        gate_up_out[None, None],
        down_grad.astype(jnp.bfloat16)[None, None],
        grad_combine[None],
    )


def solution(mesh):
    return jax.shard_map(
        on_device,
        mesh=mesh,
        in_specs=(
            P("pipe", "expert", None),
            P("pipe", "expert", None),
            P("pipe", "expert", None),
            P("pipe", "expert", None),
            P("pipe", None),
            P("pipe", "expert", None, None, None),
            P("pipe", "expert", None, None),
        ),
        out_specs=(
            P("pipe", "expert", None),
            P("pipe", "expert", None, None, None),
            P("pipe", "expert", None, None),
            P("pipe", "expert", None),
        ),
        check_vma=False,
    )
```

profile of v0, /device:TPU:0, one launch (start us, length us, event | category | flops | bytes accessed | tf_op | source)
XLA Modules:
  0.0 115.5 jit_solution(10255002716128585023)
XLA Ops:
  0.6 1.7 %fusion.5 = f32[128]{0:T(128)S(1)} fusion(bf16[1,128,4096]{2,1,0:T(8,128)(2,1)} %param.7), kind=kLoop, calls=%fused_computation.13 | loop fusion | flops 1572736 | bytes 1049088 | tf_op jit(solution)/shard_map/reduce_sum | solution.py:42
  2.3 0.7 select_reduce_fusion.2
  3.1 0.1 copy.18
  3.2 0.2 reduce-window.7
  3.4 0.1 reduce.10
  3.5 1.7 %convolution_convert_fusion.3 = bf16[8,4096]{1,0:T(8,128)(2,1)S(1)} fusion(bf16[1,128,4096]{2,1,0:T(8,128)(2,1)} %param.7, f32[4096]{0:T(1024)} %bitcast.58, f32[128]{0:T(128)S(1)} %add_sqrt_fusion, s32[128]{0:T(128)S(1)} %convert_subtract_fusion, pred[128]{0:T(512)(128)(4,1)S(1)} %get-tuple-element.10), kind=kOutput, calls=%fused_computation.7 | convolution fusion | flops 10520576 | bytes 1131648 | tf_op jit(solution)/shard_map/wst,td->wsd/dot_general | solution.py:54
  5.1 0.8 reshape.430
  6.0 6.3 %all-to-all-start.2 = ((bf16[8,8,4096]{2,1,0:T(8,128)(2,1)}), bf16[8,8,4096]{2,1,0:T(8,128)(2,1)}, u32[]{:S(2)}, u32[]{:S(2)}) async-start(bf16[8,8,4096]{2,1,0:T(8,128)(2,1)} %reshape.430), calls=%async_computation.2 | async-start | bytes 1048576 | tf_op jit(solution)/shard_map/all_to_all | solution.py:62
  12.3 1.5 %convolution_convert_fusion.4 = bf16[8,4096]{1,0:T(8,128)(2,1)S(1)} fusion(bf16[1,128,4096]{2,1,0:T(8,128)(2,1)} %param.8, s32[128]{0:T(128)S(1)} %convert_subtract_fusion, pred[128]{0:T(512)(128)(4,1)S(1)} %get-tuple-element.10), kind=kOutput, calls=%fused_computation.8 | convolution fusion | flops 8423424 | bytes 1114752 | tf_op jit(solution)/shard_map/wst,td->wsd/dot_general | solution.py:57
  13.8 14.0 %all-to-all-done.2 = bf16[8,8,4096]{2,1,0:T(8,128)(2,1)} async-done(((bf16[8,8,4096]{2,1,0:T(8,128)(2,1)}), bf16[8,8,4096]{2,1,0:T(8,128)(2,1)}, u32[]{:S(2)}, u32[]{:S(2)}) %all-to-all-start.2) | async-done | bytes 524320 | tf_op jit(solution)/shard_map/all_to_all | solution.py:62
  27.8 0.8 reshape.428
  28.6 4.1 %all-to-all-start.1 = ((bf16[8,8,4096]{2,1,0:T(8,128)(2,1)}), bf16[8,8,4096]{2,1,0:T(8,128)(2,1)}, u32[]{:S(2)}, u32[]{:S(2)}) async-start(bf16[8,8,4096]{2,1,0:T(8,128)(2,1)} %reshape.428), calls=%async_computation.1 | async-start | bytes 1048576 | tf_op jit(solution)/shard_map/all_to_all | solution.py:65
  32.8 2.1 %fusion.14 = f32[64,384]{1,0:T(8,128)S(1)} fusion(bf16[384,4096]{1,0:T(8,128)(2,1)S(1)} %bitcast.56, bf16[8,8,4096]{2,1,0:T(8,128)(2,1)} %all-to-all-done.2), kind=kOutput, calls=%fused_computation.24 | convolution fusion | flops 201326592 | bytes 3768320 | tf_op jit(solution)/shard_map/dot_general | solution.py:17
  34.9 13.2 %all-to-all-done.1 = bf16[8,8,4096]{2,1,0:T(8,128)(2,1)} async-done(((bf16[8,8,4096]{2,1,0:T(8,128)(2,1)}), bf16[8,8,4096]{2,1,0:T(8,128)(2,1)}, u32[]{:S(2)}, u32[]{:S(2)}) %all-to-all-start.1) | async-done | bytes 524320 | tf_op jit(solution)/shard_map/all_to_all | solution.py:65
  48.1 2.3 %multiply_reduce_fusion.1 = (bf16[64]{0:T(256)(128)(2,1)S(1)}, f32[64,192]{1,0:T(8,128)S(1)}) fusion(f32[64,384]{1,0:T(8,128)S(1)} %fusion.14, bf16[1,1,192,4096]{3,2,1,0:T(8,128)(2,1)} %param.13, bf16[8,8,4096]{2,1,0:T(8,128)(2,1)} %all-to-all-done.1), kind=kOutput, calls=%fused_computation.29 | convolution fusion | flops 100749248 | bytes 2244736 | tf_op jit(solution)/shard_map/dot_general | solution.py:17
  50.4 0.1 convert_element_type.163
  50.5 7.9 %all_to_all.27 = bf16[8,1,8]{2,1,0:T(2,128)(2,1)S(1)} all-to-all(bf16[8,1,8]{2,1,0:T(2,128)(2,1)S(1)} %convert_element_type.163), channel_id=1, replica_groups=mesh['pipe'=4,'expert'=8] {'expert'}, dimensions={0} | all-to-all | bytes 256 | tf_op jit(solution)/shard_map/all_to_all | solution.py:107
  58.5 0.1 select_reduce_fusion
  58.6 7.9 %all_to_all.28 = bf16[8,1,8]{2,1,0:T(2,128)(2,1)S(1)} all-to-all(bf16[8,1,8]{2,1,0:T(2,128)(2,1)S(1)} %reshape.427), channel_id=1, replica_groups=mesh['pipe'=4,'expert'=8] {'expert'}, dimensions={0} | all-to-all | bytes 256 | tf_op jit(solution)/shard_map/all_to_all | solution.py:68
  66.6 0.1 multiply_convert_fusion.2
  66.8 0.7 fusion.2
  67.5 17.8 %all_to_all.29 = bf16[8,8,4096]{2,1,0:T(8,128)(2,1)S(1)} all-to-all(bf16[8,8,4096]{2,1,0:T(8,128)(2,1)S(1)} %fusion.2), channel_id=1, replica_groups=mesh['pipe'=4,'expert'=8] {'expert'}, dimensions={0} | all-to-all | bytes 1048576 | tf_op jit(solution)/shard_map/all_to_all | solution.py:106
  85.4 1.4 %multiply_reduce_fusion = (f32[128]{0:T(128)S(1)}, f32[128,4096]{1,0:T(8,128)S(1)}) fusion(bf16[1,128,4096]{2,1,0:T(8,128)(2,1)S(1)} %copy-done.2, f32[128]{0:T(128)S(1)} %add_sqrt_fusion, f32[4096]{0:T(1024)S(1)} %bitcast.59, f32[8,4096]{1,0:T(8,128)S(1)} %convert_reduce_fusion, s32[128]{0:T(128)S(1)} %convert_subtract_fusion, ...), kind=kOutput, calls=%fused_computation.17 | convolution fusion | flops 52955008 | bytes 3294848 | tf_op jit(solution)/shard_map/wst,wsd->td/dot_general | solution.py:116
  86.8 1.6 %add_convert_fusion = bf16[128,4096]{1,0:T(8,128)(2,1)} fusion(f32[128,4096]{1,0:T(8,128)S(1)} %get-tuple-element.15, bf16[1,128,4096]{2,1,0:T(8,128)(2,1)S(1)} %copy-done.2, bf16[1,128,4096]{2,1,0:T(8,128)(2,1)S(1)} %copy-done.1, f32[128]{0:T(128)S(1)} %broadcast_multiply_fusion, f32[128]{0:T(128)S(1)} %add_sqrt_fusion), kind=kLoop, calls=%fused_computation.16 | loop fusion | flops 4194304 | bytes 5243904 | tf_op jit(solution)/shard_map/convert_element_type | solution.py:123
  88.4 2.4 %collective-permute-start = (bf16[128,4096]{1,0:T(8,128)(2,1)}, bf16[128,4096]{1,0:T(8,128)(2,1)}, u32[]{:S(2)}, u32[]{:S(2)}) collective-permute-start(bf16[128,4096]{1,0:T(8,128)(2,1)} %add_convert_fusion), channel_id=1, source_target_pairs={{8,0},{16,8},{24,16},{0,24},{9,1},{17,9},{25,17},{1,25},{10,2},{18... | collective-permute-start | bytes 3145736 | tf_op jit(solution)/shard_map/ppermute | solution.py:13
  90.8 0.6 broadcast_select_fusion
  91.4 0.1 fusion.21
  91.5 0.1 dot_general.35
  91.6 2.9 %fusion.1 = bf16[1,1,192,4096]{3,2,1,0:T(8,128)(2,1)} fusion(bf16[8,8,4096]{2,1,0:T(8,128)(2,1)} %all-to-all-done.1, f32[64]{0:T(128)S(1)} %reshape.434, f32[64,384]{1,0:T(8,128)S(1)} %fusion.14), kind=kOutput, calls=%fused_computation.4 | convolution fusion | flops 101535744 | bytes 2228736 | tf_op jit(solution)/shard_map/dot_general | solution.py:23
  94.5 3.7 %fusion = bf16[1,1,2,192,4096]{4,3,2,1,0:T(8,128)(2,1)} fusion(bf16[8,8,4096]{2,1,0:T(8,128)(2,1)} %all-to-all-done.2, bf16[2,192,64]{1,0,2:T(2,128)(2,1)S(1)} %dot_general.35), kind=kOutput, calls=%fused_computation.1 | convolution fusion | flops 202899456 | bytes 3719168 | tf_op jit(solution)/shard_map/dot_general | solution.py:23
  98.2 15.1 %collective-permute-done = bf16[128,4096]{1,0:T(8,128)(2,1)} collective-permute-done((bf16[128,4096]{1,0:T(8,128)(2,1)}, bf16[128,4096]{1,0:T(8,128)(2,1)}, u32[]{:S(2)}, u32[]{:S(2)}) %collective-permute-start) | collective-permute-done | bytes 1048608 | tf_op jit(solution)/shard_map/ppermute | solution.py:13
  113.2 2.3 %copy.24 = bf16[1,128,4096]{2,1,0:T(8,128)(2,1)} copy(bf16[1,128,4096]{2,1,0:T(8,128)(2,1)} %bitcast.10) | data formatting | bytes 2097152
  (18 shorter events, 0.3 us)
Async XLA Ops:
  0.6 32.1 %copy-start = (bf16[1,1,2,192,4096]{4,3,2,1,0:T(8,128)(2,1)S(1)}, bf16[1,1,2,192,4096]{4,3,2,1,0:T(8,128)(2,1)}, u32[]{:S(2)}) copy-start(bf16[1,1,2,192,4096]{4,3,2,1,0:T(8,128)(2,1)} %param.12) | copy-start | bytes 9437188
  6.0 21.8 %all-to-all-start.2 = ((bf16[8,8,4096]{2,1,0:T(8,128)(2,1)}), bf16[8,8,4096]{2,1,0:T(8,128)(2,1)}, u32[]{:S(2)}, u32[]{:S(2)}) async-start(bf16[8,8,4096]{2,1,0:T(8,128)(2,1)} %reshape.430), calls=%async_computation.2 | async-start | bytes 1048576 | tf_op jit(solution)/shard_map/all_to_all | solution.py:62
  28.6 19.5 %all-to-all-start.1 = ((bf16[8,8,4096]{2,1,0:T(8,128)(2,1)}), bf16[8,8,4096]{2,1,0:T(8,128)(2,1)}, u32[]{:S(2)}, u32[]{:S(2)}) async-start(bf16[8,8,4096]{2,1,0:T(8,128)(2,1)} %reshape.428), calls=%async_computation.1 | async-start | bytes 1048576 | tf_op jit(solution)/shard_map/all_to_all | solution.py:65
  66.7 18.6 %copy-start.2 = (bf16[1,128,4096]{2,1,0:T(8,128)(2,1)S(1)}, bf16[1,128,4096]{2,1,0:T(8,128)(2,1)}, u32[]{:S(2)}) copy-start(bf16[1,128,4096]{2,1,0:T(8,128)(2,1)} %param.7) | copy-start | bytes 3145732
  66.7 18.6 %copy-start.3 = (f32[1,4096]{1,0:T(1,128)S(1)}, f32[1,4096]{1,0:T(1,128)}, u32[]{:S(2)}) copy-start(f32[1,4096]{1,0:T(1,128)} %param.11) | copy-start | bytes 49156
  85.3 1.4 %copy-start.1 = (bf16[1,128,4096]{2,1,0:T(8,128)(2,1)S(1)}, bf16[1,128,4096]{2,1,0:T(8,128)(2,1)}, u32[]{:S(2)}) copy-start(bf16[1,128,4096]{2,1,0:T(8,128)(2,1)} %param.8) | copy-start | bytes 3145732
  88.4 24.9 %collective-permute-start = (bf16[128,4096]{1,0:T(8,128)(2,1)}, bf16[128,4096]{1,0:T(8,128)(2,1)}, u32[]{:S(2)}, u32[]{:S(2)}) collective-permute-start(bf16[128,4096]{1,0:T(8,128)(2,1)} %add_convert_fusion), channel_id=1, source_target_pairs={{8,0},{16,8},{24,16},{0,24},{9,1},{17,9},{25,17},{1,25},{10,2},{18... | collective-permute-start | bytes 3145736 | tf_op jit(solution)/shard_map/ppermute | solution.py:13
where the time goes:
time: 116 us
  waiting for transfers between devices  42.3 us (36%)
  blocking collectives  33.6 us (29%)
  matrix products  16.2 us (14%)
  starting transfers between devices  12.9 us (11%)
  other arithmetic  5.36 us (5%)
  local copies, waits for them, and re-layouts  4.36 us (4%)
    all_to_all x1, blocking collectives, on_device(): lax.all_to_all(input_part, 'expert', split_axis=0, concat_axis=0, tiled=T...  17.8 us
    ppermute x1, waiting for transfers between devices, shifted(): return lax.ppermute(block, axis, route)  15.1 us
    all_to_all x1, waiting for transfers between devices, on_device(): lax.all_to_all(jnp.repeat(sent_in, SPLIT, axis=0), 'expert', split_axis=0...  14 us
    all_to_all x1, waiting for transfers between devices, on_device(): lax.all_to_all(jnp.repeat(sent_grad, SPLIT, axis=0), 'expert', split_axis...  13.2 us
    all_to_all x1, blocking collectives, on_device(): lax.all_to_all(combine_part, 'expert', split_axis=0, concat_axis=0, tiled...  7.93 us
    all_to_all x1, blocking collectives, on_device(): lax.all_to_all(jnp.repeat(sent_weight, SPLIT, axis=0), 'expert', split_ax...  7.92 us
    dot_general x2, matrix products, column_product(): lax.dot_general(left_rows, right_rows, (((0,), (0,)), ((), ())), preferre...  6.57 us
    all_to_all x1, starting transfers between devices, on_device(): lax.all_to_all(jnp.repeat(sent_in, SPLIT, axis=0), 'expert', split_axis=0...  6.33 us
  transfers between devices with their start and end apart: 3, of which 3 were waited for; matrix products, arithmetic and copies ran while one was open for 9% of the time, Pallas kernels for 0%

commit v1 on v0

--- a/solution.py
+++ b/solution.py
@@ -1,10 +1,18 @@
+import functools
+
 import jax
 import jax.numpy as jnp
 from jax import lax
+from jax.experimental import pallas as pl
+from jax.experimental.pallas import tpu as pltpu
 from jax.sharding import PartitionSpec as P
 
 SPLIT = 8
 SPECIALIST_CAP = 8
+LANES = 128
+EPS = 1e-06
+F32 = jnp.float32
+BF16 = jnp.bfloat16
 
 
 def shifted(block, axis, distance):
@@ -25,7 +33,7 @@
     )
 
 
-def on_device(hidden_in, out_grad, expert_ids, route_weight, norm_gain, w_gate_up, w_down):
+def on_many(hidden_in, out_grad, expert_ids, route_weight, norm_gain, w_gate_up, w_down):
     tokens_in = hidden_in[0]
     grad_out = out_grad[0]
     chosen = expert_ids[0]
@@ -131,7 +139,241 @@
     )
 
 
+def call(kernel, outs, flops, moved, limit=24, scratch=()):
+    return pl.pallas_call(
+        kernel,
+        out_shape=[jax.ShapeDtypeStruct(shape, kind) for shape, kind in outs],
+        scratch_shapes=list(scratch),
+        compiler_params=pltpu.CompilerParams(vmem_limit_bytes=limit << 20),
+        cost_estimate=pl.CostEstimate(flops=flops, bytes_accessed=moved, transcendentals=0),
+    )
+
+
+def take_rows(place, block):
+    return lax.dot_general(place, block, (((1,), (0,)), ((), ())), preferred_element_type=F32)
+
+
+def normed_rows(rows):
+    rms = jnp.sqrt(jnp.mean(rows * rows, axis=-1, keepdims=True) + EPS)
+    return rows / rms, rms
+
+
+def place_kernel(ids_ref, hidden_ref, gain_ref, in_ref, raw_ref, place_ref):
+    tokens = ids_ref.shape[1]
+    cap = SPECIALIST_CAP
+    member = jnp.max((ids_ref[...] == 0).astype(F32), axis=0, keepdims=True)
+    member = jnp.broadcast_to(member, (cap, tokens))
+    earlier = lax.broadcasted_iota(jnp.int32, (tokens, tokens), 0) < lax.broadcasted_iota(
+        jnp.int32, (tokens, tokens), 1
+    )
+    position = take_rows(member.astype(BF16), earlier.astype(F32).astype(BF16))
+    slot = lax.broadcasted_iota(jnp.int32, (cap, tokens), 0).astype(F32)
+    place = jnp.where(position == slot, member, 0.0)
+    place_ref[...] = place
+    rows = take_rows(place.astype(BF16), hidden_ref[...])
+    raw_ref[...] = rows.astype(BF16)
+    normed, _ = normed_rows(rows)
+    in_ref[...] = (normed * gain_ref[...]).astype(BF16)
+
+
+def grad_rows_kernel(ids_ref, weight_ref, place_ref, grad_ref, out_ref):
+    width = grad_ref.shape[1]
+    place = place_ref[...]
+    out_ref[:, :width] = take_rows(place.astype(BF16), grad_ref[...]).astype(BF16)
+    weight = jnp.sum(
+        jnp.where(ids_ref[...] == 0, weight_ref[...].astype(F32), 0.0), axis=0, keepdims=True
+    )
+    taken = jnp.sum(place * weight, axis=1, keepdims=True)
+    out_ref[:, width:] = jnp.broadcast_to(taken, (place.shape[0], LANES)).astype(BF16)
+
+
+def stacked(refs, start, stop):
+    return jnp.concatenate([r[:, start:stop].astype(F32) for r in refs], axis=0)
+
+
+def project_kernel(*refs):
+    *blocks, slab_ref, out_ref = refs
+    width = slab_ref.shape[1]
+    out_ref[...] = rows_product(stacked(blocks, 0, width).astype(BF16), slab_ref[...])
+
+
+def hidden_kernel(*refs):
+    *blocks, pre_ref, down_ref, slab_ref, keep_ref, send_ref, both_ref, act_ref = refs
+    hidden, width = down_ref.shape
+    half = keep_ref.shape[0]
+    grad = stacked(blocks, 0, width).astype(BF16)
+    weight = stacked(blocks, width, width + LANES)[:, :1]
+    back = rows_product(grad, down_ref[...])
+    gate = pre_ref[:, :hidden]
+    up = pre_ref[:, hidden:]
+    sig = jax.nn.sigmoid(gate)
+    active = gate * sig
+    act = active * up
+    act_ref[...] = (weight * act).T.astype(BF16)
+    into = weight * back
+    both = jnp.concatenate(
+        [into * up * sig * (1.0 + gate * (1.0 - sig)), into * active], axis=1
+    )
+    both_ref[...] = both.T.astype(BF16)
+    part = take_rows(both.astype(BF16), slab_ref[...]).astype(BF16)
+    keep_ref[:, :width] = part[:half]
+    send_ref[:, :width] = part[half:]
+    comb = jnp.sum(act * back, axis=1, keepdims=True)
+    comb = jnp.broadcast_to(comb, (2 * half, LANES)).astype(BF16)
+    keep_ref[:, width:] = comb[:half]
+    send_ref[:, width:] = comb[half:]
+
+
+def join_kernel(keep_ref, got_ref, *refs):
+    *out_refs, comb_ref = refs
+    width = out_refs[0].shape[1]
+    total = keep_ref[...].astype(F32) + got_ref[...].astype(F32)
+    rows = out_refs[0].shape[0]
+    for k, out_ref in enumerate(out_refs):
+        out_ref[...] = total[k * rows : (k + 1) * rows, :width].astype(BF16)
+    comb_ref[...] = total[:, width:]
+
+
+def weights_kernel(*refs):
+    *blocks, both_ref, act_ref, both_out, act_out = refs
+    ins, grads = blocks[: len(blocks) // 2], blocks[len(blocks) // 2 :]
+    step = both_out.shape[1]
+    both_out[...] = take_rows(both_ref[...], stacked(ins, 0, step).astype(BF16)).astype(BF16)
+    act_out[...] = take_rows(act_ref[...], stacked(grads, 0, step).astype(BF16)).astype(BF16)
+
+
+def weight_grads(ins, grads, both, act, width):
+    chunk = min(width, 1024)
+    rows = ins[0].shape[0]
+    block = pl.BlockSpec((rows, chunk), lambda i: (0, i))
+    whole = lambda a: pl.BlockSpec(a.shape, lambda i: (0, 0))
+    return pl.pallas_call(
+        weights_kernel,
+        grid=(width // chunk,),
+        in_specs=[block] * (len(ins) + len(grads)) + [whole(both), whole(act)],
+        out_specs=[
+            pl.BlockSpec((both.shape[0], chunk), lambda i: (0, i)),
+            pl.BlockSpec((act.shape[0], chunk), lambda i: (0, i)),
+        ],
+        out_shape=[
+            jax.ShapeDtypeStruct((both.shape[0], width), BF16),
+            jax.ShapeDtypeStruct((act.shape[0], width), BF16),
+        ],
+        compiler_params=pltpu.CompilerParams(vmem_limit_bytes=24 << 20),
+        cost_estimate=pl.CostEstimate(
+            flops=2 * 64 * 576 * width, bytes_accessed=2 * 700 * width, transcendentals=0
+        ),
+    )(*ins, *grads, both, act)
+
+
+def finish_kernel(*refs):
+    *parts, raw_ref, gain_ref, place_ref, grad_ref, out_ref = refs
+    place = place_ref[...]
+    normed, rms = normed_rows(raw_ref[...].astype(F32))
+    grad = grad_ref[...]
+    own = take_rows(place.astype(BF16), grad)
+    total = sum(p[...].astype(F32) for p in parts)
+    scaled = total * gain_ref[...]
+    inner = jnp.mean(scaled * normed, axis=-1, keepdims=True)
+    rows = (own + (scaled - normed * inner) / rms).astype(BF16)
+    back = place.T
+    spread = take_rows(back.astype(BF16), rows)
+    named = jnp.sum(back, axis=1, keepdims=True) > 0.0
+    out_ref[...] = jnp.where(named, spread, grad.astype(F32)).astype(BF16)
+
+
+def combine_kernel(*refs):
+    *parts, ids_ref, place_ref, out_ref = refs
+    total = sum(p[...] for p in parts)
+    spread = jnp.sum(place_ref[...] * total, axis=0, keepdims=True)
+    out_ref[...] = jnp.where(ids_ref[...] == 0, spread, 0.0)
+
+
+def on_one(hidden_in, out_grad, expert_ids, route_weight, norm_gain, w_gate_up, w_down):
+    sections = lax.axis_size("pipe")
+    devices = lax.axis_size("expert")
+    chips = devices // 2
+    tokens, width = hidden_in.shape[1:]
+    hidden = w_down.shape[2]
+    cap = SPECIALIST_CAP
+    ids = expert_ids[0].T
+    weights = route_weight[0].T
+    slab = w_gate_up.reshape(2 * hidden, width)
+    down = w_down.reshape(hidden, width)
+    grad = out_grad[0]
+    wide = width + LANES
+
+    def across(block, offset):
+        return lax.ppermute(block, "expert", [(i, i ^ (2 * offset)) for i in range(devices)])
+
+    def beside(block):
+        return lax.ppermute(block, "expert", [(i, i ^ 1) for i in range(devices)])
+
+    def handed(block, offset):
+        route = [
+            (((p + 1) % sections) * devices + i, p * devices + (i ^ (2 * offset)))
+            for p in range(sections)
+            for i in range(devices)
+        ]
+        return lax.ppermute(block, ("pipe", "expert"), route)
+
+    next_grad = handed(grad, 0)
+    row_in, row_raw, place = call(
+        place_kernel,
+        [((cap, width), BF16), ((cap, width), BF16), ((cap, tokens), F32)],
+        2 * tokens * width * cap,
+        2 * tokens * width,
+    )(ids, hidden_in[0], norm_gain)
+    lane_in = [row_in] + [across(row_in, k) for k in range(1, chips)]
+    (row_grad,) = call(
+        grad_rows_kernel, [((cap, wide), BF16)], 2 * tokens * width * cap, 2 * tokens * width
+    )(ids, weights, place, grad)
+    lane_grad = [row_grad] + [across(row_grad, k) for k in range(1, chips)]
+    next_raw, next_gain, next_place = handed(row_raw, 0), handed(norm_gain, 0), handed(place, 0)
+    all_in = lane_in + [beside(b) for b in lane_in]
+    all_grad = lane_grad + [beside(b) for b in lane_grad]
+    total_rows = devices * cap
+    (pre,) = call(
+        project_kernel,
+        [((total_rows, 2 * hidden), F32)],
+        4 * total_rows * hidden * width,
+        4 * hidden * width,
+    )(*all_in, slab)
+    keep, send, both, act = call(
+        hidden_kernel,
+        [
+            ((total_rows // 2, wide), BF16),
+            ((total_rows // 2, wide), BF16),
+            ((2 * hidden, total_rows), BF16),
+            ((hidden, total_rows), BF16),
+        ],
+        6 * total_rows * hidden * width,
+        6 * hidden * width,
+    )(*all_grad, pre, down, slab)
+    *parts, comb = call(
+        join_kernel,
+        [((cap, width), BF16)] * chips + [((total_rows // 2, LANES), F32)],
+        total_rows * width,
+        4 * total_rows * width,
+    )(keep, beside(send))
+    got = [handed(parts[k], k) for k in range(chips)]
+    comb_parts = [comb[k * cap : (k + 1) * cap] for k in range(chips)]
+    comb_got = [comb_parts[0]] + [across(comb_parts[k], k) for k in range(1, chips)]
+    gate_up_out, down_out = weight_grads(all_in, all_grad, both, act, width)
+    (combined,) = call(combine_kernel, [((SPLIT, tokens), F32)], 1000, 1000)(*comb_got, ids, place)
+    (out,) = call(finish_kernel, [((tokens, width), BF16)], 4 * tokens * width * cap, 4 * tokens * width)(
+        *got, next_raw, next_gain, next_place, next_grad
+    )
+    return (
+        out[None],
+        gate_up_out.reshape(1, 1, 2, hidden, width),
+        down_out.reshape(1, 1, hidden, width),
+        combined.T[None],
+    )
+
+
 def solution(mesh):
+    on_device = on_one if mesh.shape["expert"] == SPLIT else on_many
     return jax.shard_map(
         on_device,
         mesh=mesh,

time: 116 us -> 53.4 us (0.46)
  waiting for transfers between devices: 42.3 us -> 6.23 us
  blocking collectives: 33.6 us -> 0 us
  starting transfers between devices: 12.9 us -> 29.6 us
  matrix products: 16.2 us -> 0 us
  Pallas kernels: 0 us -> 9.27 us
  other arithmetic: 5.36 us -> 0 us
  local copies, waits for them, and re-layouts: 4.36 us -> 7.18 us
    all_to_all x3 -> x0, blocking collectives: 33.6 us -> none  [the longest x1 17.8 us: on_device(): lax.all_to_all(input_part, 'expert', split_axis=0, concat_axis=0, tiled=T...]
    all_to_all x2 -> x0, waiting for transfers between devices: 27.2 us -> none  [the longest x1 14 us: on_device(): lax.all_to_all(jnp.repeat(sent_in, SPLIT, axis=0), 'expert', split_axis=0...]
    ppermute x1 -> x26, starting transfers between devices: 2.45 us -> 29.6 us  [the longest x8 14.5 us: handed(): return lax.ppermute(block, ('pipe', 'expert'), route)]
    dot_general x8 -> x0, matrix products: 16.2 us -> none  [the longest x2 6.57 us: column_product(): lax.dot_general(left_rows, right_rows, (((0,), (0,)), ((), ())), preferre...]
    all_to_all x2 -> x0, starting transfers between devices: 10.5 us -> none  [the longest x1 6.33 us: on_device(): lax.all_to_all(jnp.repeat(sent_in, SPLIT, axis=0), 'expert', split_axis=0...]
    pallas_call x0 -> x8, Pallas kernels: none -> 9.27 us  [the longest x1 3.17 us: weight_grads(): pl.pallas_call(weights_kernel, grid=(width // chunk,), in_specs=[block] *...]
    ppermute x1 -> x26, waiting for transfers between devices: 15.1 us -> 6.23 us  [the longest x9 4.86 us: across(): lax.ppermute(block, 'expert', [(i, i ^ 2 * offset) for i in range(devices)])]
    unnamed x9 -> x20, local copies, waits for them, and re-layouts: 2.32 us -> 7.18 us
  transfers between devices with their start and end apart: 3 -> 26, of which waited for: 3 -> 4; matrix products, arithmetic and copies ran while one was open for 9% -> 0% of each run, Pallas kernels for 0% -> 14%
where the time goes in v1:
time: 53.4 us; the launch traced here: 53 us
  starting transfers between devices  29.6 us (55%)
  Pallas kernels  9.27 us (17%)
  local copies, waits for them, and re-layouts  7.18 us (13%)
  waiting for transfers between devices  6.23 us (12%)
  between operations  0.77 us (1%)
    ppermute x8, starting transfers between devices, handed(): return lax.ppermute(block, ('pipe', 'expert'), route)  14.5 us
    ppermute x9, starting transfers between devices, across(): lax.ppermute(block, 'expert', [(i, i ^ 2 * offset) for i in range(devices)])  13.3 us
    unnamed x20, local copies, waits for them, and re-layouts  7.18 us
    ppermute x9, waiting for transfers between devices, across(): lax.ppermute(block, 'expert', [(i, i ^ 2 * offset) for i in range(devices)])  4.86 us
    pallas_call x1, Pallas kernels, weight_grads(): pl.pallas_call(weights_kernel, grid=(width // chunk,), in_specs=[block] *...  3.17 us
    pallas_call x1, Pallas kernels, on_one(): call(hidden_kernel, [((total_rows // 2, wide), BF16), ((total_rows // 2,...  1.99 us
    ppermute x9, starting transfers between devices, beside(): return lax.ppermute(block, 'expert', [(i, i ^ 1) for i in range(devices)])  1.73 us
    pallas_call x1, Pallas kernels, on_one(): call(finish_kernel, [((tokens, width), BF16)], 4 * tokens * width * cap,...  1.66 us
  transfers between devices with their start and end apart: 26, of which 4 were waited for; matrix products, arithmetic and copies ran while one was open for 0% of the time, Pallas kernels for 14%

profile of v1, /device:TPU:0, one launch (start us, length us, event | category | flops | bytes accessed | tf_op | source)
XLA Modules:
  0.0 53.0 jit_solution(9553293306571535687)
XLA Ops:
  0.6 3.9 %collective-permute-start.22 = (bf16[128,4096]{1,0:T(8,128)(2,1)}, bf16[128,4096]{1,0:T(8,128)(2,1)S(1)}, u32[]{:S(2)}, u32[]{:S(2)}) collective-permute-start(bf16[128,4096]{1,0:T(8,128)(2,1)} %bitcast.20), channel_id=1, source_target_pairs={{8,0},{9,1},{10,2},{11,3},{12,4},{13,5},{14,6},{15,7},{16,8},{17,9... | collective-permute-start | bytes 3145736 | tf_op jit(solution)/shard_map/ppermute | solution.py:318
  4.6 1.2 %copy-done.3 = bf16[1,128,4096]{2,1,0:T(8,128)(2,1)S(1)} copy-done((bf16[1,128,4096]{2,1,0:T(8,128)(2,1)S(1)}, bf16[1,128,4096]{2,1,0:T(8,128)(2,1)}, u32[]{:S(2)}) %copy-start.3) | copy-done | bytes 1048600
  5.8 0.7 %copy-done.5 = s32[1,128,8]{1,2,0:T(8,128)S(1)} copy-done((s32[1,128,8]{1,2,0:T(8,128)S(1)}, s32[1,128,8]{1,2,0:T(8,128)}, u32[]{:S(2)}) %copy-start.5) | copy-done | bytes 4120
  6.5 0.7 %copy-done.7 = f32[1,4096]{1,0:T(1,128)S(1)} copy-done((f32[1,4096]{1,0:T(1,128)S(1)}, f32[1,4096]{1,0:T(1,128)}, u32[]{:S(2)}) %copy-start.7) | copy-done | bytes 16408
  7.8 3.7 %collective-permute-start.9 = (bf16[8,4096]{1,0:T(8,128)(2,1)S(1)}, bf16[8,4096]{1,0:T(8,128)(2,1)S(1)}, u32[]{:S(2)}, u32[]{:S(2)}) collective-permute-start(bf16[8,4096]{1,0:T(8,128)(2,1)S(1)} %get-tuple-element.19.refs_0_), channel_id=1, source_target_pairs={{0,6},{1,7},{2,4},{3,5},{4,2},{5,3},{6,0},{7,1},{8,14},{9,15},{10,... | collective-permute-start | bytes 196616 | tf_op jit(solution)/shard_map/ppermute | solution.py:307
  11.5 1.2 %copy-done.4 = bf16[1,128,4096]{2,1,0:T(8,128)(2,1)S(1)} copy-done((bf16[1,128,4096]{2,1,0:T(8,128)(2,1)S(1)}, bf16[1,128,4096]{2,1,0:T(8,128)(2,1)}, u32[]{:S(2)}) %copy-start.4) | copy-done | bytes 1048600
  12.7 0.7 %copy-done.9 = bf16[1,128,8]{1,2,0:T(8,128)(2,1)S(1)} copy-done((bf16[1,128,8]{1,2,0:T(8,128)(2,1)S(1)}, bf16[1,128,8]{1,2,0:T(8,128)(2,1)}, u32[]{:S(2)}) %copy-start.9) | copy-done | bytes 2072
  13.6 2.0 %collective-permute-start.2 = (bf16[8,4224]{1,0:T(8,128)(2,1)S(1)}, bf16[8,4224]{1,0:T(8,128)(2,1)S(1)}, u32[]{:S(2)}, u32[]{:S(2)}) collective-permute-start(bf16[8,4224]{1,0:T(8,128)(2,1)S(1)} %shard_map.103.refs_0_.refs_8_), channel_id=1, source_target_pairs={{0,6},{1,7},{2,4},{3,5},{4,2},{5,3},{6,0},{7,1},{8,14},{9,15},{10,... | collective-permute-start | bytes 202760 | tf_op jit(solution)/shard_map/ppermute | solution.py:307
  15.5 1.1 %collective-permute-start.1 = (bf16[8,4224]{1,0:T(8,128)(2,1)S(1)}, bf16[8,4224]{1,0:T(8,128)(2,1)S(1)}, u32[]{:S(2)}, u32[]{:S(2)}) collective-permute-start(bf16[8,4224]{1,0:T(8,128)(2,1)S(1)} %shard_map.103.refs_0_.refs_8_), channel_id=1, source_target_pairs={{0,4},{1,5},{2,6},{3,7},{4,0},{5,1},{6,2},{7,3},{8,12},{9,13},{10,... | collective-permute-start | bytes 202760 | tf_op jit(solution)/shard_map/ppermute | solution.py:307
  16.7 1.4 %collective-permute-start.7 = (bf16[8,4096]{1,0:T(8,128)(2,1)S(1)}, bf16[8,4096]{1,0:T(8,128)(2,1)S(1)}, u32[]{:S(2)}, u32[]{:S(2)}) collective-permute-start(bf16[8,4096]{1,0:T(8,128)(2,1)S(1)} %get-tuple-element.19.refs_0_), channel_id=1, source_target_pairs={{0,2},{1,3},{2,0},{3,1},{4,6},{5,7},{6,4},{7,5},{8,10},{9,11},{10,... | collective-permute-start | bytes 196616 | tf_op jit(solution)/shard_map/ppermute | solution.py:307
  18.0 0.6 %collective-permute-start = (bf16[8,4224]{1,0:T(8,128)(2,1)S(1)}, bf16[8,4224]{1,0:T(8,128)(2,1)S(1)}, u32[]{:S(2)}, u32[]{:S(2)}) collective-permute-start(bf16[8,4224]{1,0:T(8,128)(2,1)S(1)} %shard_map.103.refs_0_.refs_8_), channel_id=1, source_target_pairs={{0,2},{1,3},{2,0},{3,1},{4,6},{5,7},{6,4},{7,5},{8,10},{9,11},{10,... | collective-permute-start | bytes 202760 | tf_op jit(solution)/shard_map/ppermute | solution.py:307
  18.7 3.5 %collective-permute-done.7.refs_1_ = bf16[8,4096]{1,0:T(8,128)(2,1)S(1)} collective-permute-done((bf16[8,4096]{1,0:T(8,128)(2,1)S(1)}, bf16[8,4096]{1,0:T(8,128)(2,1)S(1)}, u32[]{:S(2)}, u32[]{:S(2)}) %collective-permute-start.7) | collective-permute-done | bytes 65568 | tf_op jit(solution)/shard_map/ppermute | solution.py:307
  22.2 0.5 collective-permute-start.12
  22.7 0.7 %collective-permute-done.1.refs_2_.refs_10_ = bf16[8,4224]{1,0:T(8,128)(2,1)S(1)} collective-permute-done((bf16[8,4224]{1,0:T(8,128)(2,1)S(1)}, bf16[8,4224]{1,0:T(8,128)(2,1)S(1)}, u32[]{:S(2)}, u32[]{:S(2)}) %collective-permute-start.1) | collective-permute-done | bytes 67616 | tf_op jit(solution)/shard_map/ppermute | solution.py:307
  23.4 0.6 %collective-permute-done.refs_1_.refs_9_ = bf16[8,4224]{1,0:T(8,128)(2,1)S(1)} collective-permute-done((bf16[8,4224]{1,0:T(8,128)(2,1)S(1)}, bf16[8,4224]{1,0:T(8,128)(2,1)S(1)}, u32[]{:S(2)}, u32[]{:S(2)}) %collective-permute-start) | collective-permute-done | bytes 67616 | tf_op jit(solution)/shard_map/ppermute | solution.py:307
  24.1 0.5 collective-permute-start.6
  25.1 1.9 %copy-done = bf16[1,1,2,192,4096]{4,3,2,1,0:T(8,128)(2,1)S(1)} copy-done((bf16[1,1,2,192,4096]{4,3,2,1,0:T(8,128)(2,1)S(1)}, bf16[1,1,2,192,4096]{4,3,2,1,0:T(8,128)(2,1)}, u32[]{:S(2)}) %copy-start) | copy-done | bytes 3145752
  27.0 1.1 %shard_map.104.refs_8_ = f32[64,384]{1,0:T(8,128)S(1)} custom-call(bf16[8,4096]{1,0:T(8,128)(2,1)S(1)} %get-tuple-element.19.refs_0_, bf16[8,4096]{1,0:T(8,128)(2,1)S(1)} %collective-permute-done.7.refs_1_, bf16[8,4096]{1,0:T(8,128)(2,1)S(1)} %collective-permute-done.8.refs_2_, bf16[8,4096]{1,0:T(8,128)(2,1)S(1)} %collective-permute-done.9.refs_3_, ...), custom_call_target="tpu_custom_call" | custom-call | flops 201326592 | bytes 3145728 | tf_op jit(solution)/shard_map/pallas_call | solution.py:336
  28.1 0.7 %copy-done.1 = bf16[1,1,2,192,4096]{4,3,2,1,0:T(8,128)(2,1)S(1)} copy-done((bf16[1,1,2,192,4096]{4,3,2,1,0:T(8,128)(2,1)S(1)}, bf16[1,1,2,192,4096]{4,3,2,1,0:T(8,128)(2,1)}, u32[]{:S(2)}) %copy-start.1) | copy-done | bytes 3145752
  28.9 2.0 %shard_map.105 = (bf16[32,4224]{1,0:T(8,128)(2,1)S(1)}, bf16[32,4224]{1,0:T(8,128)(2,1)S(1)}, bf16[384,64]{1,0:T(8,128)(2,1)S(1)}, bf16[192,64]{1,0:T(8,128)(2,1)S(1)}) custom-call(bf16[8,4224]{1,0:T(8,128)(2,1)S(1)} %shard_map.103.refs_0_.refs_8_, bf16[8,4224]{1,0:T(8,128)(2,1)S(1)} %collective-permute-done.refs_1_.refs_9_, ...), custom_call_target="tpu_custom_call" | custom-call | flops 301989888 | bytes 4718592 | tf_op jit(solution)/shard_map/pallas_call | solution.py:342
  31.0 0.5 %collective-permute-start.20 = (f32[1,4096]{1,0:T(1,128)S(1)}, f32[1,4096]{1,0:T(1,128)S(1)}, u32[]{:S(2)}, u32[]{:S(2)}) collective-permute-start(f32[1,4096]{1,0:T(1,128)S(1)} %copy-done.8), channel_id=1, source_target_pairs={{8,0},{9,1},{10,2},{11,3},{12,4},{13,5},{14,6},{15,7},{16,8},{17,9... | collective-permute-start | bytes 49160 | tf_op jit(solution)/shard_map/ppermute | solution.py:318
  31.6 1.4 %collective-permute-start.21 = (f32[8,128]{1,0:T(8,128)S(1)}, f32[8,128]{1,0:T(8,128)S(1)}, u32[]{:S(2)}, u32[]{:S(2)}) collective-permute-start(f32[8,128]{1,0:T(8,128)S(1)} %get-tuple-element.18.place_ref.refs_5_), channel_id=1, source_target_pairs={{8,0},{9,1},{10,2},{11,3},{12,4},{13,5},{14,6},{15,7},{16,8},{17,9... | collective-permute-start | bytes 12296 | tf_op jit(solution)/shard_map/ppermute | solution.py:318
  33.0 0.5 %collective-permute-start.19 = (bf16[8,4096]{1,0:T(8,128)(2,1)S(1)}, bf16[8,4096]{1,0:T(8,128)(2,1)S(1)}, u32[]{:S(2)}, u32[]{:S(2)}) collective-permute-start(bf16[8,4096]{1,0:T(8,128)(2,1)S(1)} %get-tuple-element.26), channel_id=1, source_target_pairs={{8,0},{9,1},{10,2},{11,3},{12,4},{13,5},{14,6},{15,7},{16,8},{17,9... | collective-permute-start | bytes 196616 | tf_op jit(solution)/shard_map/ppermute | solution.py:318
  33.6 2.5 %collective-permute-start.25 = (f32[8,128]{1,0:T(8,128)S(1)}, f32[8,128]{1,0:T(8,128)S(1)}, u32[]{:S(2)}, u32[]{:S(2)}) collective-permute-start(f32[8,128]{1,0:T(8,128)S(1)} %get-tuple-element.32), channel_id=1, source_target_pairs={{0,6},{1,7},{2,4},{3,5},{4,2},{5,3},{6,0},{7,1},{8,14},{9,15},{10,... | collective-permute-start | bytes 12296 | tf_op jit(solution)/shard_map/ppermute | solution.py:307
  36.2 2.0 %collective-permute-start.23 = (f32[8,128]{1,0:T(8,128)S(1)}, f32[8,128]{1,0:T(8,128)S(1)}, u32[]{:S(2)}, u32[]{:S(2)}) collective-permute-start(f32[8,128]{1,0:T(8,128)S(1)} %get-tuple-element.34), channel_id=1, source_target_pairs={{0,2},{1,3},{2,0},{3,1},{4,6},{5,7},{6,4},{7,5},{8,10},{9,11},{10,... | collective-permute-start | bytes 12296 | tf_op jit(solution)/shard_map/ppermute | solution.py:307
  38.2 2.3 %collective-permute-start.15 = (bf16[8,4096]{1,0:T(8,128)(2,1)S(1)}, bf16[8,4096]{1,0:T(8,128)(2,1)S(1)}, u32[]{:S(2)}, u32[]{:S(2)}) collective-permute-start(bf16[8,4096]{1,0:T(8,128)(2,1)S(1)} %get-tuple-element.22), channel_id=1, source_target_pairs={{8,0},{9,1},{10,2},{11,3},{12,4},{13,5},{14,6},{15,7},{16,8},{17,9... | collective-permute-start | bytes 196616 | tf_op jit(solution)/shard_map/ppermute | solution.py:318
  40.7 3.7 %collective-permute-start.17 = (bf16[8,4096]{1,0:T(8,128)(2,1)S(1)}, bf16[8,4096]{1,0:T(8,128)(2,1)S(1)}, u32[]{:S(2)}, u32[]{:S(2)}) collective-permute-start(bf16[8,4096]{1,0:T(8,128)(2,1)S(1)} %get-tuple-element.24), channel_id=1, source_target_pairs={{8,4},{9,5},{10,6},{11,7},{12,0},{13,1},{14,2},{15,3},{16,12},{17,... | collective-permute-start | bytes 196616 | tf_op jit(solution)/shard_map/ppermute | solution.py:318
  44.4 1.9 %collective-permute-start.18 = (bf16[8,4096]{1,0:T(8,128)(2,1)S(1)}, bf16[8,4096]{1,0:T(8,128)(2,1)S(1)}, u32[]{:S(2)}, u32[]{:S(2)}) collective-permute-start(bf16[8,4096]{1,0:T(8,128)(2,1)S(1)} %get-tuple-element.25), channel_id=1, source_target_pairs={{8,6},{9,7},{10,4},{11,5},{12,2},{13,3},{14,0},{15,1},{16,14},{17,... | collective-permute-start | bytes 196616 | tf_op jit(solution)/shard_map/ppermute | solution.py:318
  46.3 3.2 %shard_map.108 = (bf16[384,4096]{1,0:T(8,128)(2,1)}, bf16[192,4096]{1,0:T(8,128)(2,1)}) custom-call(bf16[8,4096]{1,0:T(8,128)(2,1)S(1)} %get-tuple-element.19.refs_0_, bf16[8,4096]{1,0:T(8,128)(2,1)S(1)} %collective-permute-done.7.refs_1_, bf16[8,4096]{1,0:T(8,128)(2,1)S(1)} %collective-permute-done.8.refs_2_, ...), custom_call_target="tpu_custom_call" | custom-call | flops 301989888 | bytes 5734400 | tf_op jit(solution)/shard_map/pallas_call | solution.py:250
  49.5 0.6 %shard_map.109 = f32[8,128]{1,0:T(8,128)} custom-call(f32[8,128]{1,0:T(8,128)S(1)} %get-tuple-element.35.refs_0_, f32[8,128]{1,0:T(8,128)S(1)} %collective-permute-done.23.refs_1_, f32[8,128]{1,0:T(8,128)S(1)} %collective-permute-done.24.refs_2_, f32[8,128]{1,0:T(8,128)S(1)} %collective-permute-done.25.refs_3_, s32[8,128]{1,0:T(8,128)S(1)} %bitcast.24, ...), custom_call_target="tpu_custom_call" | custom-call | flops 1000 | bytes 1000 | tf_op jit(solution)/shard_map/pallas_call | solution.py:363
  50.1 1.3 %collective-permute-done.18.refs_3_ = bf16[8,4096]{1,0:T(8,128)(2,1)S(1)} collective-permute-done((bf16[8,4096]{1,0:T(8,128)(2,1)S(1)}, bf16[8,4096]{1,0:T(8,128)(2,1)S(1)}, u32[]{:S(2)}, u32[]{:S(2)}) %collective-permute-start.18) | collective-permute-done | bytes 65568 | tf_op jit(solution)/shard_map/ppermute | solution.py:318
  51.4 1.7 %shard_map.107 = bf16[128,4096]{1,0:T(8,128)(2,1)} custom-call(bf16[8,4096]{1,0:T(8,128)(2,1)S(1)} %collective-permute-done.15.refs_0_, bf16[8,4096]{1,0:T(8,128)(2,1)S(1)} %collective-permute-done.16.refs_1_, bf16[8,4096]{1,0:T(8,128)(2,1)S(1)} %collective-permute-done.17.refs_2_, bf16[8,4096]{1,0:T(8,128)(2,1)S(1)} %collective-permute-done.18.refs_3_, ...), custom_call_target="tpu_custom_call" | custom-call | flops 16777216 | bytes 2097152 | tf_op jit(solution)/shard_map/pallas_call | solution.py:364
  (49 shorter events, 1.7 us)
Async XLA Ops:
  0.6 27.5 %copy-start.2 = (bf16[1,1,192,4096]{3,2,1,0:T(8,128)(2,1)S(1)}, bf16[1,1,192,4096]{3,2,1,0:T(8,128)(2,1)}, u32[]{:S(2)}) copy-start(bf16[1,1,192,4096]{3,2,1,0:T(8,128)(2,1)} %param.13) | copy-start | bytes 4718596
  0.6 50.7 %collective-permute-start.22 = (bf16[128,4096]{1,0:T(8,128)(2,1)}, bf16[128,4096]{1,0:T(8,128)(2,1)S(1)}, u32[]{:S(2)}, u32[]{:S(2)}) collective-permute-start(bf16[128,4096]{1,0:T(8,128)(2,1)} %bitcast.20), channel_id=1, source_target_pairs={{8,0},{9,1},{10,2},{11,3},{12,4},{13,5},{14,6},{15,7},{16,8},{17,9... | collective-permute-start | bytes 3145736 | tf_op jit(solution)/shard_map/ppermute | solution.py:318
  7.7 7.8 %collective-permute-start.10 = (bf16[8,4096]{1,0:T(8,128)(2,1)S(1)}, bf16[8,4096]{1,0:T(8,128)(2,1)S(1)}, u32[]{:S(2)}, u32[]{:S(2)}) collective-permute-start(bf16[8,4096]{1,0:T(8,128)(2,1)S(1)} %get-tuple-element.19.refs_0_), channel_id=1, source_target_pairs={{0,1},{1,0},{2,3},{3,2},{4,5},{5,4},{6,7},{7,6},{8,9},{9,8},{10,11... | collective-permute-start | bytes 196616 | tf_op jit(solution)/shard_map/ppermute | solution.py:310
  7.8 8.9 %collective-permute-start.9 = (bf16[8,4096]{1,0:T(8,128)(2,1)S(1)}, bf16[8,4096]{1,0:T(8,128)(2,1)S(1)}, u32[]{:S(2)}, u32[]{:S(2)}) collective-permute-start(bf16[8,4096]{1,0:T(8,128)(2,1)S(1)} %get-tuple-element.19.refs_0_), channel_id=1, source_target_pairs={{0,6},{1,7},{2,4},{3,5},{4,2},{5,3},{6,0},{7,1},{8,14},{9,15},{10,... | collective-permute-start | bytes 196616 | tf_op jit(solution)/shard_map/ppermute | solution.py:307
  11.4 6.6 %collective-permute-start.8 = (bf16[8,4096]{1,0:T(8,128)(2,1)S(1)}, bf16[8,4096]{1,0:T(8,128)(2,1)S(1)}, u32[]{:S(2)}, u32[]{:S(2)}) collective-permute-start(bf16[8,4096]{1,0:T(8,128)(2,1)S(1)} %get-tuple-element.19.refs_0_), channel_id=1, source_target_pairs={{0,4},{1,5},{2,6},{3,7},{4,0},{5,1},{6,2},{7,3},{8,12},{9,13},{10,... | collective-permute-start | bytes 196616 | tf_op jit(solution)/shard_map/ppermute | solution.py:307
  11.4 1.2 %copy-start.4 = (bf16[1,128,4096]{2,1,0:T(8,128)(2,1)S(1)}, bf16[1,128,4096]{2,1,0:T(8,128)(2,1)}, u32[]{:S(2)}) copy-start(bf16[1,128,4096]{2,1,0:T(8,128)(2,1)} %param.8) | copy-start | bytes 3145732
  13.6 8.6 %collective-permute-start.2 = (bf16[8,4224]{1,0:T(8,128)(2,1)S(1)}, bf16[8,4224]{1,0:T(8,128)(2,1)S(1)}, u32[]{:S(2)}, u32[]{:S(2)}) collective-permute-start(bf16[8,4224]{1,0:T(8,128)(2,1)S(1)} %shard_map.103.refs_0_.refs_8_), channel_id=1, source_target_pairs={{0,6},{1,7},{2,4},{3,5},{4,2},{5,3},{6,0},{7,1},{8,14},{9,15},{10,... | collective-permute-start | bytes 202760 | tf_op jit(solution)/shard_map/ppermute | solution.py:307
  15.5 7.9 %collective-permute-start.1 = (bf16[8,4224]{1,0:T(8,128)(2,1)S(1)}, bf16[8,4224]{1,0:T(8,128)(2,1)S(1)}, u32[]{:S(2)}, u32[]{:S(2)}) collective-permute-start(bf16[8,4224]{1,0:T(8,128)(2,1)S(1)} %shard_map.103.refs_0_.refs_8_), channel_id=1, source_target_pairs={{0,4},{1,5},{2,6},{3,7},{4,0},{5,1},{6,2},{7,3},{8,12},{9,13},{10,... | collective-permute-start | bytes 202760 | tf_op jit(solution)/shard_map/ppermute | solution.py:307
  16.7 5.5 %collective-permute-start.7 = (bf16[8,4096]{1,0:T(8,128)(2,1)S(1)}, bf16[8,4096]{1,0:T(8,128)(2,1)S(1)}, u32[]{:S(2)}, u32[]{:S(2)}) collective-permute-start(bf16[8,4096]{1,0:T(8,128)(2,1)S(1)} %get-tuple-element.19.refs_0_), channel_id=1, source_target_pairs={{0,2},{1,3},{2,0},{3,1},{4,6},{5,7},{6,4},{7,5},{8,10},{9,11},{10,... | collective-permute-start | bytes 196616 | tf_op jit(solution)/shard_map/ppermute | solution.py:307
  18.0 6.0 %collective-permute-start = (bf16[8,4224]{1,0:T(8,128)(2,1)S(1)}, bf16[8,4224]{1,0:T(8,128)(2,1)S(1)}, u32[]{:S(2)}, u32[]{:S(2)}) collective-permute-start(bf16[8,4224]{1,0:T(8,128)(2,1)S(1)} %shard_map.103.refs_0_.refs_8_), channel_id=1, source_target_pairs={{0,2},{1,3},{2,0},{3,1},{4,6},{5,7},{6,4},{7,5},{8,10},{9,11},{10,... | collective-permute-start | bytes 202760 | tf_op jit(solution)/shard_map/ppermute | solution.py:307
  22.2 1.9 %collective-permute-start.13 = (bf16[8,4096]{1,0:T(8,128)(2,1)S(1)}, bf16[8,4096]{1,0:T(8,128)(2,1)S(1)}, u32[]{:S(2)}, u32[]{:S(2)}) collective-permute-start(bf16[8,4096]{1,0:T(8,128)(2,1)S(1)} %collective-permute-done.9.refs_3_), channel_id=1, source_target_pairs={{0,1},{1,0},{2,3},{3,2},{4,5},{5,4},{6,7},{7,6},{8,9},{9,8},{10,11... | collective-permute-start | bytes 196616 | tf_op jit(solution)/shard_map/ppermute | solution.py:310
  22.2 2.4 %collective-permute-start.12 = (bf16[8,4096]{1,0:T(8,128)(2,1)S(1)}, bf16[8,4096]{1,0:T(8,128)(2,1)S(1)}, u32[]{:S(2)}, u32[]{:S(2)}) collective-permute-start(bf16[8,4096]{1,0:T(8,128)(2,1)S(1)} %collective-permute-done.8.refs_2_), channel_id=1, source_target_pairs={{0,1},{1,0},{2,3},{3,2},{4,5},{5,4},{6,7},{7,6},{8,9},{9,8},{10,11... | collective-permute-start | bytes 196616 | tf_op jit(solution)/shard_map/ppermute | solution.py:310
  23.4 1.3 %collective-permute-start.11 = (bf16[8,4096]{1,0:T(8,128)(2,1)S(1)}, bf16[8,4096]{1,0:T(8,128)(2,1)S(1)}, u32[]{:S(2)}, u32[]{:S(2)}) collective-permute-start(bf16[8,4096]{1,0:T(8,128)(2,1)S(1)} %collective-permute-done.7.refs_1_), channel_id=1, source_target_pairs={{0,1},{1,0},{2,3},{3,2},{4,5},{5,4},{6,7},{7,6},{8,9},{9,8},{10,11... | collective-permute-start | bytes 196616 | tf_op jit(solution)/shard_map/ppermute | solution.py:310
  24.0 4.0 %collective-permute-start.3 = (bf16[8,4224]{1,0:T(8,128)(2,1)S(1)}, bf16[8,4224]{1,0:T(8,128)(2,1)S(1)}, u32[]{:S(2)}, u32[]{:S(2)}) collective-permute-start(bf16[8,4224]{1,0:T(8,128)(2,1)S(1)} %shard_map.103.refs_0_.refs_8_), channel_id=1, source_target_pairs={{0,1},{1,0},{2,3},{3,2},{4,5},{5,4},{6,7},{7,6},{8,9},{9,8},{10,11... | collective-permute-start | bytes 202760 | tf_op jit(solution)/shard_map/ppermute | solution.py:310
  24.1 4.0 %collective-permute-start.6 = (bf16[8,4224]{1,0:T(8,128)(2,1)S(1)}, bf16[8,4224]{1,0:T(8,128)(2,1)S(1)}, u32[]{:S(2)}, u32[]{:S(2)}) collective-permute-start(bf16[8,4224]{1,0:T(8,128)(2,1)S(1)} %collective-permute-done.2.refs_3_.refs_11_), channel_id=1, source_target_pairs={{0,1},{1,0},{2,3},{3,2},{4,5},{5,4},{6,7},{7,6},{8,9},{9,8},{10,11... | collective-permute-start | bytes 202760 | tf_op jit(solution)/shard_map/ppermute | solution.py:310
  24.6 3.5 %collective-permute-start.5 = (bf16[8,4224]{1,0:T(8,128)(2,1)S(1)}, bf16[8,4224]{1,0:T(8,128)(2,1)S(1)}, u32[]{:S(2)}, u32[]{:S(2)}) collective-permute-start(bf16[8,4224]{1,0:T(8,128)(2,1)S(1)} %collective-permute-done.1.refs_2_.refs_10_), channel_id=1, source_target_pairs={{0,1},{1,0},{2,3},{3,2},{4,5},{5,4},{6,7},{7,6},{8,9},{9,8},{10,11... | collective-permute-start | bytes 202760 | tf_op jit(solution)/shard_map/ppermute | solution.py:310
  24.7 3.4 %collective-permute-start.4 = (bf16[8,4224]{1,0:T(8,128)(2,1)S(1)}, bf16[8,4224]{1,0:T(8,128)(2,1)S(1)}, u32[]{:S(2)}, u32[]{:S(2)}) collective-permute-start(bf16[8,4224]{1,0:T(8,128)(2,1)S(1)} %collective-permute-done.refs_1_.refs_9_), channel_id=1, source_target_pairs={{0,1},{1,0},{2,3},{3,2},{4,5},{5,4},{6,7},{7,6},{8,9},{9,8},{10,11... | collective-permute-start | bytes 202760 | tf_op jit(solution)/shard_map/ppermute | solution.py:310
  25.1 1.9 %copy-start = (bf16[1,1,2,192,4096]{4,3,2,1,0:T(8,128)(2,1)S(1)}, bf16[1,1,2,192,4096]{4,3,2,1,0:T(8,128)(2,1)}, u32[]{:S(2)}) copy-start(bf16[1,1,2,192,4096]{4,3,2,1,0:T(8,128)(2,1)} %param.12) | copy-start | bytes 9437188
  27.0 1.9 %copy-start.1 = (bf16[1,1,2,192,4096]{4,3,2,1,0:T(8,128)(2,1)S(1)}, bf16[1,1,2,192,4096]{4,3,2,1,0:T(8,128)(2,1)}, u32[]{:S(2)}) copy-start(bf16[1,1,2,192,4096]{4,3,2,1,0:T(8,128)(2,1)} %param.12) | copy-start | bytes 9437188
  28.1 3.0 %copy-start.8 = (f32[1,4096]{1,0:T(1,128)S(1)}, f32[1,4096]{1,0:T(1,128)}, u32[]{:S(2)}) copy-start(f32[1,4096]{1,0:T(1,128)} %gain_ref.1) | copy-start | bytes 49156
  28.9 20.6 %copy-start.6 = (s32[1,128,8]{1,2,0:T(8,128)S(1)}, s32[1,128,8]{1,2,0:T(8,128)}, u32[]{:S(2)}) copy-start(s32[1,128,8]{1,2,0:T(8,128)} %param.9) | copy-start | bytes 12292
  30.9 2.7 %collective-permute-start.14 = (bf16[32,4224]{1,0:T(8,128)(2,1)S(1)}, bf16[32,4224]{1,0:T(8,128)(2,1)S(1)}, u32[]{:S(2)}, u32[]{:S(2)}) collective-permute-start(bf16[32,4224]{1,0:T(8,128)(2,1)S(1)} %get-tuple-element.21), channel_id=1, source_target_pairs={{0,1},{1,0},{2,3},{3,2},{4,5},{5,4},{6,7},{7,6},{8,9},{9,8},{10,11... | collective-permute-start | bytes 811016 | tf_op jit(solution)/shard_map/ppermute | solution.py:310
  31.0 5.1 %collective-permute-start.20 = (f32[1,4096]{1,0:T(1,128)S(1)}, f32[1,4096]{1,0:T(1,128)S(1)}, u32[]{:S(2)}, u32[]{:S(2)}) collective-permute-start(f32[1,4096]{1,0:T(1,128)S(1)} %copy-done.8), channel_id=1, source_target_pairs={{8,0},{9,1},{10,2},{11,3},{12,4},{13,5},{14,6},{15,7},{16,8},{17,9... | collective-permute-start | bytes 49160 | tf_op jit(solution)/shard_map/ppermute | solution.py:318
  31.6 4.6 %collective-permute-start.21 = (f32[8,128]{1,0:T(8,128)S(1)}, f32[8,128]{1,0:T(8,128)S(1)}, u32[]{:S(2)}, u32[]{:S(2)}) collective-permute-start(f32[8,128]{1,0:T(8,128)S(1)} %get-tuple-element.18.place_ref.refs_5_), channel_id=1, source_target_pairs={{8,0},{9,1},{10,2},{11,3},{12,4},{13,5},{14,6},{15,7},{16,8},{17,9... | collective-permute-start | bytes 12296 | tf_op jit(solution)/shard_map/ppermute | solution.py:318
  33.0 5.2 %collective-permute-start.19 = (bf16[8,4096]{1,0:T(8,128)(2,1)S(1)}, bf16[8,4096]{1,0:T(8,128)(2,1)S(1)}, u32[]{:S(2)}, u32[]{:S(2)}) collective-permute-start(bf16[8,4096]{1,0:T(8,128)(2,1)S(1)} %get-tuple-element.26), channel_id=1, source_target_pairs={{8,0},{9,1},{10,2},{11,3},{12,4},{13,5},{14,6},{15,7},{16,8},{17,9... | collective-permute-start | bytes 196616 | tf_op jit(solution)/shard_map/ppermute | solution.py:318
  33.6 6.9 %collective-permute-start.25 = (f32[8,128]{1,0:T(8,128)S(1)}, f32[8,128]{1,0:T(8,128)S(1)}, u32[]{:S(2)}, u32[]{:S(2)}) collective-permute-start(f32[8,128]{1,0:T(8,128)S(1)} %get-tuple-element.32), channel_id=1, source_target_pairs={{0,6},{1,7},{2,4},{3,5},{4,2},{5,3},{6,0},{7,1},{8,14},{9,15},{10,... | collective-permute-start | bytes 12296 | tf_op jit(solution)/shard_map/ppermute | solution.py:307
  36.2 4.5 %collective-permute-start.24 = (f32[8,128]{1,0:T(8,128)S(1)}, f32[8,128]{1,0:T(8,128)S(1)}, u32[]{:S(2)}, u32[]{:S(2)}) collective-permute-start(f32[8,128]{1,0:T(8,128)S(1)} %get-tuple-element.33), channel_id=1, source_target_pairs={{0,4},{1,5},{2,6},{3,7},{4,0},{5,1},{6,2},{7,3},{8,12},{9,13},{10,... | collective-permute-start | bytes 12296 | tf_op jit(solution)/shard_map/ppermute | solution.py:307
  36.2 8.2 %collective-permute-start.23 = (f32[8,128]{1,0:T(8,128)S(1)}, f32[8,128]{1,0:T(8,128)S(1)}, u32[]{:S(2)}, u32[]{:S(2)}) collective-permute-start(f32[8,128]{1,0:T(8,128)S(1)} %get-tuple-element.34), channel_id=1, source_target_pairs={{0,2},{1,3},{2,0},{3,1},{4,6},{5,7},{6,4},{7,5},{8,10},{9,11},{10,... | collective-permute-start | bytes 12296 | tf_op jit(solution)/shard_map/ppermute | solution.py:307
  38.2 11.9 %collective-permute-start.15 = (bf16[8,4096]{1,0:T(8,128)(2,1)S(1)}, bf16[8,4096]{1,0:T(8,128)(2,1)S(1)}, u32[]{:S(2)}, u32[]{:S(2)}) collective-permute-start(bf16[8,4096]{1,0:T(8,128)(2,1)S(1)} %get-tuple-element.22), channel_id=1, source_target_pairs={{8,0},{9,1},{10,2},{11,3},{12,4},{13,5},{14,6},{15,7},{16,8},{17,9... | collective-permute-start | bytes 196616 | tf_op jit(solution)/shard_map/ppermute | solution.py:318
  40.5 9.5 %collective-permute-start.16 = (bf16[8,4096]{1,0:T(8,128)(2,1)S(1)}, bf16[8,4096]{1,0:T(8,128)(2,1)S(1)}, u32[]{:S(2)}, u32[]{:S(2)}) collective-permute-start(bf16[8,4096]{1,0:T(8,128)(2,1)S(1)} %get-tuple-element.23), channel_id=1, source_target_pairs={{8,2},{9,3},{10,0},{11,1},{12,6},{13,7},{14,4},{15,5},{16,10},{17,... | collective-permute-start | bytes 196616 | tf_op jit(solution)/shard_map/ppermute | solution.py:318
  40.7 9.4 %collective-permute-start.17 = (bf16[8,4096]{1,0:T(8,128)(2,1)S(1)}, bf16[8,4096]{1,0:T(8,128)(2,1)S(1)}, u32[]{:S(2)}, u32[]{:S(2)}) collective-permute-start(bf16[8,4096]{1,0:T(8,128)(2,1)S(1)} %get-tuple-element.24), channel_id=1, source_target_pairs={{8,4},{9,5},{10,6},{11,7},{12,0},{13,1},{14,2},{15,3},{16,12},{17,... | collective-permute-start | bytes 196616 | tf_op jit(solution)/shard_map/ppermute | solution.py:318
  44.4 7.0 %collective-permute-start.18 = (bf16[8,4096]{1,0:T(8,128)(2,1)S(1)}, bf16[8,4096]{1,0:T(8,128)(2,1)S(1)}, u32[]{:S(2)}, u32[]{:S(2)}) collective-permute-start(bf16[8,4096]{1,0:T(8,128)(2,1)S(1)} %get-tuple-element.25), channel_id=1, source_target_pairs={{8,6},{9,7},{10,4},{11,5},{12,2},{13,3},{14,0},{15,1},{16,14},{17,... | collective-permute-start | bytes 196616 | tf_op jit(solution)/shard_map/ppermute | solution.py:318
  (4 other events, 3.3 us)

commit v2 on v1

--- a/solution.py
+++ b/solution.py
@@ -139,9 +139,11 @@
     )
 
 
-def call(kernel, outs, flops, moved, limit=24, scratch=()):
+def call(kernel, outs, flops, moved, in_specs=None, scratch=(), limit=24):
+    given = {} if in_specs is None else {"in_specs": in_specs}
     return pl.pallas_call(
         kernel,
+        **given,
         out_shape=[jax.ShapeDtypeStruct(shape, kind) for shape, kind in outs],
         scratch_shapes=list(scratch),
         compiler_params=pltpu.CompilerParams(vmem_limit_bytes=limit << 20),
@@ -149,6 +151,10 @@
     )
 
 
+IN_HBM = pl.BlockSpec(memory_space=pltpu.HBM)
+IN_VMEM = pl.BlockSpec(memory_space=pltpu.VMEM)
+
+
 def take_rows(place, block):
     return lax.dot_general(place, block, (((1,), (0,)), ((), ())), preferred_element_type=F32)
 
@@ -158,10 +164,26 @@
     return rows / rms, rms
 
 
-def place_kernel(ids_ref, hidden_ref, gain_ref, in_ref, raw_ref, place_ref):
+def rows_kernel(ids_hbm, weight_hbm, gain_hbm, hidden_hbm, grad_hbm, rows_ref, side_ref, place_ref,
+                ids_ref, weight_ref, gain_ref, hidden_ref, grad_ref, sems):
+    copies = [
+        pltpu.make_async_copy(src, dst, sems.at[i])
+        for i, (src, dst) in enumerate([
+            (ids_hbm, ids_ref),
+            (hidden_hbm, hidden_ref),
+            (gain_hbm, gain_ref),
+            (weight_hbm, weight_ref),
+            (grad_hbm, grad_ref),
+        ])
+    ]
+    for copy in copies:
+        copy.start()
+    width = hidden_ref.shape[1]
     tokens = ids_ref.shape[1]
     cap = SPECIALIST_CAP
-    member = jnp.max((ids_ref[...] == 0).astype(F32), axis=0, keepdims=True)
+    copies[0].wait()
+    hit = ids_ref[...] == 0
+    member = jnp.max(hit.astype(F32), axis=0, keepdims=True)
     member = jnp.broadcast_to(member, (cap, tokens))
     earlier = lax.broadcasted_iota(jnp.int32, (tokens, tokens), 0) < lax.broadcasted_iota(
         jnp.int32, (tokens, tokens), 1
@@ -170,110 +192,142 @@
     slot = lax.broadcasted_iota(jnp.int32, (cap, tokens), 0).astype(F32)
     place = jnp.where(position == slot, member, 0.0)
     place_ref[...] = place
-    rows = take_rows(place.astype(BF16), hidden_ref[...])
-    raw_ref[...] = rows.astype(BF16)
-    normed, _ = normed_rows(rows)
-    in_ref[...] = (normed * gain_ref[...]).astype(BF16)
-
-
-def grad_rows_kernel(ids_ref, weight_ref, place_ref, grad_ref, out_ref):
-    width = grad_ref.shape[1]
-    place = place_ref[...]
-    out_ref[:, :width] = take_rows(place.astype(BF16), grad_ref[...]).astype(BF16)
+    copies[1].wait()
+    raw = take_rows(place.astype(BF16), hidden_ref[...])
+    normed, _ = normed_rows(raw)
+    copies[2].wait()
+    gain = gain_ref[...]
+    normed_in = normed * gain
+    high = gain.astype(BF16).astype(F32)
+    middle = (gain - high).astype(BF16).astype(F32)
+    low = gain - high - middle
+    blank = jnp.zeros((cap - 3, width), F32)
+    side_ref[:, :width] = jnp.concatenate([raw, high, middle, low, blank], axis=0).astype(BF16)
+    side_ref[:, width:] = jnp.concatenate([place, jnp.zeros((cap, tokens), F32)], axis=0).astype(BF16)
+    copies[3].wait()
     weight = jnp.sum(
-        jnp.where(ids_ref[...] == 0, weight_ref[...].astype(F32), 0.0), axis=0, keepdims=True
+        jnp.where(hit, weight_ref[...].astype(F32), 0.0), axis=0, keepdims=True
     )
     taken = jnp.sum(place * weight, axis=1, keepdims=True)
-    out_ref[:, width:] = jnp.broadcast_to(taken, (place.shape[0], LANES)).astype(BF16)
-
-
-def stacked(refs, start, stop):
-    return jnp.concatenate([r[:, start:stop].astype(F32) for r in refs], axis=0)
-
-
-def project_kernel(*refs):
-    *blocks, slab_ref, out_ref = refs
-    width = slab_ref.shape[1]
-    out_ref[...] = rows_product(stacked(blocks, 0, width).astype(BF16), slab_ref[...])
+    taken = jnp.broadcast_to(taken, (cap, LANES))
+    rows_ref[:, width:] = jnp.concatenate([taken, taken], axis=0).astype(BF16)
+    copies[4].wait()
+    grad = take_rows(place.astype(BF16), grad_ref[...])
+    rows_ref[:, :width] = jnp.concatenate([normed_in, grad], axis=0).astype(BF16)
+
+
+def fetch_kernel(slab_hbm, down_hbm, after_ref, slab_ref, down_ref, sems):
+    del after_ref
+    first = pltpu.make_async_copy(slab_hbm, slab_ref, sems.at[0])
+    second = pltpu.make_async_copy(down_hbm, down_ref, sems.at[1])
+    first.start()
+    second.start()
+    first.wait()
+    second.wait()
+
+
+def halves(rows, cap):
+    blocks = range(rows.shape[0] // (2 * cap))
+    return [
+        jnp.concatenate([rows[(2 * b + h) * cap : (2 * b + h + 1) * cap] for b in blocks], axis=0)
+        for h in (0, 1)
+    ]
+
+
+def padded(rows, half, cap):
+    blank = jnp.zeros((cap, rows.shape[1]), rows.dtype)
+    pieces = []
+    for b in range(rows.shape[0] // cap):
+        own = rows[b * cap : (b + 1) * cap]
+        pieces += [own, blank] if half == 0 else [blank, own]
+    return jnp.concatenate(pieces, axis=0)
 
 
 def hidden_kernel(*refs):
-    *blocks, pre_ref, down_ref, slab_ref, keep_ref, send_ref, both_ref, act_ref = refs
+    *blocks, slab_ref, down_ref, keep_ref, send_ref, both_ref, act_ref = refs
     hidden, width = down_ref.shape
     half = keep_ref.shape[0]
-    grad = stacked(blocks, 0, width).astype(BF16)
-    weight = stacked(blocks, width, width + LANES)[:, :1]
-    back = rows_product(grad, down_ref[...])
-    gate = pre_ref[:, :hidden]
-    up = pre_ref[:, hidden:]
+    cap = SPECIALIST_CAP
+    rows = jnp.concatenate([r[:, :width] for r in blocks], axis=0)
+    pre, _ = halves(rows_product(rows, slab_ref[...]), cap)
+    _, back = halves(rows_product(rows, down_ref[...]), cap)
+    weight = jnp.concatenate([r[:, width:].astype(F32)[:cap, :1] for r in blocks], axis=0)
+    gate = pre[:, :hidden]
+    up = pre[:, hidden:]
     sig = jax.nn.sigmoid(gate)
     active = gate * sig
     act = active * up
-    act_ref[...] = (weight * act).T.astype(BF16)
     into = weight * back
     both = jnp.concatenate(
         [into * up * sig * (1.0 + gate * (1.0 - sig)), into * active], axis=1
     )
-    both_ref[...] = both.T.astype(BF16)
     part = take_rows(both.astype(BF16), slab_ref[...]).astype(BF16)
+    send_ref[:, :width] = part[half:]
     keep_ref[:, :width] = part[:half]
-    send_ref[:, :width] = part[half:]
     comb = jnp.sum(act * back, axis=1, keepdims=True)
     comb = jnp.broadcast_to(comb, (2 * half, LANES)).astype(BF16)
+    send_ref[:, width:] = comb[half:]
     keep_ref[:, width:] = comb[:half]
-    send_ref[:, width:] = comb[half:]
+    both_ref[...] = padded(both, 0, cap).T.astype(BF16)
+    act_ref[...] = padded(weight * act, 1, cap).T.astype(BF16)
 
 
 def join_kernel(keep_ref, got_ref, *refs):
     *out_refs, comb_ref = refs
-    width = out_refs[0].shape[1]
+    rows, width = out_refs[0].shape
     total = keep_ref[...].astype(F32) + got_ref[...].astype(F32)
-    rows = out_refs[0].shape[0]
     for k, out_ref in enumerate(out_refs):
         out_ref[...] = total[k * rows : (k + 1) * rows, :width].astype(BF16)
     comb_ref[...] = total[:, width:]
 
 
-def weights_kernel(*refs):
-    *blocks, both_ref, act_ref, both_out, act_out = refs
-    ins, grads = blocks[: len(blocks) // 2], blocks[len(blocks) // 2 :]
-    step = both_out.shape[1]
-    both_out[...] = take_rows(both_ref[...], stacked(ins, 0, step).astype(BF16)).astype(BF16)
-    act_out[...] = take_rows(act_ref[...], stacked(grads, 0, step).astype(BF16)).astype(BF16)
-
-
-def weight_grads(ins, grads, both, act, width):
+def weights_kernel(chips, *refs):
+    blocks, refs = refs[: 2 * chips], refs[2 * chips :]
+    both_ref, act_ref, comb_ref, both_out, act_out, *comb_refs = refs
+    rows = jnp.concatenate([r[...] for r in blocks], axis=0)
+    both_out[...] = take_rows(both_ref[...], rows).astype(BF16)
+    act_out[...] = take_rows(act_ref[...], rows).astype(BF16)
+    cap = comb_refs[0].shape[0]
+    for k, out_ref in enumerate(comb_refs):
+        out_ref[...] = comb_ref[k * cap : (k + 1) * cap]
+
+
+def weight_grads(blocks, both, act, comb, chips, width):
     chunk = min(width, 1024)
-    rows = ins[0].shape[0]
-    block = pl.BlockSpec((rows, chunk), lambda i: (0, i))
-    whole = lambda a: pl.BlockSpec(a.shape, lambda i: (0, 0))
+    across = lambda rows: pl.BlockSpec((rows, chunk), lambda i: (0, i))
+    whole = lambda shape: pl.BlockSpec(shape, lambda i: (0, 0))
+    comb_shape = (comb.shape[0] // chips, comb.shape[1])
+    hidden = act.shape[0]
     return pl.pallas_call(
-        weights_kernel,
+        functools.partial(weights_kernel, chips),
         grid=(width // chunk,),
-        in_specs=[block] * (len(ins) + len(grads)) + [whole(both), whole(act)],
-        out_specs=[
-            pl.BlockSpec((both.shape[0], chunk), lambda i: (0, i)),
-            pl.BlockSpec((act.shape[0], chunk), lambda i: (0, i)),
-        ],
+        in_specs=[across(b.shape[0]) for b in blocks]
+        + [whole(both.shape), whole(act.shape), whole(comb.shape)],
+        out_specs=[across(2 * hidden), across(hidden)] + [whole(comb_shape)] * chips,
         out_shape=[
-            jax.ShapeDtypeStruct((both.shape[0], width), BF16),
-            jax.ShapeDtypeStruct((act.shape[0], width), BF16),
-        ],
+            jax.ShapeDtypeStruct((2 * hidden, width), BF16),
+            jax.ShapeDtypeStruct((hidden, width), BF16),
+        ]
+        + [jax.ShapeDtypeStruct(comb_shape, F32)] * chips,
         compiler_params=pltpu.CompilerParams(vmem_limit_bytes=24 << 20),
         cost_estimate=pl.CostEstimate(
-            flops=2 * 64 * 576 * width, bytes_accessed=2 * 700 * width, transcendentals=0
-        ),
-    )(*ins, *grads, both, act)
+            flops=6 * 128 * hidden * width, bytes_accessed=6 * hidden * width, transcendentals=0
+        ),
+    )(*blocks, both, act, comb)
 
 
 def finish_kernel(*refs):
-    *parts, raw_ref, gain_ref, place_ref, grad_ref, out_ref = refs
-    place = place_ref[...]
-    normed, rms = normed_rows(raw_ref[...].astype(F32))
+    *parts, side_ref, grad_ref, out_ref = refs
+    cap = SPECIALIST_CAP
+    width = grad_ref.shape[1]
+    side = side_ref[...].astype(F32)
+    place = side[:cap, width:]
+    gain = side[cap : cap + 1, :width] + side[cap + 1 : cap + 2, :width] + side[cap + 2 : cap + 3, :width]
+    normed, rms = normed_rows(side[:cap, :width])
     grad = grad_ref[...]
     own = take_rows(place.astype(BF16), grad)
     total = sum(p[...].astype(F32) for p in parts)
-    scaled = total * gain_ref[...]
+    scaled = total * gain
     inner = jnp.mean(scaled * normed, axis=-1, keepdims=True)
     rows = (own + (scaled - normed * inner) / rms).astype(BF16)
     back = place.T
@@ -301,7 +355,9 @@
     slab = w_gate_up.reshape(2 * hidden, width)
     down = w_down.reshape(hidden, width)
     grad = out_grad[0]
+    in_hbm = lambda a: pltpu.with_memory_space_constraint(a, pltpu.HBM)
     wide = width + LANES
+    total_rows = devices * cap
 
     def across(block, offset):
         return lax.ppermute(block, "expert", [(i, i ^ (2 * offset)) for i in range(devices)])
@@ -317,39 +373,44 @@
         ]
         return lax.ppermute(block, ("pipe", "expert"), route)
 
+    rows, side, place = call(
+        rows_kernel,
+        [((2 * cap, wide), BF16), ((2 * cap, wide), BF16), ((cap, tokens), F32)],
+        4 * tokens * width * cap,
+        4 * tokens * width,
+        in_specs=[IN_HBM] * 5,
+        scratch=[
+            pltpu.VMEM(ids.shape, ids.dtype),
+            pltpu.VMEM(weights.shape, weights.dtype),
+            pltpu.VMEM(norm_gain.shape, norm_gain.dtype),
+            pltpu.VMEM((tokens, width), BF16),
+            pltpu.VMEM((tokens, width), BF16),
+            pltpu.SemaphoreType.DMA((5,)),
+        ],
+    )(*map(in_hbm, (ids, weights, norm_gain, hidden_in[0], grad)))
+    lane = [rows] + [across(rows, k) for k in range(1, chips)]
+    next_side = handed(side, 0)
     next_grad = handed(grad, 0)
-    row_in, row_raw, place = call(
-        place_kernel,
-        [((cap, width), BF16), ((cap, width), BF16), ((cap, tokens), F32)],
-        2 * tokens * width * cap,
-        2 * tokens * width,
-    )(ids, hidden_in[0], norm_gain)
-    lane_in = [row_in] + [across(row_in, k) for k in range(1, chips)]
-    (row_grad,) = call(
-        grad_rows_kernel, [((cap, wide), BF16)], 2 * tokens * width * cap, 2 * tokens * width
-    )(ids, weights, place, grad)
-    lane_grad = [row_grad] + [across(row_grad, k) for k in range(1, chips)]
-    next_raw, next_gain, next_place = handed(row_raw, 0), handed(norm_gain, 0), handed(place, 0)
-    all_in = lane_in + [beside(b) for b in lane_in]
-    all_grad = lane_grad + [beside(b) for b in lane_grad]
-    total_rows = devices * cap
-    (pre,) = call(
-        project_kernel,
-        [((total_rows, 2 * hidden), F32)],
-        4 * total_rows * hidden * width,
-        4 * hidden * width,
-    )(*all_in, slab)
+    slab_near, down_near = call(
+        fetch_kernel,
+        [(slab.shape, BF16), (down.shape, BF16)],
+        0,
+        6 * hidden * width,
+        in_specs=[IN_HBM, IN_HBM, pl.BlockSpec(memory_space=pl.ANY)],
+        scratch=[pltpu.SemaphoreType.DMA((2,))],
+    )(in_hbm(slab), in_hbm(down), place)
+    blocks = lane + [beside(b) for b in lane]
     keep, send, both, act = call(
         hidden_kernel,
         [
             ((total_rows // 2, wide), BF16),
             ((total_rows // 2, wide), BF16),
-            ((2 * hidden, total_rows), BF16),
-            ((hidden, total_rows), BF16),
+            ((2 * hidden, 2 * total_rows), BF16),
+            ((hidden, 2 * total_rows), BF16),
         ],
-        6 * total_rows * hidden * width,
+        10 * total_rows * hidden * width,
         6 * hidden * width,
-    )(*all_grad, pre, down, slab)
+    )(*blocks, slab_near, down_near)
     *parts, comb = call(
         join_kernel,
         [((cap, width), BF16)] * chips + [((total_rows // 2, LANES), F32)],
@@ -357,12 +418,11 @@
         4 * total_rows * width,
     )(keep, beside(send))
     got = [handed(parts[k], k) for k in range(chips)]
-    comb_parts = [comb[k * cap : (k + 1) * cap] for k in range(chips)]
+    gate_up_out, down_out, *comb_parts = weight_grads(blocks, both, act, comb, chips, width)
     comb_got = [comb_parts[0]] + [across(comb_parts[k], k) for k in range(1, chips)]
-    gate_up_out, down_out = weight_grads(all_in, all_grad, both, act, width)
     (combined,) = call(combine_kernel, [((SPLIT, tokens), F32)], 1000, 1000)(*comb_got, ids, place)
     (out,) = call(finish_kernel, [((tokens, width), BF16)], 4 * tokens * width * cap, 4 * tokens * width)(
-        *got, next_raw, next_gain, next_place, next_grad
+        *got, next_side, next_grad
     )
     return (
         out[None],

time: 53.4 us -> 51.1 us (0.957)
  waiting for transfers between devices: 6.23 us -> 15.1 us
  starting transfers between devices: 29.6 us -> 21.6 us
  local copies, waits for them, and re-layouts: 7.18 us -> 0.01 us
  Pallas kernels: 9.27 us -> 13.5 us
    unnamed x20 -> x2, local copies, waits for them, and re-layouts: 7.18 us -> 0.01 us
    ppermute x9 -> x6, waiting for transfers between devices: 4.86 us -> 10.1 us  [across(): lax.ppermute(block, 'expert', [(i, i ^ 2 * offset) for i in range(devices)])]
    ppermute x9 -> x6, starting transfers between devices: 13.3 us -> 8.84 us  [across(): lax.ppermute(block, 'expert', [(i, i ^ 2 * offset) for i in range(devices)])]
    pallas_call x4 -> x3, Pallas kernels: 4.95 us -> 8.8 us  [the longest x1 4.37 us: weight_grads(): pl.pallas_call(functools.partial(weights_kernel, chips), grid=(width // c...]
    ppermute x8 -> x6, waiting for transfers between devices: 1.32 us -> 4.01 us  [handed(): return lax.ppermute(block, ('pipe', 'expert'), route)]
    ppermute x8 -> x6, starting transfers between devices: 14.5 us -> 12.2 us  [handed(): return lax.ppermute(block, ('pipe', 'expert'), route)]
    ppermute x9 -> x5, starting transfers between devices: 1.73 us -> 0.59 us  [beside(): return lax.ppermute(block, 'expert', [(i, i ^ 1) for i in range(devices)])]
    ppermute x9 -> x5, waiting for transfers between devices: 0.05 us -> 0.96 us  [beside(): return lax.ppermute(block, 'expert', [(i, i ^ 1) for i in range(devices)])]
  transfers between devices with their start and end apart: 26 -> 17, of which waited for: 4 -> 5; matrix products, arithmetic and copies ran while one was open for 0% -> 0% of each run, Pallas kernels for 14% -> 23%
where the time goes in v2:
time: 51.1 us; the launch traced here: 51 us
  starting transfers between devices  21.6 us (42%)
  waiting for transfers between devices  15.1 us (30%)
  Pallas kernels  13.5 us (26%)
  between operations  0.72 us (1%)
    ppermute x6, starting transfers between devices, handed(): return lax.ppermute(block, ('pipe', 'expert'), route)  12.2 us
    ppermute x6, waiting for transfers between devices, across(): lax.ppermute(block, 'expert', [(i, i ^ 2 * offset) for i in range(devices)])  10.1 us
    ppermute x6, starting transfers between devices, across(): lax.ppermute(block, 'expert', [(i, i ^ 2 * offset) for i in range(devices)])  8.84 us
    pallas_call x1, Pallas kernels, weight_grads(): pl.pallas_call(functools.partial(weights_kernel, chips), grid=(width // c...  4.37 us
    ppermute x6, waiting for transfers between devices, handed(): return lax.ppermute(block, ('pipe', 'expert'), route)  4.01 us
    pallas_call x1, Pallas kernels, on_one(): call(hidden_kernel, [((total_rows // 2, wide), BF16), ((total_rows // 2,...  2.37 us
    pallas_call x1, Pallas kernels, on_one(): call(fetch_kernel, [(slab.shape, BF16), (down.shape, BF16)], 0, 6 * hidde...  2.37 us
    pallas_call x1, Pallas kernels, on_one(): call(rows_kernel, [((2 * cap, wide), BF16), ((2 * cap, wide), BF16), ((ca...  2.06 us
  transfers between devices with their start and end apart: 17, of which 5 were waited for; matrix products, arithmetic and copies ran while one was open for 0% of the time, Pallas kernels for 23%

profile of v2, /device:TPU:0, one launch (start us, length us, event | category | flops | bytes accessed | tf_op | source)
XLA Modules:
  0.0 51.0 jit_solution(13296388284441827646)
XLA Ops:
  0.6 3.9 %collective-permute-start.13 = (bf16[128,4096]{1,0:T(8,128)(2,1)}, bf16[128,4096]{1,0:T(8,128)(2,1)S(1)}, u32[]{:S(2)}, u32[]{:S(2)}) collective-permute-start(bf16[128,4096]{1,0:T(8,128)(2,1)} %bitcast.22), channel_id=1, source_target_pairs={{8,0},{9,1},{10,2},{11,3},{12,4},{13,5},{14,6},{15,7},{16,8},{17,9... | collective-permute-start | bytes 3145736 | tf_op jit(solution)/shard_map/ppermute | solution.py:374
  4.6 2.1 %shard_map.102 = (bf16[16,4224]{1,0:T(8,128)(2,1)S(1)}, bf16[16,4224]{1,0:T(8,128)(2,1)S(1)}, f32[8,128]{1,0:T(8,128)S(1)}) custom-call(s32[8,128]{1,0:T(8,128)} %bitcast.16, bf16[8,128]{1,0:T(8,128)(2,1)} %bitcast.25, f32[1,4096]{1,0:T(1,128)} %gain_hbm.1, bf16[128,4096]{1,0:T(8,128)(2,1)} %bitcast.21, bf16[128,4096]{1,0:T(8,128)(2,1)} %bitcast.23), custom_call_target="tpu_custom_call" | custom-call | flops 16777216 | bytes 2097152 | tf_op jit(solution)/shard_map/pallas_call | solution.py:376
  6.6 1.6 %collective-permute-start = (bf16[16,4224]{1,0:T(8,128)(2,1)S(1)}, bf16[16,4224]{1,0:T(8,128)(2,1)S(1)}, u32[]{:S(2)}, u32[]{:S(2)}) collective-permute-start(bf16[16,4224]{1,0:T(8,128)(2,1)S(1)} %get-tuple-element.24.refs_0_), channel_id=1, source_target_pairs={{0,2},{1,3},{2,0},{3,1},{4,6},{5,7},{6,4},{7,5},{8,10},{9,11},{10,... | collective-permute-start | bytes 405512 | tf_op jit(solution)/shard_map/ppermute | solution.py:363
  8.3 2.6 %collective-permute-start.1 = (bf16[16,4224]{1,0:T(8,128)(2,1)S(1)}, bf16[16,4224]{1,0:T(8,128)(2,1)S(1)}, u32[]{:S(2)}, u32[]{:S(2)}) collective-permute-start(bf16[16,4224]{1,0:T(8,128)(2,1)S(1)} %get-tuple-element.24.refs_0_), channel_id=1, source_target_pairs={{0,4},{1,5},{2,6},{3,7},{4,0},{5,1},{6,2},{7,3},{8,12},{9,13},{10,... | collective-permute-start | bytes 405512 | tf_op jit(solution)/shard_map/ppermute | solution.py:363
  10.9 0.2 collective-permute-start.2
  11.1 2.2 %collective-permute-done.refs_1_ = bf16[16,4224]{1,0:T(8,128)(2,1)S(1)} collective-permute-done((bf16[16,4224]{1,0:T(8,128)(2,1)S(1)}, bf16[16,4224]{1,0:T(8,128)(2,1)S(1)}, u32[]{:S(2)}, u32[]{:S(2)}) %collective-permute-start) | collective-permute-done | bytes 135200 | tf_op jit(solution)/shard_map/ppermute | solution.py:363
  13.3 7.9 %collective-permute-done.1.refs_2_ = bf16[16,4224]{1,0:T(8,128)(2,1)S(1)} collective-permute-done((bf16[16,4224]{1,0:T(8,128)(2,1)S(1)}, bf16[16,4224]{1,0:T(8,128)(2,1)S(1)}, u32[]{:S(2)}, u32[]{:S(2)}) %collective-permute-start.1) | collective-permute-done | bytes 135200 | tf_op jit(solution)/shard_map/ppermute | solution.py:363
  21.2 0.5 collective-permute-start.6
  21.8 2.4 %shard_map.103 = (bf16[384,4096]{1,0:T(8,128)(2,1)S(1)}, bf16[192,4096]{1,0:T(8,128)(2,1)S(1)}) custom-call(bf16[384,4096]{1,0:T(8,128)(2,1)} %bitcast.18, bf16[192,4096]{1,0:T(8,128)(2,1)} %bitcast.19, f32[8,128]{1,0:T(8,128)S(1)} %get-tuple-element.25.after_ref.refs_5_), custom_call_target="tpu_custom_call" | custom-call | bytes 4718592 | tf_op jit(solution)/shard_map/pallas_call | solution.py:394
  24.1 0.0 collective-permute-done.3.refs_4_
  24.2 0.0 collective-permute-done.6.refs_7_
  24.2 0.0 copy-start
  24.2 2.4 %shard_map.104 = (bf16[32,4224]{1,0:T(8,128)(2,1)S(1)}, bf16[32,4224]{1,0:T(8,128)(2,1)S(1)}, bf16[384,128]{1,0:T(8,128)(2,1)S(1)}, bf16[192,128]{1,0:T(8,128)(2,1)S(1)}) custom-call(bf16[16,4224]{1,0:T(8,128)(2,1)S(1)} %get-tuple-element.24.refs_0_, bf16[16,4224]{1,0:T(8,128)(2,1)S(1)} %collective-permute-done.refs_1_, ...), custom_call_target="tpu_custom_call" | custom-call | flops 503316480 | bytes 4718592 | tf_op jit(solution)/shard_map/pallas_call | solution.py:403
  26.6 0.1 collective-permute-start.7
  26.6 0.6 %collective-permute-start.12 = (bf16[16,4224]{1,0:T(8,128)(2,1)S(1)}, bf16[16,4224]{1,0:T(8,128)(2,1)S(1)}, u32[]{:S(2)}, u32[]{:S(2)}) collective-permute-start(bf16[16,4224]{1,0:T(8,128)(2,1)S(1)} %get-tuple-element.34), channel_id=1, source_target_pairs={{8,0},{9,1},{10,2},{11,3},{12,4},{13,5},{14,6},{15,7},{16,8},{17,9... | collective-permute-start | bytes 405512 | tf_op jit(solution)/shard_map/ppermute | solution.py:374
  27.2 0.9 %collective-permute-done.7.got_ref = bf16[32,4224]{1,0:T(8,128)(2,1)S(1)} collective-permute-done((bf16[32,4224]{1,0:T(8,128)(2,1)S(1)}, bf16[32,4224]{1,0:T(8,128)(2,1)S(1)}, u32[]{:S(2)}, u32[]{:S(2)}) %collective-permute-start.7) | collective-permute-done | bytes 270368 | tf_op jit(solution)/shard_map/ppermute | solution.py:366
  28.2 0.1 shard_map.105
  28.2 4.4 %shard_map.107 = (bf16[384,4096]{1,0:T(8,128)(2,1)}, bf16[192,4096]{1,0:T(8,128)(2,1)}, f32[8,128]{1,0:T(8,128)S(1)}, f32[8,128]{1,0:T(8,128)S(1)}, f32[8,128]{1,0:T(8,128)S(1)}, /*index=5*/f32[8,128]{1,0:T(8,128)S(1)}) custom-call(bf16[16,4224]{1,0:T(8,128)(2,1)S(1)} %get-tuple-element.24.refs_0_, bf16[16,4224]{1,0:T(8,128)(2,1)S(1)} %collective-permute-done.refs_1_, ...), custom_call_target="tpu_custom_call" | custom-call | flops 603979776 | bytes 4718592 | tf_op jit(solution)/shard_map/pallas_call | solution.py:301
  32.6 1.7 %collective-permute-start.14 = (f32[8,128]{1,0:T(8,128)S(1)}, f32[8,128]{1,0:T(8,128)S(1)}, u32[]{:S(2)}, u32[]{:S(2)}) collective-permute-start(f32[8,128]{1,0:T(8,128)S(1)} %get-tuple-element.41), channel_id=1, source_target_pairs={{0,2},{1,3},{2,0},{3,1},{4,6},{5,7},{6,4},{7,5},{8,10},{9,11},{10,... | collective-permute-start | bytes 12296 | tf_op jit(solution)/shard_map/ppermute | solution.py:363
  34.3 1.3 %collective-permute-start.15 = (f32[8,128]{1,0:T(8,128)S(1)}, f32[8,128]{1,0:T(8,128)S(1)}, u32[]{:S(2)}, u32[]{:S(2)}) collective-permute-start(f32[8,128]{1,0:T(8,128)S(1)} %get-tuple-element.42), channel_id=1, source_target_pairs={{0,4},{1,5},{2,6},{3,7},{4,0},{5,1},{6,2},{7,3},{8,12},{9,13},{10,... | collective-permute-start | bytes 12296 | tf_op jit(solution)/shard_map/ppermute | solution.py:363
  35.6 1.4 %collective-permute-start.16 = (f32[8,128]{1,0:T(8,128)S(1)}, f32[8,128]{1,0:T(8,128)S(1)}, u32[]{:S(2)}, u32[]{:S(2)}) collective-permute-start(f32[8,128]{1,0:T(8,128)S(1)} %get-tuple-element.43), channel_id=1, source_target_pairs={{0,6},{1,7},{2,4},{3,5},{4,2},{5,3},{6,0},{7,1},{8,14},{9,15},{10,... | collective-permute-start | bytes 12296 | tf_op jit(solution)/shard_map/ppermute | solution.py:363
  37.0 0.0 collective-permute-done.12.refs_4_
  37.0 0.5 %collective-permute-start.8 = (bf16[8,4096]{1,0:T(8,128)(2,1)S(1)}, bf16[8,4096]{1,0:T(8,128)(2,1)S(1)}, u32[]{:S(2)}, u32[]{:S(2)}) collective-permute-start(bf16[8,4096]{1,0:T(8,128)(2,1)S(1)} %get-tuple-element.30), channel_id=1, source_target_pairs={{8,0},{9,1},{10,2},{11,3},{12,4},{13,5},{14,6},{15,7},{16,8},{17,9... | collective-permute-start | bytes 196616 | tf_op jit(solution)/shard_map/ppermute | solution.py:374
  37.6 1.6 %collective-permute-start.9 = (bf16[8,4096]{1,0:T(8,128)(2,1)S(1)}, bf16[8,4096]{1,0:T(8,128)(2,1)S(1)}, u32[]{:S(2)}, u32[]{:S(2)}) collective-permute-start(bf16[8,4096]{1,0:T(8,128)(2,1)S(1)} %get-tuple-element.31), channel_id=1, source_target_pairs={{8,2},{9,3},{10,0},{11,1},{12,6},{13,7},{14,4},{15,5},{16,10},{17,... | collective-permute-start | bytes 196616 | tf_op jit(solution)/shard_map/ppermute | solution.py:374
  39.2 3.1 %collective-permute-start.10 = (bf16[8,4096]{1,0:T(8,128)(2,1)S(1)}, bf16[8,4096]{1,0:T(8,128)(2,1)S(1)}, u32[]{:S(2)}, u32[]{:S(2)}) collective-permute-start(bf16[8,4096]{1,0:T(8,128)(2,1)S(1)} %get-tuple-element.32), channel_id=1, source_target_pairs={{8,4},{9,5},{10,6},{11,7},{12,0},{13,1},{14,2},{15,3},{16,12},{17,... | collective-permute-start | bytes 196616 | tf_op jit(solution)/shard_map/ppermute | solution.py:374
  42.3 0.0 collective-permute-done.16.refs_3_
  42.3 2.3 %collective-permute-start.11 = (bf16[8,4096]{1,0:T(8,128)(2,1)S(1)}, bf16[8,4096]{1,0:T(8,128)(2,1)S(1)}, u32[]{:S(2)}, u32[]{:S(2)}) collective-permute-start(bf16[8,4096]{1,0:T(8,128)(2,1)S(1)} %get-tuple-element.33), channel_id=1, source_target_pairs={{8,6},{9,7},{10,4},{11,5},{12,2},{13,3},{14,0},{15,1},{16,14},{17,... | collective-permute-start | bytes 196616 | tf_op jit(solution)/shard_map/ppermute | solution.py:374
  44.7 0.6 %shard_map.108 = f32[8,128]{1,0:T(8,128)} custom-call(f32[8,128]{1,0:T(8,128)S(1)} %get-tuple-element.40.refs_0_, f32[8,128]{1,0:T(8,128)S(1)} %collective-permute-done.14.refs_1_, f32[8,128]{1,0:T(8,128)S(1)} %collective-permute-done.15.refs_2_, f32[8,128]{1,0:T(8,128)S(1)} %collective-permute-done.16.refs_3_, s32[8,128]{1,0:T(8,128)S(1)} %bitcast.17, ...), custom_call_target="tpu_custom_call" | custom-call | flops 1000 | bytes 1000 | tf_op jit(solution)/shard_map/pallas_call | solution.py:423
  45.3 0.0 collective-permute-done.8.refs_0_
  45.3 2.0 %collective-permute-done.10.refs_2_ = bf16[8,4096]{1,0:T(8,128)(2,1)S(1)} collective-permute-done((bf16[8,4096]{1,0:T(8,128)(2,1)S(1)}, bf16[8,4096]{1,0:T(8,128)(2,1)S(1)}, u32[]{:S(2)}, u32[]{:S(2)}) %collective-permute-start.10) | collective-permute-done | bytes 65568 | tf_op jit(solution)/shard_map/ppermute | solution.py:374
  47.3 2.0 %collective-permute-done.11.refs_3_ = bf16[8,4096]{1,0:T(8,128)(2,1)S(1)} collective-permute-done((bf16[8,4096]{1,0:T(8,128)(2,1)S(1)}, bf16[8,4096]{1,0:T(8,128)(2,1)S(1)}, u32[]{:S(2)}, u32[]{:S(2)}) %collective-permute-start.11) | collective-permute-done | bytes 65568 | tf_op jit(solution)/shard_map/ppermute | solution.py:374
  49.3 1.7 %shard_map.106 = bf16[128,4096]{1,0:T(8,128)(2,1)} custom-call(bf16[8,4096]{1,0:T(8,128)(2,1)S(1)} %collective-permute-done.8.refs_0_, bf16[8,4096]{1,0:T(8,128)(2,1)S(1)} %collective-permute-done.9.refs_1_, bf16[8,4096]{1,0:T(8,128)(2,1)S(1)} %collective-permute-done.10.refs_2_, bf16[8,4096]{1,0:T(8,128)(2,1)S(1)} %collective-permute-done.11.refs_3_, ...), custom_call_target="tpu_custom_call" | custom-call | flops 16777216 | bytes 2097152 | tf_op jit(solution)/shard_map/pallas_call | solution.py:424
  (11 shorter events, 0.0 us)
Async XLA Ops:
  0.6 48.7 %collective-permute-start.13 = (bf16[128,4096]{1,0:T(8,128)(2,1)}, bf16[128,4096]{1,0:T(8,128)(2,1)S(1)}, u32[]{:S(2)}, u32[]{:S(2)}) collective-permute-start(bf16[128,4096]{1,0:T(8,128)(2,1)} %bitcast.22), channel_id=1, source_target_pairs={{8,0},{9,1},{10,2},{11,3},{12,4},{13,5},{14,6},{15,7},{16,8},{17,9... | collective-permute-start | bytes 3145736 | tf_op jit(solution)/shard_map/ppermute | solution.py:374
  6.6 6.7 %collective-permute-start = (bf16[16,4224]{1,0:T(8,128)(2,1)S(1)}, bf16[16,4224]{1,0:T(8,128)(2,1)S(1)}, u32[]{:S(2)}, u32[]{:S(2)}) collective-permute-start(bf16[16,4224]{1,0:T(8,128)(2,1)S(1)} %get-tuple-element.24.refs_0_), channel_id=1, source_target_pairs={{0,2},{1,3},{2,0},{3,1},{4,6},{5,7},{6,4},{7,5},{8,10},{9,11},{10,... | collective-permute-start | bytes 405512 | tf_op jit(solution)/shard_map/ppermute | solution.py:363
  8.3 13.0 %collective-permute-start.1 = (bf16[16,4224]{1,0:T(8,128)(2,1)S(1)}, bf16[16,4224]{1,0:T(8,128)(2,1)S(1)}, u32[]{:S(2)}, u32[]{:S(2)}) collective-permute-start(bf16[16,4224]{1,0:T(8,128)(2,1)S(1)} %get-tuple-element.24.refs_0_), channel_id=1, source_target_pairs={{0,4},{1,5},{2,6},{3,7},{4,0},{5,1},{6,2},{7,3},{8,12},{9,13},{10,... | collective-permute-start | bytes 405512 | tf_op jit(solution)/shard_map/ppermute | solution.py:363
  10.9 10.4 %collective-permute-start.2 = (bf16[16,4224]{1,0:T(8,128)(2,1)S(1)}, bf16[16,4224]{1,0:T(8,128)(2,1)S(1)}, u32[]{:S(2)}, u32[]{:S(2)}) collective-permute-start(bf16[16,4224]{1,0:T(8,128)(2,1)S(1)} %get-tuple-element.24.refs_0_), channel_id=1, source_target_pairs={{0,6},{1,7},{2,4},{3,5},{4,2},{5,3},{6,0},{7,1},{8,14},{9,15},{10,... | collective-permute-start | bytes 405512 | tf_op jit(solution)/shard_map/ppermute | solution.py:363
  11.1 13.0 %collective-permute-start.3 = (bf16[16,4224]{1,0:T(8,128)(2,1)S(1)}, bf16[16,4224]{1,0:T(8,128)(2,1)S(1)}, u32[]{:S(2)}, u32[]{:S(2)}) collective-permute-start(bf16[16,4224]{1,0:T(8,128)(2,1)S(1)} %get-tuple-element.24.refs_0_), channel_id=1, source_target_pairs={{0,1},{1,0},{2,3},{3,2},{4,5},{5,4},{6,7},{7,6},{8,9},{9,8},{10,11... | collective-permute-start | bytes 405512 | tf_op jit(solution)/shard_map/ppermute | solution.py:366
  13.3 10.8 %collective-permute-start.4 = (bf16[16,4224]{1,0:T(8,128)(2,1)S(1)}, bf16[16,4224]{1,0:T(8,128)(2,1)S(1)}, u32[]{:S(2)}, u32[]{:S(2)}) collective-permute-start(bf16[16,4224]{1,0:T(8,128)(2,1)S(1)} %collective-permute-done.refs_1_), channel_id=1, source_target_pairs={{0,1},{1,0},{2,3},{3,2},{4,5},{5,4},{6,7},{7,6},{8,9},{9,8},{10,11... | collective-permute-start | bytes 405512 | tf_op jit(solution)/shard_map/ppermute | solution.py:366
  21.2 2.9 %collective-permute-start.5 = (bf16[16,4224]{1,0:T(8,128)(2,1)S(1)}, bf16[16,4224]{1,0:T(8,128)(2,1)S(1)}, u32[]{:S(2)}, u32[]{:S(2)}) collective-permute-start(bf16[16,4224]{1,0:T(8,128)(2,1)S(1)} %collective-permute-done.1.refs_2_), channel_id=1, source_target_pairs={{0,1},{1,0},{2,3},{3,2},{4,5},{5,4},{6,7},{7,6},{8,9},{9,8},{10,11... | collective-permute-start | bytes 405512 | tf_op jit(solution)/shard_map/ppermute | solution.py:366
  21.2 2.9 %collective-permute-start.6 = (bf16[16,4224]{1,0:T(8,128)(2,1)S(1)}, bf16[16,4224]{1,0:T(8,128)(2,1)S(1)}, u32[]{:S(2)}, u32[]{:S(2)}) collective-permute-start(bf16[16,4224]{1,0:T(8,128)(2,1)S(1)} %collective-permute-done.2.refs_3_), channel_id=1, source_target_pairs={{0,1},{1,0},{2,3},{3,2},{4,5},{5,4},{6,7},{7,6},{8,9},{9,8},{10,11... | collective-permute-start | bytes 405512 | tf_op jit(solution)/shard_map/ppermute | solution.py:366
  24.2 20.5 %copy-start = (s32[1,128,8]{1,2,0:T(8,128)S(1)}, s32[1,128,8]{1,2,0:T(8,128)}, u32[]{:S(2)}) copy-start(s32[1,128,8]{1,2,0:T(8,128)} %param.9) | copy-start | bytes 12292
  26.6 1.6 %collective-permute-start.7 = (bf16[32,4224]{1,0:T(8,128)(2,1)S(1)}, bf16[32,4224]{1,0:T(8,128)(2,1)S(1)}, u32[]{:S(2)}, u32[]{:S(2)}) collective-permute-start(bf16[32,4224]{1,0:T(8,128)(2,1)S(1)} %get-tuple-element.29), channel_id=1, source_target_pairs={{0,1},{1,0},{2,3},{3,2},{4,5},{5,4},{6,7},{7,6},{8,9},{9,8},{10,11... | collective-permute-start | bytes 811016 | tf_op jit(solution)/shard_map/ppermute | solution.py:366
  26.6 10.4 %collective-permute-start.12 = (bf16[16,4224]{1,0:T(8,128)(2,1)S(1)}, bf16[16,4224]{1,0:T(8,128)(2,1)S(1)}, u32[]{:S(2)}, u32[]{:S(2)}) collective-permute-start(bf16[16,4224]{1,0:T(8,128)(2,1)S(1)} %get-tuple-element.34), channel_id=1, source_target_pairs={{8,0},{9,1},{10,2},{11,3},{12,4},{13,5},{14,6},{15,7},{16,8},{17,9... | collective-permute-start | bytes 405512 | tf_op jit(solution)/shard_map/ppermute | solution.py:374
  32.6 4.9 %collective-permute-start.14 = (f32[8,128]{1,0:T(8,128)S(1)}, f32[8,128]{1,0:T(8,128)S(1)}, u32[]{:S(2)}, u32[]{:S(2)}) collective-permute-start(f32[8,128]{1,0:T(8,128)S(1)} %get-tuple-element.41), channel_id=1, source_target_pairs={{0,2},{1,3},{2,0},{3,1},{4,6},{5,7},{6,4},{7,5},{8,10},{9,11},{10,... | collective-permute-start | bytes 12296 | tf_op jit(solution)/shard_map/ppermute | solution.py:363
  34.3 4.9 %collective-permute-start.15 = (f32[8,128]{1,0:T(8,128)S(1)}, f32[8,128]{1,0:T(8,128)S(1)}, u32[]{:S(2)}, u32[]{:S(2)}) collective-permute-start(f32[8,128]{1,0:T(8,128)S(1)} %get-tuple-element.42), channel_id=1, source_target_pairs={{0,4},{1,5},{2,6},{3,7},{4,0},{5,1},{6,2},{7,3},{8,12},{9,13},{10,... | collective-permute-start | bytes 12296 | tf_op jit(solution)/shard_map/ppermute | solution.py:363
  35.6 6.7 %collective-permute-start.16 = (f32[8,128]{1,0:T(8,128)S(1)}, f32[8,128]{1,0:T(8,128)S(1)}, u32[]{:S(2)}, u32[]{:S(2)}) collective-permute-start(f32[8,128]{1,0:T(8,128)S(1)} %get-tuple-element.43), channel_id=1, source_target_pairs={{0,6},{1,7},{2,4},{3,5},{4,2},{5,3},{6,0},{7,1},{8,14},{9,15},{10,... | collective-permute-start | bytes 12296 | tf_op jit(solution)/shard_map/ppermute | solution.py:363
  37.0 8.3 %collective-permute-start.8 = (bf16[8,4096]{1,0:T(8,128)(2,1)S(1)}, bf16[8,4096]{1,0:T(8,128)(2,1)S(1)}, u32[]{:S(2)}, u32[]{:S(2)}) collective-permute-start(bf16[8,4096]{1,0:T(8,128)(2,1)S(1)} %get-tuple-element.30), channel_id=1, source_target_pairs={{8,0},{9,1},{10,2},{11,3},{12,4},{13,5},{14,6},{15,7},{16,8},{17,9... | collective-permute-start | bytes 196616 | tf_op jit(solution)/shard_map/ppermute | solution.py:374
  37.6 7.7 %collective-permute-start.9 = (bf16[8,4096]{1,0:T(8,128)(2,1)S(1)}, bf16[8,4096]{1,0:T(8,128)(2,1)S(1)}, u32[]{:S(2)}, u32[]{:S(2)}) collective-permute-start(bf16[8,4096]{1,0:T(8,128)(2,1)S(1)} %get-tuple-element.31), channel_id=1, source_target_pairs={{8,2},{9,3},{10,0},{11,1},{12,6},{13,7},{14,4},{15,5},{16,10},{17,... | collective-permute-start | bytes 196616 | tf_op jit(solution)/shard_map/ppermute | solution.py:374
  39.2 8.1 %collective-permute-start.10 = (bf16[8,4096]{1,0:T(8,128)(2,1)S(1)}, bf16[8,4096]{1,0:T(8,128)(2,1)S(1)}, u32[]{:S(2)}, u32[]{:S(2)}) collective-permute-start(bf16[8,4096]{1,0:T(8,128)(2,1)S(1)} %get-tuple-element.32), channel_id=1, source_target_pairs={{8,4},{9,5},{10,6},{11,7},{12,0},{13,1},{14,2},{15,3},{16,12},{17,... | collective-permute-start | bytes 196616 | tf_op jit(solution)/shard_map/ppermute | solution.py:374
  42.3 7.0 %collective-permute-start.11 = (bf16[8,4096]{1,0:T(8,128)(2,1)S(1)}, bf16[8,4096]{1,0:T(8,128)(2,1)S(1)}, u32[]{:S(2)}, u32[]{:S(2)}) collective-permute-start(bf16[8,4096]{1,0:T(8,128)(2,1)S(1)} %get-tuple-element.33), channel_id=1, source_target_pairs={{8,6},{9,7},{10,4},{11,5},{12,2},{13,3},{14,0},{15,1},{16,14},{17,... | collective-permute-start | bytes 196616 | tf_op jit(solution)/shard_map/ppermute | solution.py:374

commit v3 on v2

--- a/solution.py
+++ b/solution.py
@@ -164,8 +164,10 @@
     return rows / rms, rms
 
 
-def rows_kernel(ids_hbm, weight_hbm, gain_hbm, hidden_hbm, grad_hbm, rows_ref, side_ref, place_ref,
-                ids_ref, weight_ref, gain_ref, hidden_ref, grad_ref, sems):
+def rows_kernel(ids_hbm, weight_hbm, gain_hbm, hidden_hbm, grad_hbm, rows_ref, hand_ref, place_ref,
+                ids_ref, weight_ref, gain_ref, hidden_ref, sems):
+    tokens, width = hidden_ref.shape
+    cap = SPECIALIST_CAP
     copies = [
         pltpu.make_async_copy(src, dst, sems.at[i])
         for i, (src, dst) in enumerate([
@@ -173,14 +175,11 @@
             (hidden_hbm, hidden_ref),
             (gain_hbm, gain_ref),
             (weight_hbm, weight_ref),
-            (grad_hbm, grad_ref),
+            (grad_hbm, hand_ref.at[:tokens, :width]),
         ])
     ]
     for copy in copies:
         copy.start()
-    width = hidden_ref.shape[1]
-    tokens = ids_ref.shape[1]
-    cap = SPECIALIST_CAP
     copies[0].wait()
     hit = ids_ref[...] == 0
     member = jnp.max(hit.astype(F32), axis=0, keepdims=True)
@@ -202,8 +201,9 @@
     middle = (gain - high).astype(BF16).astype(F32)
     low = gain - high - middle
     blank = jnp.zeros((cap - 3, width), F32)
-    side_ref[:, :width] = jnp.concatenate([raw, high, middle, low, blank], axis=0).astype(BF16)
-    side_ref[:, width:] = jnp.concatenate([place, jnp.zeros((cap, tokens), F32)], axis=0).astype(BF16)
+    hand_ref[tokens:, :width] = jnp.concatenate([raw, high, middle, low, blank], axis=0).astype(BF16)
+    hand_ref[tokens:, width:] = jnp.concatenate([place, jnp.zeros_like(place)], axis=0).astype(BF16)
+    hand_ref[:tokens, width:] = jnp.zeros((tokens, LANES), BF16)
     copies[3].wait()
     weight = jnp.sum(
         jnp.where(hit, weight_ref[...].astype(F32), 0.0), axis=0, keepdims=True
@@ -212,16 +212,16 @@
     taken = jnp.broadcast_to(taken, (cap, LANES))
     rows_ref[:, width:] = jnp.concatenate([taken, taken], axis=0).astype(BF16)
     copies[4].wait()
-    grad = take_rows(place.astype(BF16), grad_ref[...])
+    grad = take_rows(place.astype(BF16), hand_ref[:tokens, :width])
     rows_ref[:, :width] = jnp.concatenate([normed_in, grad], axis=0).astype(BF16)
 
 
-def fetch_kernel(slab_hbm, down_hbm, after_ref, slab_ref, down_ref, sems):
-    del after_ref
+def fetch_kernel(slab_hbm, down_hbm, rows_ref, slab_ref, down_ref, again_ref, sems):
     first = pltpu.make_async_copy(slab_hbm, slab_ref, sems.at[0])
     second = pltpu.make_async_copy(down_hbm, down_ref, sems.at[1])
     first.start()
     second.start()
+    again_ref[...] = rows_ref[...]
     first.wait()
     second.wait()
 
@@ -244,11 +244,12 @@
 
 
 def hidden_kernel(*refs):
-    *blocks, slab_ref, down_ref, keep_ref, send_ref, both_ref, act_ref = refs
+    *blocks, slab_ref, down_ref, keep_ref, send_ref, rows_ref, both_ref, act_ref = refs
     hidden, width = down_ref.shape
     half = keep_ref.shape[0]
     cap = SPECIALIST_CAP
     rows = jnp.concatenate([r[:, :width] for r in blocks], axis=0)
+    rows_ref[...] = rows
     pre, _ = halves(rows_product(rows, slab_ref[...]), cap)
     _, back = halves(rows_product(rows, down_ref[...]), cap)
     weight = jnp.concatenate([r[:, width:].astype(F32)[:cap, :1] for r in blocks], axis=0)
@@ -272,61 +273,77 @@
     act_ref[...] = padded(weight * act, 1, cap).T.astype(BF16)
 
 
-def join_kernel(keep_ref, got_ref, *refs):
-    *out_refs, comb_ref = refs
-    rows, width = out_refs[0].shape
+def halve_kernel(keep_ref, got_ref, own_ref, other_ref):
     total = keep_ref[...].astype(F32) + got_ref[...].astype(F32)
-    for k, out_ref in enumerate(out_refs):
-        out_ref[...] = total[k * rows : (k + 1) * rows, :width].astype(BF16)
-    comb_ref[...] = total[:, width:]
-
-
-def weights_kernel(chips, *refs):
-    blocks, refs = refs[: 2 * chips], refs[2 * chips :]
-    both_ref, act_ref, comb_ref, both_out, act_out, *comb_refs = refs
-    rows = jnp.concatenate([r[...] for r in blocks], axis=0)
+    half = own_ref.shape[0]
+    width = own_ref.shape[1] - LANES
+    other_ref[:, :width] = total[half:, :width].astype(BF16)
+    own_ref[:, :width] = total[:half, :width].astype(BF16)
+    comb = total[:, width:]
+    high = comb.astype(BF16).astype(F32)
+    lane = lax.broadcasted_iota(jnp.int32, comb.shape, 1)
+    comb = jnp.where(lane < LANES // 2, high, comb - high).astype(BF16)
+    other_ref[:, width:] = comb[half:]
+    own_ref[:, width:] = comb[:half]
+
+
+def split_kernel(keep_ref, got_ref, own_ref, other_ref, own_comb_ref, other_comb_ref):
+    total = keep_ref[...].astype(F32) + got_ref[...].astype(F32)
+    half, width = own_ref.shape
+    other_ref[...] = total[half:, :width].astype(BF16)
+    own_ref[...] = total[:half, :width].astype(BF16)
+    comb = total[:, width:]
+    comb = comb + pltpu.roll(comb, LANES // 2, 1)
+    other_comb_ref[...] = comb[half:]
+    own_comb_ref[...] = comb[:half]
+
+
+def weights_kernel(rows_ref, both_ref, act_ref, after_ref, both_out, act_out):
+    del after_ref
+    chunk = both_out.shape[1]
+    rows = rows_ref[:, pl.ds(pl.multiple_of(pl.program_id(0) * chunk, chunk), chunk)]
     both_out[...] = take_rows(both_ref[...], rows).astype(BF16)
     act_out[...] = take_rows(act_ref[...], rows).astype(BF16)
-    cap = comb_refs[0].shape[0]
-    for k, out_ref in enumerate(comb_refs):
-        out_ref[...] = comb_ref[k * cap : (k + 1) * cap]
-
-
-def weight_grads(blocks, both, act, comb, chips, width):
+
+
+def weight_grads(rows, both, act, after):
+    width = rows.shape[1]
+    hidden = act.shape[0]
     chunk = min(width, 1024)
-    across = lambda rows: pl.BlockSpec((rows, chunk), lambda i: (0, i))
-    whole = lambda shape: pl.BlockSpec(shape, lambda i: (0, 0))
-    comb_shape = (comb.shape[0] // chips, comb.shape[1])
-    hidden = act.shape[0]
+    across = lambda count: pl.BlockSpec((count, chunk), lambda i: (0, i))
     return pl.pallas_call(
-        functools.partial(weights_kernel, chips),
+        weights_kernel,
         grid=(width // chunk,),
-        in_specs=[across(b.shape[0]) for b in blocks]
-        + [whole(both.shape), whole(act.shape), whole(comb.shape)],
-        out_specs=[across(2 * hidden), across(hidden)] + [whole(comb_shape)] * chips,
+        in_specs=[IN_VMEM, IN_VMEM, IN_VMEM, pl.BlockSpec(memory_space=pl.ANY)],
+        out_specs=[across(2 * hidden), across(hidden)],
         out_shape=[
             jax.ShapeDtypeStruct((2 * hidden, width), BF16),
             jax.ShapeDtypeStruct((hidden, width), BF16),
-        ]
-        + [jax.ShapeDtypeStruct(comb_shape, F32)] * chips,
+        ],
         compiler_params=pltpu.CompilerParams(vmem_limit_bytes=24 << 20),
         cost_estimate=pl.CostEstimate(
-            flops=6 * 128 * hidden * width, bytes_accessed=6 * hidden * width, transcendentals=0
-        ),
-    )(*blocks, both, act, comb)
-
-
-def finish_kernel(*refs):
-    *parts, side_ref, grad_ref, out_ref = refs
+            flops=6 * rows.shape[0] * hidden * width,
+            bytes_accessed=6 * hidden * width,
+            transcendentals=0,
+        ),
+    )(rows, both, act, after)
+
+
+def finish_kernel(own_ref, other_ref, hand_ref, own_comb_ref, other_comb_ref, ids_ref, place_ref,
+                  out_ref, comb_ref):
     cap = SPECIALIST_CAP
-    width = grad_ref.shape[1]
-    side = side_ref[...].astype(F32)
+    tokens, width = out_ref.shape
+    comb = own_comb_ref[...] + other_comb_ref[...]
+    comb = jnp.sum(place_ref[...] * comb, axis=0, keepdims=True)
+    comb_ref[...] = jnp.where(ids_ref[...] == 0, comb, 0.0)
+    side = hand_ref[tokens:, :].astype(F32)
     place = side[:cap, width:]
-    gain = side[cap : cap + 1, :width] + side[cap + 1 : cap + 2, :width] + side[cap + 2 : cap + 3, :width]
+    gain = side[cap : cap + 1, :width] + side[cap + 1 : cap + 2, :width]
+    gain = gain + side[cap + 2 : cap + 3, :width]
     normed, rms = normed_rows(side[:cap, :width])
-    grad = grad_ref[...]
+    grad = hand_ref[:tokens, :width]
     own = take_rows(place.astype(BF16), grad)
-    total = sum(p[...].astype(F32) for p in parts)
+    total = own_ref[...].astype(F32) + other_ref[...].astype(F32)
     scaled = total * gain
     inner = jnp.mean(scaled * normed, axis=-1, keepdims=True)
     rows = (own + (scaled - normed * inner) / rms).astype(BF16)
@@ -336,17 +353,9 @@
     out_ref[...] = jnp.where(named, spread, grad.astype(F32)).astype(BF16)
 
 
-def combine_kernel(*refs):
-    *parts, ids_ref, place_ref, out_ref = refs
-    total = sum(p[...] for p in parts)
-    spread = jnp.sum(place_ref[...] * total, axis=0, keepdims=True)
-    out_ref[...] = jnp.where(ids_ref[...] == 0, spread, 0.0)
-
-
 def on_one(hidden_in, out_grad, expert_ids, route_weight, norm_gain, w_gate_up, w_down):
     sections = lax.axis_size("pipe")
     devices = lax.axis_size("expert")
-    chips = devices // 2
     tokens, width = hidden_in.shape[1:]
     hidden = w_down.shape[2]
     cap = SPECIALIST_CAP
@@ -354,7 +363,6 @@
     weights = route_weight[0].T
     slab = w_gate_up.reshape(2 * hidden, width)
     down = w_down.reshape(hidden, width)
-    grad = out_grad[0]
     in_hbm = lambda a: pltpu.with_memory_space_constraint(a, pltpu.HBM)
     wide = width + LANES
     total_rows = devices * cap
@@ -373,9 +381,9 @@
         ]
         return lax.ppermute(block, ("pipe", "expert"), route)
 
-    rows, side, place = call(
+    rows, hand, place = call(
         rows_kernel,
-        [((2 * cap, wide), BF16), ((2 * cap, wide), BF16), ((cap, tokens), F32)],
+        [((2 * cap, wide), BF16), ((tokens + 2 * cap, wide), BF16), ((cap, tokens), F32)],
         4 * tokens * width * cap,
         4 * tokens * width,
         in_specs=[IN_HBM] * 5,
@@ -384,46 +392,51 @@
             pltpu.VMEM(weights.shape, weights.dtype),
             pltpu.VMEM(norm_gain.shape, norm_gain.dtype),
             pltpu.VMEM((tokens, width), BF16),
-            pltpu.VMEM((tokens, width), BF16),
             pltpu.SemaphoreType.DMA((5,)),
         ],
-    )(*map(in_hbm, (ids, weights, norm_gain, hidden_in[0], grad)))
-    lane = [rows] + [across(rows, k) for k in range(1, chips)]
-    next_side = handed(side, 0)
-    next_grad = handed(grad, 0)
-    slab_near, down_near = call(
+    )(*map(in_hbm, (ids, weights, norm_gain, hidden_in[0], out_grad[0])))
+    far = across(rows, 2)
+    near = across(rows, 1)
+    farthest = across(far, 1)
+    handed_block = handed(hand, 0)
+    slab_near, down_near, rows_again = call(
         fetch_kernel,
-        [(slab.shape, BF16), (down.shape, BF16)],
+        [(slab.shape, BF16), (down.shape, BF16), (rows.shape, BF16)],
         0,
         6 * hidden * width,
-        in_specs=[IN_HBM, IN_HBM, pl.BlockSpec(memory_space=pl.ANY)],
+        in_specs=[IN_HBM, IN_HBM, IN_VMEM],
         scratch=[pltpu.SemaphoreType.DMA((2,))],
-    )(in_hbm(slab), in_hbm(down), place)
-    blocks = lane + [beside(b) for b in lane]
-    keep, send, both, act = call(
+    )(in_hbm(slab), in_hbm(down), rows)
+    lane = [rows, far, near, farthest]
+    blocks = lane + [beside(b) for b in (rows_again, far, near, farthest)]
+    keep, send, all_rows, both, act = call(
         hidden_kernel,
         [
             ((total_rows // 2, wide), BF16),
             ((total_rows // 2, wide), BF16),
+            ((2 * total_rows, width), BF16),
             ((2 * hidden, 2 * total_rows), BF16),
             ((hidden, 2 * total_rows), BF16),
         ],
         10 * total_rows * hidden * width,
         6 * hidden * width,
     )(*blocks, slab_near, down_near)
-    *parts, comb = call(
-        join_kernel,
-        [((cap, width), BF16)] * chips + [((total_rows // 2, LANES), F32)],
-        total_rows * width,
-        4 * total_rows * width,
+    own_half, other_half = call(
+        halve_kernel, [((2 * cap, wide), BF16)] * 2, 4 * cap * width, 16 * cap * width
     )(keep, beside(send))
-    got = [handed(parts[k], k) for k in range(chips)]
-    gate_up_out, down_out, *comb_parts = weight_grads(blocks, both, act, comb, chips, width)
-    comb_got = [comb_parts[0]] + [across(comb_parts[k], k) for k in range(1, chips)]
-    (combined,) = call(combine_kernel, [((SPLIT, tokens), F32)], 1000, 1000)(*comb_got, ids, place)
-    (out,) = call(finish_kernel, [((tokens, width), BF16)], 4 * tokens * width * cap, 4 * tokens * width)(
-        *got, next_side, next_grad
-    )
+    own, other, own_comb, other_comb = call(
+        split_kernel,
+        [((cap, width), BF16)] * 2 + [((cap, LANES), F32)] * 2,
+        2 * cap * width,
+        8 * cap * width,
+    )(own_half, across(other_half, 1))
+    gate_up_out, down_out = weight_grads(all_rows, both, act, own_comb)
+    out, combined = call(
+        finish_kernel,
+        [((tokens, width), BF16), ((SPLIT, tokens), F32)],
+        4 * tokens * width * cap,
+        4 * tokens * width,
+    )(handed(own, 0), handed(other, 2), handed_block, own_comb, across(other_comb, 2), ids, place)
     return (
         out[None],
         gate_up_out.reshape(1, 1, 2, hidden, width),

time: 51.1 us -> 42.3 us (0.83)
  starting transfers between devices: 21.6 us -> 15 us
  Pallas kernels: 13.5 us -> 11.8 us
    ppermute x6 -> x3, starting transfers between devices: 12.2 us -> 8.08 us  [handed(): return lax.ppermute(block, ('pipe', 'expert'), route)]
    ppermute x6 -> x3, waiting for transfers between devices: 4.01 us -> 0.01 us  [handed(): return lax.ppermute(block, ('pipe', 'expert'), route)]
    ppermute x6 -> x5, starting transfers between devices: 8.84 us -> 6.08 us  [across(): lax.ppermute(block, 'expert', [(i, i ^ 2 * offset) for i in range(devices)])]
    ppermute x5, waiting for transfers between devices: 0.96 us -> 2.74 us  [beside(): return lax.ppermute(block, 'expert', [(i, i ^ 1) for i in range(devices)])]
    pallas_call x6, Pallas kernels: 11.1 us -> 9.42 us  [the longest x1 3.17 us: weight_grads(): pl.pallas_call(weights_kernel, grid=(width // chunk,), in_specs=[IN_VMEM,...]
    ppermute x6 -> x5, waiting for transfers between devices: 10.1 us -> 11.9 us  [across(): lax.ppermute(block, 'expert', [(i, i ^ 2 * offset) for i in range(devices)])]
  transfers between devices with their start and end apart: 17 -> 13, of which waited for: 5 -> 6; matrix products, arithmetic and copies ran while one was open for 0% -> 0% of each run, Pallas kernels for 23% -> 19%
where the time goes in v3:
time: 42.3 us; the launch traced here: 42.1 us
  starting transfers between devices  15 us (35%)
  waiting for transfers between devices  14.6 us (35%)
  Pallas kernels  11.8 us (28%)
  between operations  0.71 us (2%)
    ppermute x5, waiting for transfers between devices, across(): lax.ppermute(block, 'expert', [(i, i ^ 2 * offset) for i in range(devices)])  11.9 us
    ppermute x3, starting transfers between devices, handed(): return lax.ppermute(block, ('pipe', 'expert'), route)  8.08 us
    ppermute x5, starting transfers between devices, across(): lax.ppermute(block, 'expert', [(i, i ^ 2 * offset) for i in range(devices)])  6.08 us
    pallas_call x1, Pallas kernels, weight_grads(): pl.pallas_call(weights_kernel, grid=(width // chunk,), in_specs=[IN_VMEM,...  3.17 us
    ppermute x5, waiting for transfers between devices, beside(): return lax.ppermute(block, 'expert', [(i, i ^ 1) for i in range(devices)])  2.74 us
    pallas_call x1, Pallas kernels, on_one(): call(hidden_kernel, [((total_rows // 2, wide), BF16), ((total_rows // 2,...  2.37 us
    pallas_call x1, Pallas kernels, on_one(): call(fetch_kernel, [(slab.shape, BF16), (down.shape, BF16), (rows.shape,...  2.37 us
    pallas_call x1, Pallas kernels, on_one(): call(rows_kernel, [((2 * cap, wide), BF16), ((tokens + 2 * cap, wide), BF...  2.07 us
  transfers between devices with their start and end apart: 13, of which 6 were waited for; matrix products, arithmetic and copies ran while one was open for 0% of the time, Pallas kernels for 19%

profile of v3, /device:TPU:0, one launch (start us, length us, event | category | flops | bytes accessed | tf_op | source)
XLA Modules:
  0.0 42.1 jit_solution(10348151302336152819)
XLA Ops:
  0.6 2.1 %shard_map.102 = (bf16[16,4224]{1,0:T(8,128)(2,1)S(1)}, bf16[144,4224]{1,0:T(8,128)(2,1)S(1)}, f32[8,128]{1,0:T(8,128)S(1)}) custom-call(s32[8,128]{1,0:T(8,128)} %bitcast.16, bf16[8,128]{1,0:T(8,128)(2,1)} %bitcast.22, f32[1,4096]{1,0:T(1,128)} %gain_hbm.1, bf16[128,4096]{1,0:T(8,128)(2,1)} %bitcast.20, bf16[128,4096]{1,0:T(8,128)(2,1)} %bitcast.21), custom_call_target="tpu_custom_call" | custom-call | flops 16777216 | bytes 2097152 | tf_op jit(solution)/shard_map/pallas_call | solution.py:384
  2.7 3.9 %collective-permute-start.11 = (bf16[144,4224]{1,0:T(8,128)(2,1)S(1)}, bf16[144,4224]{1,0:T(8,128)(2,1)S(1)}, u32[]{:S(2)}, u32[]{:S(2)}) collective-permute-start(bf16[144,4224]{1,0:T(8,128)(2,1)S(1)} %get-tuple-element.35), channel_id=1, source_target_pairs={{8,0},{9,1},{10,2},{11,3},{12,4},{13,5},{14,6},{15,7},{16,8},{17,9... | collective-permute-start | bytes 3649544 | tf_op jit(solution)/shard_map/ppermute | solution.py:382
  6.7 2.6 %collective-permute-start = (bf16[16,4224]{1,0:T(8,128)(2,1)S(1)}, bf16[16,4224]{1,0:T(8,128)(2,1)S(1)}, u32[]{:S(2)}, u32[]{:S(2)}) collective-permute-start(bf16[16,4224]{1,0:T(8,128)(2,1)S(1)} %get-tuple-element.25.rows_ref.refs_0_), channel_id=1, source_target_pairs={{0,4},{1,5},{2,6},{3,7},{4,0},{5,1},{6,2},{7,3},{8,12},{9,13},{10,... | collective-permute-start | bytes 405512 | tf_op jit(solution)/shard_map/ppermute | solution.py:371
  9.2 1.6 %collective-permute-start.1 = (bf16[16,4224]{1,0:T(8,128)(2,1)S(1)}, bf16[16,4224]{1,0:T(8,128)(2,1)S(1)}, u32[]{:S(2)}, u32[]{:S(2)}) collective-permute-start(bf16[16,4224]{1,0:T(8,128)(2,1)S(1)} %get-tuple-element.25.rows_ref.refs_0_), channel_id=1, source_target_pairs={{0,2},{1,3},{2,0},{3,1},{4,6},{5,7},{6,4},{7,5},{8,10},{9,11},{10,... | collective-permute-start | bytes 405512 | tf_op jit(solution)/shard_map/ppermute | solution.py:371
  10.8 4.8 %collective-permute-done.refs_1_ = bf16[16,4224]{1,0:T(8,128)(2,1)S(1)} collective-permute-done((bf16[16,4224]{1,0:T(8,128)(2,1)S(1)}, bf16[16,4224]{1,0:T(8,128)(2,1)S(1)}, u32[]{:S(2)}, u32[]{:S(2)}) %collective-permute-start) | collective-permute-done | bytes 135200 | tf_op jit(solution)/shard_map/ppermute | solution.py:371
  15.6 0.6 %collective-permute-start.2 = (bf16[16,4224]{1,0:T(8,128)(2,1)S(1)}, bf16[16,4224]{1,0:T(8,128)(2,1)S(1)}, u32[]{:S(2)}, u32[]{:S(2)}) collective-permute-start(bf16[16,4224]{1,0:T(8,128)(2,1)S(1)} %collective-permute-done.refs_1_), channel_id=1, source_target_pairs={{0,2},{1,3},{2,0},{3,1},{4,6},{5,7},{6,4},{7,5},{8,10},{9,11},{10,... | collective-permute-start | bytes 405512 | tf_op jit(solution)/shard_map/ppermute | solution.py:371
  16.2 2.4 %shard_map.103 = (bf16[384,4096]{1,0:T(8,128)(2,1)S(1)}, bf16[192,4096]{1,0:T(8,128)(2,1)S(1)}, bf16[16,4224]{1,0:T(8,128)(2,1)S(1)}) custom-call(bf16[384,4096]{1,0:T(8,128)(2,1)} %bitcast.18, bf16[192,4096]{1,0:T(8,128)(2,1)} %bitcast.19, bf16[16,4224]{1,0:T(8,128)(2,1)S(1)} %get-tuple-element.25.rows_ref.refs_0_), custom_call_target="tpu_custom_call" | custom-call | bytes 4718592 | tf_op jit(solution)/shard_map/pallas_call | solution.py:402
  18.5 0.1 collective-permute-start.3
  18.6 0.5 %collective-permute-start.4 = (bf16[16,4224]{1,0:T(8,128)(2,1)S(1)}, bf16[16,4224]{1,0:T(8,128)(2,1)S(1)}, u32[]{:S(2)}, u32[]{:S(2)}) collective-permute-start(bf16[16,4224]{1,0:T(8,128)(2,1)S(1)} %collective-permute-done.refs_1_), channel_id=1, source_target_pairs={{0,1},{1,0},{2,3},{3,2},{4,5},{5,4},{6,7},{7,6},{8,9},{9,8},{10,11... | collective-permute-start | bytes 405512 | tf_op jit(solution)/shard_map/ppermute | solution.py:374
  19.1 0.0 collective-permute-done.1.refs_2_
  19.1 0.1 collective-permute-start.5
  19.2 1.4 %collective-permute-done.2.refs_3_ = bf16[16,4224]{1,0:T(8,128)(2,1)S(1)} collective-permute-done((bf16[16,4224]{1,0:T(8,128)(2,1)S(1)}, bf16[16,4224]{1,0:T(8,128)(2,1)S(1)}, u32[]{:S(2)}, u32[]{:S(2)}) %collective-permute-start.2) | collective-permute-done | bytes 135200 | tf_op jit(solution)/shard_map/ppermute | solution.py:371
  20.6 0.0 collective-permute-start.6
  20.6 0.0 collective-permute-done.3.refs_4_
  20.6 0.0 collective-permute-done.5.refs_6_
  20.6 0.0 collective-permute-done.4.refs_5_
  20.6 1.3 %collective-permute-done.6.refs_7_ = bf16[16,4224]{1,0:T(8,128)(2,1)S(1)} collective-permute-done((bf16[16,4224]{1,0:T(8,128)(2,1)S(1)}, bf16[16,4224]{1,0:T(8,128)(2,1)S(1)}, u32[]{:S(2)}, u32[]{:S(2)}) %collective-permute-start.6) | collective-permute-done | bytes 135200 | tf_op jit(solution)/shard_map/ppermute | solution.py:374
  22.0 2.4 %shard_map.104 = (bf16[32,4224]{1,0:T(8,128)(2,1)S(1)}, bf16[32,4224]{1,0:T(8,128)(2,1)S(1)}, bf16[128,4096]{1,0:T(8,128)(2,1)S(1)}, bf16[384,128]{1,0:T(8,128)(2,1)S(1)}, bf16[192,128]{1,0:T(8,128)(2,1)S(1)}) custom-call(bf16[16,4224]{1,0:T(8,128)(2,1)S(1)} %get-tuple-element.25.rows_ref.refs_0_, bf16[16,4224]{1,0:T(8,128)(2,1)S(1)} %collective-permute-done.refs_1_, ...), custom_call_target="tpu_custom_call" | custom-call | flops 503316480 | bytes 4718592 | tf_op jit(solution)/shard_map/pallas_call | solution.py:412
  24.3 0.0 copy-start
  24.4 0.2 collective-permute-start.7
  24.6 1.4 %collective-permute-done.7.got_ref = bf16[32,4224]{1,0:T(8,128)(2,1)S(1)} collective-permute-done((bf16[32,4224]{1,0:T(8,128)(2,1)S(1)}, bf16[32,4224]{1,0:T(8,128)(2,1)S(1)}, u32[]{:S(2)}, u32[]{:S(2)}) %collective-permute-start.7) | collective-permute-done | bytes 270368 | tf_op jit(solution)/shard_map/ppermute | solution.py:374
  26.0 0.1 shard_map.105
  26.0 1.1 %collective-permute-start.8 = (bf16[16,4224]{1,0:T(8,128)(2,1)S(1)}, bf16[16,4224]{1,0:T(8,128)(2,1)S(1)}, u32[]{:S(2)}, u32[]{:S(2)}) collective-permute-start(bf16[16,4224]{1,0:T(8,128)(2,1)S(1)} %get-tuple-element.32), channel_id=1, source_target_pairs={{0,2},{1,3},{2,0},{3,1},{4,6},{5,7},{6,4},{7,5},{8,10},{9,11},{10,... | collective-permute-start | bytes 405512 | tf_op jit(solution)/shard_map/ppermute | solution.py:371
  27.2 4.6 %collective-permute-done.8.got_ref = bf16[16,4224]{1,0:T(8,128)(2,1)S(1)} collective-permute-done((bf16[16,4224]{1,0:T(8,128)(2,1)S(1)}, bf16[16,4224]{1,0:T(8,128)(2,1)S(1)}, u32[]{:S(2)}, u32[]{:S(2)}) %collective-permute-start.8) | collective-permute-done | bytes 135200 | tf_op jit(solution)/shard_map/ppermute | solution.py:371
  31.7 0.1 shard_map.106
  31.8 0.6 %collective-permute-start.9 = (bf16[8,4096]{1,0:T(8,128)(2,1)S(1)}, bf16[8,4096]{1,0:T(8,128)(2,1)S(1)}, u32[]{:S(2)}, u32[]{:S(2)}) collective-permute-start(bf16[8,4096]{1,0:T(8,128)(2,1)S(1)} %get-tuple-element.33), channel_id=1, source_target_pairs={{8,0},{9,1},{10,2},{11,3},{12,4},{13,5},{14,6},{15,7},{16,8},{17,9... | collective-permute-start | bytes 196616 | tf_op jit(solution)/shard_map/ppermute | solution.py:382
  32.4 3.6 %collective-permute-start.10 = (bf16[8,4096]{1,0:T(8,128)(2,1)S(1)}, bf16[8,4096]{1,0:T(8,128)(2,1)S(1)}, u32[]{:S(2)}, u32[]{:S(2)}) collective-permute-start(bf16[8,4096]{1,0:T(8,128)(2,1)S(1)} %get-tuple-element.34), channel_id=1, source_target_pairs={{8,4},{9,5},{10,6},{11,7},{12,0},{13,1},{14,2},{15,3},{16,12},{17,... | collective-permute-start | bytes 196616 | tf_op jit(solution)/shard_map/ppermute | solution.py:382
  36.0 0.2 collective-permute-start.12
  36.2 3.2 %shard_map.108 = (bf16[384,4096]{1,0:T(8,128)(2,1)}, bf16[192,4096]{1,0:T(8,128)(2,1)}) custom-call(bf16[128,4096]{1,0:T(8,128)(2,1)S(1)} %get-tuple-element.40.rows_ref, bf16[384,128]{1,0:T(8,128)(2,1)S(1)} %get-tuple-element.41.both_ref, bf16[192,128]{1,0:T(8,128)(2,1)S(1)} %get-tuple-element.42.act_ref, f32[8,128]{1,0:T(8,128)S(1)} %get-tuple-element.36.own_comb_ref.after_ref), custom_call_target="tpu_custom_call" | custom-call | flops 603979776 | bytes 4718592 | tf_op jit(solution)/shard_map/pallas_call | solution.py:314
  39.4 1.1 %collective-permute-done.12.other_comb_ref = f32[8,128]{1,0:T(8,128)S(1)} collective-permute-done((f32[8,128]{1,0:T(8,128)S(1)}, f32[8,128]{1,0:T(8,128)S(1)}, u32[]{:S(2)}, u32[]{:S(2)}) %collective-permute-start.12) | collective-permute-done | bytes 4128 | tf_op jit(solution)/shard_map/ppermute | solution.py:371
  40.5 0.0 collective-permute-done.11.hand_ref
  40.5 1.7 %shard_map.107 = (bf16[128,4096]{1,0:T(8,128)(2,1)}, f32[8,128]{1,0:T(8,128)}) custom-call(bf16[8,4096]{1,0:T(8,128)(2,1)S(1)} %collective-permute-done.9.own_ref, bf16[8,4096]{1,0:T(8,128)(2,1)S(1)} %collective-permute-done.10.other_ref, bf16[144,4224]{1,0:T(8,128)(2,1)S(1)} %collective-permute-done.11.hand_ref, ...), custom_call_target="tpu_custom_call" | custom-call | flops 16777216 | bytes 2097152 | tf_op jit(solution)/shard_map/pallas_call | solution.py:434
  (3 shorter events, 0.0 us)
Async XLA Ops:
  2.7 37.8 %collective-permute-start.11 = (bf16[144,4224]{1,0:T(8,128)(2,1)S(1)}, bf16[144,4224]{1,0:T(8,128)(2,1)S(1)}, u32[]{:S(2)}, u32[]{:S(2)}) collective-permute-start(bf16[144,4224]{1,0:T(8,128)(2,1)S(1)} %get-tuple-element.35), channel_id=1, source_target_pairs={{8,0},{9,1},{10,2},{11,3},{12,4},{13,5},{14,6},{15,7},{16,8},{17,9... | collective-permute-start | bytes 3649544 | tf_op jit(solution)/shard_map/ppermute | solution.py:382
  6.7 8.9 %collective-permute-start = (bf16[16,4224]{1,0:T(8,128)(2,1)S(1)}, bf16[16,4224]{1,0:T(8,128)(2,1)S(1)}, u32[]{:S(2)}, u32[]{:S(2)}) collective-permute-start(bf16[16,4224]{1,0:T(8,128)(2,1)S(1)} %get-tuple-element.25.rows_ref.refs_0_), channel_id=1, source_target_pairs={{0,4},{1,5},{2,6},{3,7},{4,0},{5,1},{6,2},{7,3},{8,12},{9,13},{10,... | collective-permute-start | bytes 405512 | tf_op jit(solution)/shard_map/ppermute | solution.py:371
  9.2 9.9 %collective-permute-start.1 = (bf16[16,4224]{1,0:T(8,128)(2,1)S(1)}, bf16[16,4224]{1,0:T(8,128)(2,1)S(1)}, u32[]{:S(2)}, u32[]{:S(2)}) collective-permute-start(bf16[16,4224]{1,0:T(8,128)(2,1)S(1)} %get-tuple-element.25.rows_ref.refs_0_), channel_id=1, source_target_pairs={{0,2},{1,3},{2,0},{3,1},{4,6},{5,7},{6,4},{7,5},{8,10},{9,11},{10,... | collective-permute-start | bytes 405512 | tf_op jit(solution)/shard_map/ppermute | solution.py:371
  15.6 5.0 %collective-permute-start.2 = (bf16[16,4224]{1,0:T(8,128)(2,1)S(1)}, bf16[16,4224]{1,0:T(8,128)(2,1)S(1)}, u32[]{:S(2)}, u32[]{:S(2)}) collective-permute-start(bf16[16,4224]{1,0:T(8,128)(2,1)S(1)} %collective-permute-done.refs_1_), channel_id=1, source_target_pairs={{0,2},{1,3},{2,0},{3,1},{4,6},{5,7},{6,4},{7,5},{8,10},{9,11},{10,... | collective-permute-start | bytes 405512 | tf_op jit(solution)/shard_map/ppermute | solution.py:371
  18.5 2.1 %collective-permute-start.3 = (bf16[16,4224]{1,0:T(8,128)(2,1)S(1)}, bf16[16,4224]{1,0:T(8,128)(2,1)S(1)}, u32[]{:S(2)}, u32[]{:S(2)}) collective-permute-start(bf16[16,4224]{1,0:T(8,128)(2,1)S(1)} %get-tuple-element.26), channel_id=1, source_target_pairs={{0,1},{1,0},{2,3},{3,2},{4,5},{5,4},{6,7},{7,6},{8,9},{9,8},{10,11... | collective-permute-start | bytes 405512 | tf_op jit(solution)/shard_map/ppermute | solution.py:374
  18.6 2.0 %collective-permute-start.4 = (bf16[16,4224]{1,0:T(8,128)(2,1)S(1)}, bf16[16,4224]{1,0:T(8,128)(2,1)S(1)}, u32[]{:S(2)}, u32[]{:S(2)}) collective-permute-start(bf16[16,4224]{1,0:T(8,128)(2,1)S(1)} %collective-permute-done.refs_1_), channel_id=1, source_target_pairs={{0,1},{1,0},{2,3},{3,2},{4,5},{5,4},{6,7},{7,6},{8,9},{9,8},{10,11... | collective-permute-start | bytes 405512 | tf_op jit(solution)/shard_map/ppermute | solution.py:374
  19.1 1.5 %collective-permute-start.5 = (bf16[16,4224]{1,0:T(8,128)(2,1)S(1)}, bf16[16,4224]{1,0:T(8,128)(2,1)S(1)}, u32[]{:S(2)}, u32[]{:S(2)}) collective-permute-start(bf16[16,4224]{1,0:T(8,128)(2,1)S(1)} %collective-permute-done.1.refs_2_), channel_id=1, source_target_pairs={{0,1},{1,0},{2,3},{3,2},{4,5},{5,4},{6,7},{7,6},{8,9},{9,8},{10,11... | collective-permute-start | bytes 405512 | tf_op jit(solution)/shard_map/ppermute | solution.py:374
  20.6 1.4 %collective-permute-start.6 = (bf16[16,4224]{1,0:T(8,128)(2,1)S(1)}, bf16[16,4224]{1,0:T(8,128)(2,1)S(1)}, u32[]{:S(2)}, u32[]{:S(2)}) collective-permute-start(bf16[16,4224]{1,0:T(8,128)(2,1)S(1)} %collective-permute-done.2.refs_3_), channel_id=1, source_target_pairs={{0,1},{1,0},{2,3},{3,2},{4,5},{5,4},{6,7},{7,6},{8,9},{9,8},{10,11... | collective-permute-start | bytes 405512 | tf_op jit(solution)/shard_map/ppermute | solution.py:374
  24.3 16.1 %copy-start = (s32[1,128,8]{1,2,0:T(8,128)S(1)}, s32[1,128,8]{1,2,0:T(8,128)}, u32[]{:S(2)}) copy-start(s32[1,128,8]{1,2,0:T(8,128)} %param.9) | copy-start | bytes 12292
  24.4 1.6 %collective-permute-start.7 = (bf16[32,4224]{1,0:T(8,128)(2,1)S(1)}, bf16[32,4224]{1,0:T(8,128)(2,1)S(1)}, u32[]{:S(2)}, u32[]{:S(2)}) collective-permute-start(bf16[32,4224]{1,0:T(8,128)(2,1)S(1)} %get-tuple-element.30), channel_id=1, source_target_pairs={{0,1},{1,0},{2,3},{3,2},{4,5},{5,4},{6,7},{7,6},{8,9},{9,8},{10,11... | collective-permute-start | bytes 811016 | tf_op jit(solution)/shard_map/ppermute | solution.py:374
  26.0 5.7 %collective-permute-start.8 = (bf16[16,4224]{1,0:T(8,128)(2,1)S(1)}, bf16[16,4224]{1,0:T(8,128)(2,1)S(1)}, u32[]{:S(2)}, u32[]{:S(2)}) collective-permute-start(bf16[16,4224]{1,0:T(8,128)(2,1)S(1)} %get-tuple-element.32), channel_id=1, source_target_pairs={{0,2},{1,3},{2,0},{3,1},{4,6},{5,7},{6,4},{7,5},{8,10},{9,11},{10,... | collective-permute-start | bytes 405512 | tf_op jit(solution)/shard_map/ppermute | solution.py:371
  31.8 8.6 %collective-permute-start.9 = (bf16[8,4096]{1,0:T(8,128)(2,1)S(1)}, bf16[8,4096]{1,0:T(8,128)(2,1)S(1)}, u32[]{:S(2)}, u32[]{:S(2)}) collective-permute-start(bf16[8,4096]{1,0:T(8,128)(2,1)S(1)} %get-tuple-element.33), channel_id=1, source_target_pairs={{8,0},{9,1},{10,2},{11,3},{12,4},{13,5},{14,6},{15,7},{16,8},{17,9... | collective-permute-start | bytes 196616 | tf_op jit(solution)/shard_map/ppermute | solution.py:382
  32.4 8.1 %collective-permute-start.10 = (bf16[8,4096]{1,0:T(8,128)(2,1)S(1)}, bf16[8,4096]{1,0:T(8,128)(2,1)S(1)}, u32[]{:S(2)}, u32[]{:S(2)}) collective-permute-start(bf16[8,4096]{1,0:T(8,128)(2,1)S(1)} %get-tuple-element.34), channel_id=1, source_target_pairs={{8,4},{9,5},{10,6},{11,7},{12,0},{13,1},{14,2},{15,3},{16,12},{17,... | collective-permute-start | bytes 196616 | tf_op jit(solution)/shard_map/ppermute | solution.py:382
  36.0 4.5 %collective-permute-start.12 = (f32[8,128]{1,0:T(8,128)S(1)}, f32[8,128]{1,0:T(8,128)S(1)}, u32[]{:S(2)}, u32[]{:S(2)}) collective-permute-start(f32[8,128]{1,0:T(8,128)S(1)} %get-tuple-element.37), channel_id=1, source_target_pairs={{0,4},{1,5},{2,6},{3,7},{4,0},{5,1},{6,2},{7,3},{8,12},{9,13},{10,... | collective-permute-start | bytes 12296 | tf_op jit(solution)/shard_map/ppermute | solution.py:371

commit v4 on v3

--- a/solution.py
+++ b/solution.py
@@ -164,8 +164,14 @@
     return rows / rms, rms
 
 
-def rows_kernel(ids_hbm, weight_hbm, gain_hbm, hidden_hbm, grad_hbm, rows_ref, hand_ref, place_ref,
-                ids_ref, weight_ref, gain_ref, hidden_ref, sems):
+def in_parts(values):
+    high = values.astype(BF16).astype(F32)
+    middle = (values - high).astype(BF16).astype(F32)
+    return high, middle, values - high - middle
+
+
+def rows_kernel(ids_hbm, weight_hbm, gain_hbm, hidden_hbm, grad_hbm, rows_ref, normed_ref, place_ref,
+                ids_ref, weight_ref, gain_ref, hidden_ref, grad_ref, sems):
     tokens, width = hidden_ref.shape
     cap = SPECIALIST_CAP
     copies = [
@@ -175,7 +181,7 @@
             (hidden_hbm, hidden_ref),
             (gain_hbm, gain_ref),
             (weight_hbm, weight_ref),
-            (grad_hbm, hand_ref.at[:tokens, :width]),
+            (grad_hbm, grad_ref),
         ])
     ]
     for copy in copies:
@@ -192,27 +198,22 @@
     place = jnp.where(position == slot, member, 0.0)
     place_ref[...] = place
     copies[1].wait()
-    raw = take_rows(place.astype(BF16), hidden_ref[...])
-    normed, _ = normed_rows(raw)
+    normed, rms = normed_rows(take_rows(place.astype(BF16), hidden_ref[...]))
+    normed_ref[...] = normed
     copies[2].wait()
-    gain = gain_ref[...]
-    normed_in = normed * gain
-    high = gain.astype(BF16).astype(F32)
-    middle = (gain - high).astype(BF16).astype(F32)
-    low = gain - high - middle
-    blank = jnp.zeros((cap - 3, width), F32)
-    hand_ref[tokens:, :width] = jnp.concatenate([raw, high, middle, low, blank], axis=0).astype(BF16)
-    hand_ref[tokens:, width:] = jnp.concatenate([place, jnp.zeros_like(place)], axis=0).astype(BF16)
-    hand_ref[:tokens, width:] = jnp.zeros((tokens, LANES), BF16)
+    normed_in = normed * gain_ref[...]
     copies[3].wait()
     weight = jnp.sum(
         jnp.where(hit, weight_ref[...].astype(F32), 0.0), axis=0, keepdims=True
     )
     taken = jnp.sum(place * weight, axis=1, keepdims=True)
-    taken = jnp.broadcast_to(taken, (cap, LANES))
-    rows_ref[:, width:] = jnp.concatenate([taken, taken], axis=0).astype(BF16)
+    lane = lax.broadcasted_iota(jnp.int32, (cap, LANES), 1)
+    extra = jnp.broadcast_to(taken, (cap, LANES))
+    for number, part in enumerate(in_parts(rms)):
+        extra = jnp.where(lane == number + 1, part, extra)
+    rows_ref[:, width:] = jnp.concatenate([extra, place], axis=0).astype(BF16)
     copies[4].wait()
-    grad = take_rows(place.astype(BF16), hand_ref[:tokens, :width])
+    grad = take_rows(place.astype(BF16), grad_ref[...])
     rows_ref[:, :width] = jnp.concatenate([normed_in, grad], axis=0).astype(BF16)
 
 
@@ -287,15 +288,26 @@
     own_ref[:, width:] = comb[:half]
 
 
-def split_kernel(keep_ref, got_ref, own_ref, other_ref, own_comb_ref, other_comb_ref):
+def split_kernel(keep_ref, got_ref, normed_ref, rows_ref, far_ref, gain_ref, after_ref,
+                 own_ref, other_ref, own_comb_ref, other_comb_ref):
+    del after_ref
+    cap, width = own_ref.shape
     total = keep_ref[...].astype(F32) + got_ref[...].astype(F32)
-    half, width = own_ref.shape
-    other_ref[...] = total[half:, :width].astype(BF16)
-    own_ref[...] = total[:half, :width].astype(BF16)
+    gain = gain_ref[...]
+    far = far_ref[...].astype(F32)
+    extra = jnp.concatenate([rows_ref[:, width:].astype(F32)[:cap], far[:cap, width:]], axis=0)
+    rms = extra[:, 1:2] + extra[:, 2:3] + extra[:, 3:4]
+    normed = jnp.concatenate([normed_ref[...], far[:cap, :width] / gain], axis=0)
+    scaled = total[:, :width] * gain
+    inner = jnp.mean(scaled * normed, axis=-1, keepdims=True)
+    change = (scaled - normed * inner) / rms
+    other_ref[:, :width] = change[cap:].astype(BF16)
+    other_ref[:, width:] = far[cap:, width:].astype(BF16)
+    own_ref[...] = change[:cap].astype(BF16)
     comb = total[:, width:]
     comb = comb + pltpu.roll(comb, LANES // 2, 1)
-    other_comb_ref[...] = comb[half:]
-    own_comb_ref[...] = comb[:half]
+    other_comb_ref[...] = comb[cap:]
+    own_comb_ref[...] = comb[:cap]
 
 
 def weights_kernel(rows_ref, both_ref, act_ref, after_ref, both_out, act_out):
@@ -329,28 +341,50 @@
     )(rows, both, act, after)
 
 
-def finish_kernel(own_ref, other_ref, hand_ref, own_comb_ref, other_comb_ref, ids_ref, place_ref,
+def finish_kernel(other_ref, own_ref, grad_ref, other_comb_ref, own_comb_ref, ids_ref, place_ref,
                   out_ref, comb_ref):
-    cap = SPECIALIST_CAP
-    tokens, width = out_ref.shape
-    comb = own_comb_ref[...] + other_comb_ref[...]
-    comb = jnp.sum(place_ref[...] * comb, axis=0, keepdims=True)
-    comb_ref[...] = jnp.where(ids_ref[...] == 0, comb, 0.0)
-    side = hand_ref[tokens:, :].astype(F32)
-    place = side[:cap, width:]
-    gain = side[cap : cap + 1, :width] + side[cap + 1 : cap + 2, :width]
-    gain = gain + side[cap + 2 : cap + 3, :width]
-    normed, rms = normed_rows(side[:cap, :width])
-    grad = hand_ref[:tokens, :width]
-    own = take_rows(place.astype(BF16), grad)
-    total = own_ref[...].astype(F32) + other_ref[...].astype(F32)
-    scaled = total * gain
-    inner = jnp.mean(scaled * normed, axis=-1, keepdims=True)
-    rows = (own + (scaled - normed * inner) / rms).astype(BF16)
-    back = place.T
+    width = grad_ref.shape[1]
+    chunk = out_ref.shape[1]
+
+    @pl.when(pl.program_id(0) == 0)
+    def _():
+        comb = own_comb_ref[...] + other_comb_ref[...]
+        comb = jnp.sum(place_ref[...] * comb, axis=0, keepdims=True)
+        comb_ref[...] = jnp.where(ids_ref[...] == 0, comb, 0.0)
+
+    columns = pl.ds(pl.multiple_of(pl.program_id(0) * chunk, chunk), chunk)
+    place = other_ref[:, width:]
+    grad = grad_ref[:, columns]
+    change = own_ref[:, columns].astype(F32) + other_ref[:, columns].astype(F32)
+    rows = (take_rows(place, grad) + change).astype(BF16)
+    back = place.astype(F32).T
     spread = take_rows(back.astype(BF16), rows)
     named = jnp.sum(back, axis=1, keepdims=True) > 0.0
     out_ref[...] = jnp.where(named, spread, grad.astype(F32)).astype(BF16)
+
+
+def finish(other, own, grad, other_comb, own_comb, ids, place):
+    tokens, width = grad.shape
+    chunk = min(width, 1024)
+    return pl.pallas_call(
+        finish_kernel,
+        grid=(width // chunk,),
+        in_specs=[IN_VMEM] * 7,
+        out_specs=[
+            pl.BlockSpec((tokens, chunk), lambda i: (0, i)),
+            pl.BlockSpec(ids.shape, lambda i: (0, 0)),
+        ],
+        out_shape=[
+            jax.ShapeDtypeStruct((tokens, width), BF16),
+            jax.ShapeDtypeStruct(ids.shape, F32),
+        ],
+        compiler_params=pltpu.CompilerParams(vmem_limit_bytes=24 << 20),
+        cost_estimate=pl.CostEstimate(
+            flops=4 * tokens * width * place.shape[0],
+            bytes_accessed=4 * tokens * width,
+            transcendentals=0,
+        ),
+    )(other, own, grad, other_comb, own_comb, ids, place)
 
 
 def on_one(hidden_in, out_grad, expert_ids, route_weight, norm_gain, w_gate_up, w_down):
@@ -381,9 +415,10 @@
         ]
         return lax.ppermute(block, ("pipe", "expert"), route)
 
-    rows, hand, place = call(
+    next_grad = handed(out_grad[0], 0)
+    rows, normed, place = call(
         rows_kernel,
-        [((2 * cap, wide), BF16), ((tokens + 2 * cap, wide), BF16), ((cap, tokens), F32)],
+        [((2 * cap, wide), BF16), ((cap, width), F32), ((cap, tokens), F32)],
         4 * tokens * width * cap,
         4 * tokens * width,
         in_specs=[IN_HBM] * 5,
@@ -392,13 +427,13 @@
             pltpu.VMEM(weights.shape, weights.dtype),
             pltpu.VMEM(norm_gain.shape, norm_gain.dtype),
             pltpu.VMEM((tokens, width), BF16),
+            pltpu.VMEM((tokens, width), BF16),
             pltpu.SemaphoreType.DMA((5,)),
         ],
     )(*map(in_hbm, (ids, weights, norm_gain, hidden_in[0], out_grad[0])))
     far = across(rows, 2)
     near = across(rows, 1)
     farthest = across(far, 1)
-    handed_block = handed(hand, 0)
     slab_near, down_near, rows_again = call(
         fetch_kernel,
         [(slab.shape, BF16), (down.shape, BF16), (rows.shape, BF16)],
@@ -424,19 +459,17 @@
     own_half, other_half = call(
         halve_kernel, [((2 * cap, wide), BF16)] * 2, 4 * cap * width, 16 * cap * width
     )(keep, beside(send))
+    gate_up_out, down_out = weight_grads(all_rows, both, act, own_half)
     own, other, own_comb, other_comb = call(
         split_kernel,
-        [((cap, width), BF16)] * 2 + [((cap, LANES), F32)] * 2,
+        [((cap, width), BF16), ((cap, wide), BF16)] + [((cap, LANES), F32)] * 2,
         2 * cap * width,
         8 * cap * width,
-    )(own_half, across(other_half, 1))
-    gate_up_out, down_out = weight_grads(all_rows, both, act, own_comb)
-    out, combined = call(
-        finish_kernel,
-        [((tokens, width), BF16), ((SPLIT, tokens), F32)],
-        4 * tokens * width * cap,
-        4 * tokens * width,
-    )(handed(own, 0), handed(other, 2), handed_block, own_comb, across(other_comb, 2), ids, place)
+        in_specs=[IN_VMEM] * 6 + [IN_HBM],
+    )(own_half, across(other_half, 1), normed, rows, far, norm_gain, in_hbm(down_out))
+    out, combined = finish(
+        handed(other, 2), handed(own, 0), next_grad, across(other_comb, 2), own_comb, ids, place
+    )
     return (
         out[None],
         gate_up_out.reshape(1, 1, 2, hidden, width),

time: 42.3 us -> 43.3 us (1.024)
  Pallas kernels: 11.8 us -> 12.7 us
    pallas_call x3, Pallas kernels: 3.8 us -> 4.67 us  [the longest x1 2.46 us: finish(): pl.pallas_call(finish_kernel, grid=(width // chunk,), in_specs=[IN_VMEM]...]
  transfers between devices with their start and end apart: 13 -> 13, of which waited for: 6 -> 6; matrix products, arithmetic and copies ran while one was open for 0% -> 0% of each run, Pallas kernels for 19% -> 24%
where the time goes in v4:
time: 43.3 us; the launch traced here: 43.1 us
  starting transfers between devices  15.1 us (35%)
  waiting for transfers between devices  14.6 us (34%)
  Pallas kernels  12.7 us (29%)
  between operations  0.72 us (2%)
    ppermute x5, waiting for transfers between devices, across(): lax.ppermute(block, 'expert', [(i, i ^ 2 * offset) for i in range(devices)])  11.9 us
    ppermute x3, starting transfers between devices, handed(): return lax.ppermute(block, ('pipe', 'expert'), route)  8.11 us
    ppermute x5, starting transfers between devices, across(): lax.ppermute(block, 'expert', [(i, i ^ 2 * offset) for i in range(devices)])  6.15 us
    pallas_call x1, Pallas kernels, weight_grads(): pl.pallas_call(weights_kernel, grid=(width // chunk,), in_specs=[IN_VMEM,...  3.18 us
    ppermute x5, waiting for transfers between devices, beside(): return lax.ppermute(block, 'expert', [(i, i ^ 1) for i in range(devices)])  2.74 us
    pallas_call x1, Pallas kernels, finish(): pl.pallas_call(finish_kernel, grid=(width // chunk,), in_specs=[IN_VMEM]...  2.46 us
    pallas_call x1, Pallas kernels, on_one(): call(hidden_kernel, [((total_rows // 2, wide), BF16), ((total_rows // 2,...  2.37 us
    pallas_call x1, Pallas kernels, on_one(): call(fetch_kernel, [(slab.shape, BF16), (down.shape, BF16), (rows.shape,...  2.37 us
  transfers between devices with their start and end apart: 13, of which 6 were waited for; matrix products, arithmetic and copies ran while one was open for 0% of the time, Pallas kernels for 24%

profile of v4, /device:TPU:0, one launch (start us, length us, event | category | flops | bytes accessed | tf_op | source)
XLA Modules:
  0.0 43.1 jit_solution(2655988977983214232)
XLA Ops:
  0.6 3.9 %collective-permute-start.11 = (bf16[128,4096]{1,0:T(8,128)(2,1)}, bf16[128,4096]{1,0:T(8,128)(2,1)S(1)}, u32[]{:S(2)}, u32[]{:S(2)}) collective-permute-start(bf16[128,4096]{1,0:T(8,128)(2,1)} %bitcast.22), channel_id=1, source_target_pairs={{8,0},{9,1},{10,2},{11,3},{12,4},{13,5},{14,6},{15,7},{16,8},{17,9... | collective-permute-start | bytes 3145736 | tf_op jit(solution)/shard_map/ppermute | solution.py:416
  4.6 2.0 %shard_map.102 = (bf16[16,4224]{1,0:T(8,128)(2,1)S(1)}, f32[8,4096]{1,0:T(8,128)S(1)}, f32[8,128]{1,0:T(8,128)S(1)}) custom-call(s32[8,128]{1,0:T(8,128)} %bitcast.16, bf16[8,128]{1,0:T(8,128)(2,1)} %bitcast.24, f32[1,4096]{1,0:T(1,128)} %gain_ref.1, bf16[128,4096]{1,0:T(8,128)(2,1)} %bitcast.21, bf16[128,4096]{1,0:T(8,128)(2,1)} %bitcast.23), custom_call_target="tpu_custom_call" | custom-call | flops 16777216 | bytes 2097152 | tf_op jit(solution)/shard_map/pallas_call | solution.py:419
  6.6 2.7 %collective-permute-start = (bf16[16,4224]{1,0:T(8,128)(2,1)S(1)}, bf16[16,4224]{1,0:T(8,128)(2,1)S(1)}, u32[]{:S(2)}, u32[]{:S(2)}) collective-permute-start(bf16[16,4224]{1,0:T(8,128)(2,1)S(1)} %get-tuple-element.25.rows_ref.refs_0_), channel_id=1, source_target_pairs={{0,4},{1,5},{2,6},{3,7},{4,0},{5,1},{6,2},{7,3},{8,12},{9,13},{10,... | collective-permute-start | bytes 405512 | tf_op jit(solution)/shard_map/ppermute | solution.py:405
  9.2 1.6 %collective-permute-start.1 = (bf16[16,4224]{1,0:T(8,128)(2,1)S(1)}, bf16[16,4224]{1,0:T(8,128)(2,1)S(1)}, u32[]{:S(2)}, u32[]{:S(2)}) collective-permute-start(bf16[16,4224]{1,0:T(8,128)(2,1)S(1)} %get-tuple-element.25.rows_ref.refs_0_), channel_id=1, source_target_pairs={{0,2},{1,3},{2,0},{3,1},{4,6},{5,7},{6,4},{7,5},{8,10},{9,11},{10,... | collective-permute-start | bytes 405512 | tf_op jit(solution)/shard_map/ppermute | solution.py:405
  10.8 4.8 %collective-permute-done.refs_1_.far_ref = bf16[16,4224]{1,0:T(8,128)(2,1)S(1)} collective-permute-done((bf16[16,4224]{1,0:T(8,128)(2,1)S(1)}, bf16[16,4224]{1,0:T(8,128)(2,1)S(1)}, u32[]{:S(2)}, u32[]{:S(2)}) %collective-permute-start) | collective-permute-done | bytes 135200 | tf_op jit(solution)/shard_map/ppermute | solution.py:405
  15.6 0.6 %collective-permute-start.2 = (bf16[16,4224]{1,0:T(8,128)(2,1)S(1)}, bf16[16,4224]{1,0:T(8,128)(2,1)S(1)}, u32[]{:S(2)}, u32[]{:S(2)}) collective-permute-start(bf16[16,4224]{1,0:T(8,128)(2,1)S(1)} %collective-permute-done.refs_1_.far_ref), channel_id=1, source_target_pairs={{0,2},{1,3},{2,0},{3,1},{4,6},{5,7},{6,4},{7,5},{8,10},{9,11},{10,... | collective-permute-start | bytes 405512 | tf_op jit(solution)/shard_map/ppermute | solution.py:405
  16.2 2.4 %shard_map.103 = (bf16[384,4096]{1,0:T(8,128)(2,1)S(1)}, bf16[192,4096]{1,0:T(8,128)(2,1)S(1)}, bf16[16,4224]{1,0:T(8,128)(2,1)S(1)}) custom-call(bf16[384,4096]{1,0:T(8,128)(2,1)} %bitcast.18, bf16[192,4096]{1,0:T(8,128)(2,1)} %bitcast.20, bf16[16,4224]{1,0:T(8,128)(2,1)S(1)} %get-tuple-element.25.rows_ref.refs_0_), custom_call_target="tpu_custom_call" | custom-call | bytes 4718592 | tf_op jit(solution)/shard_map/pallas_call | solution.py:437
  18.5 0.1 collective-permute-start.3
  18.6 0.5 %collective-permute-start.4 = (bf16[16,4224]{1,0:T(8,128)(2,1)S(1)}, bf16[16,4224]{1,0:T(8,128)(2,1)S(1)}, u32[]{:S(2)}, u32[]{:S(2)}) collective-permute-start(bf16[16,4224]{1,0:T(8,128)(2,1)S(1)} %collective-permute-done.refs_1_.far_ref), channel_id=1, source_target_pairs={{0,1},{1,0},{2,3},{3,2},{4,5},{5,4},{6,7},{7,6},{8,9},{9,8},{10,11... | collective-permute-start | bytes 405512 | tf_op jit(solution)/shard_map/ppermute | solution.py:408
  19.1 0.0 collective-permute-done.1.refs_2_
  19.1 0.1 collective-permute-start.5
  19.2 1.4 %collective-permute-done.2.refs_3_ = bf16[16,4224]{1,0:T(8,128)(2,1)S(1)} collective-permute-done((bf16[16,4224]{1,0:T(8,128)(2,1)S(1)}, bf16[16,4224]{1,0:T(8,128)(2,1)S(1)}, u32[]{:S(2)}, u32[]{:S(2)}) %collective-permute-start.2) | collective-permute-done | bytes 135200 | tf_op jit(solution)/shard_map/ppermute | solution.py:405
  20.6 0.0 collective-permute-start.6
  20.6 0.0 collective-permute-done.3.refs_4_
  20.6 0.0 collective-permute-done.4.refs_5_
  20.6 1.3 %collective-permute-done.6.refs_7_ = bf16[16,4224]{1,0:T(8,128)(2,1)S(1)} collective-permute-done((bf16[16,4224]{1,0:T(8,128)(2,1)S(1)}, bf16[16,4224]{1,0:T(8,128)(2,1)S(1)}, u32[]{:S(2)}, u32[]{:S(2)}) %collective-permute-start.6) | collective-permute-done | bytes 135200 | tf_op jit(solution)/shard_map/ppermute | solution.py:408
  22.0 2.4 %shard_map.104 = (bf16[32,4224]{1,0:T(8,128)(2,1)S(1)}, bf16[32,4224]{1,0:T(8,128)(2,1)S(1)}, bf16[128,4096]{1,0:T(8,128)(2,1)S(1)}, bf16[384,128]{1,0:T(8,128)(2,1)S(1)}, bf16[192,128]{1,0:T(8,128)(2,1)S(1)}) custom-call(bf16[16,4224]{1,0:T(8,128)(2,1)S(1)} %get-tuple-element.25.rows_ref.refs_0_, bf16[16,4224]{1,0:T(8,128)(2,1)S(1)} %collective-permute-done.refs_1_.far_ref, ...), custom_call_target="tpu_custom_call" | custom-call | flops 503316480 | bytes 4718592 | tf_op jit(solution)/shard_map/pallas_call | solution.py:447
  24.3 0.0 copy-start.1
  24.4 0.2 collective-permute-start.7
  24.6 1.4 %collective-permute-done.7.got_ref = bf16[32,4224]{1,0:T(8,128)(2,1)S(1)} collective-permute-done((bf16[32,4224]{1,0:T(8,128)(2,1)S(1)}, bf16[32,4224]{1,0:T(8,128)(2,1)S(1)}, u32[]{:S(2)}, u32[]{:S(2)}) %collective-permute-start.7) | collective-permute-done | bytes 270368 | tf_op jit(solution)/shard_map/ppermute | solution.py:408
  26.0 0.1 shard_map.105
  26.0 1.1 %collective-permute-start.8 = (bf16[16,4224]{1,0:T(8,128)(2,1)S(1)}, bf16[16,4224]{1,0:T(8,128)(2,1)S(1)}, u32[]{:S(2)}, u32[]{:S(2)}) collective-permute-start(bf16[16,4224]{1,0:T(8,128)(2,1)S(1)} %get-tuple-element.32), channel_id=1, source_target_pairs={{0,2},{1,3},{2,0},{3,1},{4,6},{5,7},{6,4},{7,5},{8,10},{9,11},{10,... | collective-permute-start | bytes 405512 | tf_op jit(solution)/shard_map/ppermute | solution.py:405
  27.2 3.2 %shard_map.106 = (bf16[384,4096]{1,0:T(8,128)(2,1)}, bf16[192,4096]{1,0:T(8,128)(2,1)}) custom-call(bf16[128,4096]{1,0:T(8,128)(2,1)S(1)} %get-tuple-element.34.rows_ref, bf16[384,128]{1,0:T(8,128)(2,1)S(1)} %get-tuple-element.35.both_ref, bf16[192,128]{1,0:T(8,128)(2,1)S(1)} %get-tuple-element.36.act_ref, ...), custom_call_target="tpu_custom_call" | custom-call | flops 603979776 | bytes 4718592 | tf_op jit(solution)/shard_map/pallas_call | solution.py:326
  30.3 1.4 %collective-permute-done.8.got_ref = bf16[16,4224]{1,0:T(8,128)(2,1)S(1)} collective-permute-done((bf16[16,4224]{1,0:T(8,128)(2,1)S(1)}, bf16[16,4224]{1,0:T(8,128)(2,1)S(1)}, u32[]{:S(2)}, u32[]{:S(2)}) %collective-permute-start.8) | collective-permute-done | bytes 135200 | tf_op jit(solution)/shard_map/ppermute | solution.py:405
  31.7 0.2 shard_map.107
  32.0 2.7 %collective-permute-start.9 = (bf16[8,4224]{1,0:T(8,128)(2,1)S(1)}, bf16[8,4224]{1,0:T(8,128)(2,1)S(1)}, u32[]{:S(2)}, u32[]{:S(2)}) collective-permute-start(bf16[8,4224]{1,0:T(8,128)(2,1)S(1)} %get-tuple-element.38), channel_id=1, source_target_pairs={{8,4},{9,5},{10,6},{11,7},{12,0},{13,1},{14,2},{15,3},{16,12},{17,... | collective-permute-start | bytes 202760 | tf_op jit(solution)/shard_map/ppermute | solution.py:416
  34.7 1.4 %collective-permute-start.10 = (bf16[8,4096]{1,0:T(8,128)(2,1)S(1)}, bf16[8,4096]{1,0:T(8,128)(2,1)S(1)}, u32[]{:S(2)}, u32[]{:S(2)}) collective-permute-start(bf16[8,4096]{1,0:T(8,128)(2,1)S(1)} %get-tuple-element.39), channel_id=1, source_target_pairs={{8,0},{9,1},{10,2},{11,3},{12,4},{13,5},{14,6},{15,7},{16,8},{17,9... | collective-permute-start | bytes 196616 | tf_op jit(solution)/shard_map/ppermute | solution.py:416
  36.1 0.2 collective-permute-start.12
  36.4 4.3 %collective-permute-done.12.other_comb_ref = f32[8,128]{1,0:T(8,128)S(1)} collective-permute-done((f32[8,128]{1,0:T(8,128)S(1)}, f32[8,128]{1,0:T(8,128)S(1)}, u32[]{:S(2)}, u32[]{:S(2)}) %collective-permute-start.12) | collective-permute-done | bytes 4128 | tf_op jit(solution)/shard_map/ppermute | solution.py:405
  40.6 0.0 collective-permute-done.10.own_ref
  40.6 0.0 collective-permute-done.9.other_ref
  40.7 2.5 %shard_map.108 = (bf16[128,4096]{1,0:T(8,128)(2,1)}, f32[8,128]{1,0:T(8,128)}) custom-call(bf16[8,4224]{1,0:T(8,128)(2,1)S(1)} %collective-permute-done.9.other_ref, bf16[8,4096]{1,0:T(8,128)(2,1)S(1)} %collective-permute-done.10.own_ref, bf16[128,4096]{1,0:T(8,128)(2,1)S(1)} %collective-permute-done.11.grad_ref, ...), custom_call_target="tpu_custom_call" | custom-call | flops 16777216 | bytes 2097152 | tf_op jit(solution)/shard_map/pallas_call | solution.py:369
  (5 shorter events, 0.0 us)
Async XLA Ops:
  0.6 40.0 %collective-permute-start.11 = (bf16[128,4096]{1,0:T(8,128)(2,1)}, bf16[128,4096]{1,0:T(8,128)(2,1)S(1)}, u32[]{:S(2)}, u32[]{:S(2)}) collective-permute-start(bf16[128,4096]{1,0:T(8,128)(2,1)} %bitcast.22), channel_id=1, source_target_pairs={{8,0},{9,1},{10,2},{11,3},{12,4},{13,5},{14,6},{15,7},{16,8},{17,9... | collective-permute-start | bytes 3145736 | tf_op jit(solution)/shard_map/ppermute | solution.py:416
  6.6 9.0 %collective-permute-start = (bf16[16,4224]{1,0:T(8,128)(2,1)S(1)}, bf16[16,4224]{1,0:T(8,128)(2,1)S(1)}, u32[]{:S(2)}, u32[]{:S(2)}) collective-permute-start(bf16[16,4224]{1,0:T(8,128)(2,1)S(1)} %get-tuple-element.25.rows_ref.refs_0_), channel_id=1, source_target_pairs={{0,4},{1,5},{2,6},{3,7},{4,0},{5,1},{6,2},{7,3},{8,12},{9,13},{10,... | collective-permute-start | bytes 405512 | tf_op jit(solution)/shard_map/ppermute | solution.py:405
  9.2 9.9 %collective-permute-start.1 = (bf16[16,4224]{1,0:T(8,128)(2,1)S(1)}, bf16[16,4224]{1,0:T(8,128)(2,1)S(1)}, u32[]{:S(2)}, u32[]{:S(2)}) collective-permute-start(bf16[16,4224]{1,0:T(8,128)(2,1)S(1)} %get-tuple-element.25.rows_ref.refs_0_), channel_id=1, source_target_pairs={{0,2},{1,3},{2,0},{3,1},{4,6},{5,7},{6,4},{7,5},{8,10},{9,11},{10,... | collective-permute-start | bytes 405512 | tf_op jit(solution)/shard_map/ppermute | solution.py:405
  15.6 5.0 %collective-permute-start.2 = (bf16[16,4224]{1,0:T(8,128)(2,1)S(1)}, bf16[16,4224]{1,0:T(8,128)(2,1)S(1)}, u32[]{:S(2)}, u32[]{:S(2)}) collective-permute-start(bf16[16,4224]{1,0:T(8,128)(2,1)S(1)} %collective-permute-done.refs_1_.far_ref), channel_id=1, source_target_pairs={{0,2},{1,3},{2,0},{3,1},{4,6},{5,7},{6,4},{7,5},{8,10},{9,11},{10,... | collective-permute-start | bytes 405512 | tf_op jit(solution)/shard_map/ppermute | solution.py:405
  18.5 2.1 %collective-permute-start.3 = (bf16[16,4224]{1,0:T(8,128)(2,1)S(1)}, bf16[16,4224]{1,0:T(8,128)(2,1)S(1)}, u32[]{:S(2)}, u32[]{:S(2)}) collective-permute-start(bf16[16,4224]{1,0:T(8,128)(2,1)S(1)} %get-tuple-element.26), channel_id=1, source_target_pairs={{0,1},{1,0},{2,3},{3,2},{4,5},{5,4},{6,7},{7,6},{8,9},{9,8},{10,11... | collective-permute-start | bytes 405512 | tf_op jit(solution)/shard_map/ppermute | solution.py:408
  18.6 2.0 %collective-permute-start.4 = (bf16[16,4224]{1,0:T(8,128)(2,1)S(1)}, bf16[16,4224]{1,0:T(8,128)(2,1)S(1)}, u32[]{:S(2)}, u32[]{:S(2)}) collective-permute-start(bf16[16,4224]{1,0:T(8,128)(2,1)S(1)} %collective-permute-done.refs_1_.far_ref), channel_id=1, source_target_pairs={{0,1},{1,0},{2,3},{3,2},{4,5},{5,4},{6,7},{7,6},{8,9},{9,8},{10,11... | collective-permute-start | bytes 405512 | tf_op jit(solution)/shard_map/ppermute | solution.py:408
  19.1 1.5 %collective-permute-start.5 = (bf16[16,4224]{1,0:T(8,128)(2,1)S(1)}, bf16[16,4224]{1,0:T(8,128)(2,1)S(1)}, u32[]{:S(2)}, u32[]{:S(2)}) collective-permute-start(bf16[16,4224]{1,0:T(8,128)(2,1)S(1)} %collective-permute-done.1.refs_2_), channel_id=1, source_target_pairs={{0,1},{1,0},{2,3},{3,2},{4,5},{5,4},{6,7},{7,6},{8,9},{9,8},{10,11... | collective-permute-start | bytes 405512 | tf_op jit(solution)/shard_map/ppermute | solution.py:408
  20.6 1.4 %collective-permute-start.6 = (bf16[16,4224]{1,0:T(8,128)(2,1)S(1)}, bf16[16,4224]{1,0:T(8,128)(2,1)S(1)}, u32[]{:S(2)}, u32[]{:S(2)}) collective-permute-start(bf16[16,4224]{1,0:T(8,128)(2,1)S(1)} %collective-permute-done.2.refs_3_), channel_id=1, source_target_pairs={{0,1},{1,0},{2,3},{3,2},{4,5},{5,4},{6,7},{7,6},{8,9},{9,8},{10,11... | collective-permute-start | bytes 405512 | tf_op jit(solution)/shard_map/ppermute | solution.py:408
  22.0 9.8 %copy-start = (f32[1,4096]{1,0:T(1,128)S(1)}, f32[1,4096]{1,0:T(1,128)}, u32[]{:S(2)}) copy-start(f32[1,4096]{1,0:T(1,128)} %gain_ref.1) | copy-start | bytes 49156
  24.3 16.3 %copy-start.1 = (s32[1,128,8]{1,2,0:T(8,128)S(1)}, s32[1,128,8]{1,2,0:T(8,128)}, u32[]{:S(2)}) copy-start(s32[1,128,8]{1,2,0:T(8,128)} %param.9) | copy-start | bytes 12292
  24.4 1.6 %collective-permute-start.7 = (bf16[32,4224]{1,0:T(8,128)(2,1)S(1)}, bf16[32,4224]{1,0:T(8,128)(2,1)S(1)}, u32[]{:S(2)}, u32[]{:S(2)}) collective-permute-start(bf16[32,4224]{1,0:T(8,128)(2,1)S(1)} %get-tuple-element.30), channel_id=1, source_target_pairs={{0,1},{1,0},{2,3},{3,2},{4,5},{5,4},{6,7},{7,6},{8,9},{9,8},{10,11... | collective-permute-start | bytes 811016 | tf_op jit(solution)/shard_map/ppermute | solution.py:408
  26.0 5.7 %collective-permute-start.8 = (bf16[16,4224]{1,0:T(8,128)(2,1)S(1)}, bf16[16,4224]{1,0:T(8,128)(2,1)S(1)}, u32[]{:S(2)}, u32[]{:S(2)}) collective-permute-start(bf16[16,4224]{1,0:T(8,128)(2,1)S(1)} %get-tuple-element.32), channel_id=1, source_target_pairs={{0,2},{1,3},{2,0},{3,1},{4,6},{5,7},{6,4},{7,5},{8,10},{9,11},{10,... | collective-permute-start | bytes 405512 | tf_op jit(solution)/shard_map/ppermute | solution.py:405
  32.0 8.7 %collective-permute-start.9 = (bf16[8,4224]{1,0:T(8,128)(2,1)S(1)}, bf16[8,4224]{1,0:T(8,128)(2,1)S(1)}, u32[]{:S(2)}, u32[]{:S(2)}) collective-permute-start(bf16[8,4224]{1,0:T(8,128)(2,1)S(1)} %get-tuple-element.38), channel_id=1, source_target_pairs={{8,4},{9,5},{10,6},{11,7},{12,0},{13,1},{14,2},{15,3},{16,12},{17,... | collective-permute-start | bytes 202760 | tf_op jit(solution)/shard_map/ppermute | solution.py:416
  34.7 5.9 %collective-permute-start.10 = (bf16[8,4096]{1,0:T(8,128)(2,1)S(1)}, bf16[8,4096]{1,0:T(8,128)(2,1)S(1)}, u32[]{:S(2)}, u32[]{:S(2)}) collective-permute-start(bf16[8,4096]{1,0:T(8,128)(2,1)S(1)} %get-tuple-element.39), channel_id=1, source_target_pairs={{8,0},{9,1},{10,2},{11,3},{12,4},{13,5},{14,6},{15,7},{16,8},{17,9... | collective-permute-start | bytes 196616 | tf_op jit(solution)/shard_map/ppermute | solution.py:416
  36.1 4.5 %collective-permute-start.12 = (f32[8,128]{1,0:T(8,128)S(1)}, f32[8,128]{1,0:T(8,128)S(1)}, u32[]{:S(2)}, u32[]{:S(2)}) collective-permute-start(f32[8,128]{1,0:T(8,128)S(1)} %get-tuple-element.40), channel_id=1, source_target_pairs={{0,4},{1,5},{2,6},{3,7},{4,0},{5,1},{6,2},{7,3},{8,12},{9,13},{10,... | collective-permute-start | bytes 12296 | tf_op jit(solution)/shard_map/ppermute | solution.py:405

commit v5 on v4

--- a/solution.py
+++ b/solution.py
@@ -344,47 +344,18 @@
 def finish_kernel(other_ref, own_ref, grad_ref, other_comb_ref, own_comb_ref, ids_ref, place_ref,
                   out_ref, comb_ref):
     width = grad_ref.shape[1]
-    chunk = out_ref.shape[1]
-
-    @pl.when(pl.program_id(0) == 0)
-    def _():
-        comb = own_comb_ref[...] + other_comb_ref[...]
-        comb = jnp.sum(place_ref[...] * comb, axis=0, keepdims=True)
-        comb_ref[...] = jnp.where(ids_ref[...] == 0, comb, 0.0)
-
-    columns = pl.ds(pl.multiple_of(pl.program_id(0) * chunk, chunk), chunk)
+    comb = own_comb_ref[...] + other_comb_ref[...]
+    comb = jnp.sum(place_ref[...] * comb, axis=0, keepdims=True)
+    comb_ref[...] = jnp.where(ids_ref[...] == 0, comb, 0.0)
     place = other_ref[:, width:]
-    grad = grad_ref[:, columns]
-    change = own_ref[:, columns].astype(F32) + other_ref[:, columns].astype(F32)
-    rows = (take_rows(place, grad) + change).astype(BF16)
+    grad = grad_ref[...]
+    own = take_rows(place, grad)
+    change = own_ref[...].astype(F32) + other_ref[:, :width].astype(F32)
+    rows = (own + change).astype(BF16)
     back = place.astype(F32).T
     spread = take_rows(back.astype(BF16), rows)
     named = jnp.sum(back, axis=1, keepdims=True) > 0.0
     out_ref[...] = jnp.where(named, spread, grad.astype(F32)).astype(BF16)
-
-
-def finish(other, own, grad, other_comb, own_comb, ids, place):
-    tokens, width = grad.shape
-    chunk = min(width, 1024)
-    return pl.pallas_call(
-        finish_kernel,
-        grid=(width // chunk,),
-        in_specs=[IN_VMEM] * 7,
-        out_specs=[
-            pl.BlockSpec((tokens, chunk), lambda i: (0, i)),
-            pl.BlockSpec(ids.shape, lambda i: (0, 0)),
-        ],
-        out_shape=[
-            jax.ShapeDtypeStruct((tokens, width), BF16),
-            jax.ShapeDtypeStruct(ids.shape, F32),
-        ],
-        compiler_params=pltpu.CompilerParams(vmem_limit_bytes=24 << 20),
-        cost_estimate=pl.CostEstimate(
-            flops=4 * tokens * width * place.shape[0],
-            bytes_accessed=4 * tokens * width,
-            transcendentals=0,
-        ),
-    )(other, own, grad, other_comb, own_comb, ids, place)
 
 
 def on_one(hidden_in, out_grad, expert_ids, route_weight, norm_gain, w_gate_up, w_down):
@@ -437,7 +408,7 @@
     slab_near, down_near, rows_again = call(
         fetch_kernel,
         [(slab.shape, BF16), (down.shape, BF16), (rows.shape, BF16)],
-        0,
+        30_000_000_000,
         6 * hidden * width,
         in_specs=[IN_HBM, IN_HBM, IN_VMEM],
         scratch=[pltpu.SemaphoreType.DMA((2,))],
@@ -467,9 +438,12 @@
         8 * cap * width,
         in_specs=[IN_VMEM] * 6 + [IN_HBM],
     )(own_half, across(other_half, 1), normed, rows, far, norm_gain, in_hbm(down_out))
-    out, combined = finish(
-        handed(other, 2), handed(own, 0), next_grad, across(other_comb, 2), own_comb, ids, place
-    )
+    out, combined = call(
+        finish_kernel,
+        [((tokens, width), BF16), ((SPLIT, tokens), F32)],
+        4 * tokens * width * cap,
+        4 * tokens * width,
+    )(handed(other, 2), handed(own, 0), next_grad, across(other_comb, 2), own_comb, ids, place)
     return (
         out[None],
         gate_up_out.reshape(1, 1, 2, hidden, width),

time: 43.3 us -> 41.2 us (0.952)
  waiting for transfers between devices: 14.6 us -> 12.3 us
  starting transfers between devices: 15.1 us -> 16.2 us
  Pallas kernels: 12.7 us -> 11.7 us
    ppermute x5, waiting for transfers between devices: 11.9 us -> 9.55 us  [across(): lax.ppermute(block, 'expert', [(i, i ^ 2 * offset) for i in range(devices)])]
    ppermute x5, starting transfers between devices: 6.15 us -> 7.7 us  [across(): lax.ppermute(block, 'expert', [(i, i ^ 2 * offset) for i in range(devices)])]
    pallas_call x1, Pallas kernels: 2.46 us -> 1.52 us  [on_one(): call(finish_kernel, [((tokens, width), BF16), ((SPLIT, tokens), F32)], 4...]
    ppermute x3, starting transfers between devices: 8.11 us -> 7.67 us  [handed(): return lax.ppermute(block, ('pipe', 'expert'), route)]
  transfers between devices with their start and end apart: 13 -> 13, of which waited for: 6 -> 6; matrix products, arithmetic and copies ran while one was open for 0% -> 0% of each run, Pallas kernels for 24% -> 20%
where the time goes in v5:
time: 41.2 us; the launch traced here: 41 us
  starting transfers between devices  16.2 us (39%)
  waiting for transfers between devices  12.3 us (30%)
  Pallas kernels  11.7 us (28%)
  between operations  0.72 us (2%)
    ppermute x5, waiting for transfers between devices, across(): lax.ppermute(block, 'expert', [(i, i ^ 2 * offset) for i in range(devices)])  9.55 us
    ppermute x5, starting transfers between devices, across(): lax.ppermute(block, 'expert', [(i, i ^ 2 * offset) for i in range(devices)])  7.7 us
    ppermute x3, starting transfers between devices, handed(): return lax.ppermute(block, ('pipe', 'expert'), route)  7.67 us
    pallas_call x1, Pallas kernels, weight_grads(): pl.pallas_call(weights_kernel, grid=(width // chunk,), in_specs=[IN_VMEM,...  3.18 us
    ppermute x5, waiting for transfers between devices, beside(): return lax.ppermute(block, 'expert', [(i, i ^ 1) for i in range(devices)])  2.73 us
    pallas_call x1, Pallas kernels, on_one(): call(fetch_kernel, [(slab.shape, BF16), (down.shape, BF16), (rows.shape,...  2.37 us
    pallas_call x1, Pallas kernels, on_one(): call(hidden_kernel, [((total_rows // 2, wide), BF16), ((total_rows // 2,...  2.37 us
    pallas_call x1, Pallas kernels, on_one(): call(rows_kernel, [((2 * cap, wide), BF16), ((cap, width), F32), ((cap, t...  2 us
  transfers between devices with their start and end apart: 13, of which 6 were waited for; matrix products, arithmetic and copies ran while one was open for 0% of the time, Pallas kernels for 20%

profile of v5, /device:TPU:0, one launch (start us, length us, event | category | flops | bytes accessed | tf_op | source)
XLA Modules:
  0.0 41.0 jit_solution(6454834233722701260)
XLA Ops:
  0.6 2.0 %shard_map.102 = (bf16[16,4224]{1,0:T(8,128)(2,1)S(1)}, f32[8,4096]{1,0:T(8,128)S(1)}, f32[8,128]{1,0:T(8,128)S(1)}) custom-call(s32[8,128]{1,0:T(8,128)} %bitcast.16, bf16[8,128]{1,0:T(8,128)(2,1)} %bitcast.22, f32[1,4096]{1,0:T(1,128)} %gain_ref.1, bf16[128,4096]{1,0:T(8,128)(2,1)} %bitcast.19, bf16[128,4096]{1,0:T(8,128)(2,1)} %bitcast.20), custom_call_target="tpu_custom_call" | custom-call | flops 16777216 | bytes 2097152 | tf_op jit(solution)/shard_map/pallas_call | solution.py:390
  2.6 4.1 %collective-permute-start = (bf16[16,4224]{1,0:T(8,128)(2,1)S(1)}, bf16[16,4224]{1,0:T(8,128)(2,1)S(1)}, u32[]{:S(2)}, u32[]{:S(2)}) collective-permute-start(bf16[16,4224]{1,0:T(8,128)(2,1)S(1)} %get-tuple-element.25.rows_ref.refs_0_), channel_id=1, source_target_pairs={{0,4},{1,5},{2,6},{3,7},{4,0},{5,1},{6,2},{7,3},{8,12},{9,13},{10,... | collective-permute-start | bytes 405512 | tf_op jit(solution)/shard_map/ppermute | solution.py:376
  6.7 1.6 %collective-permute-start.1 = (bf16[16,4224]{1,0:T(8,128)(2,1)S(1)}, bf16[16,4224]{1,0:T(8,128)(2,1)S(1)}, u32[]{:S(2)}, u32[]{:S(2)}) collective-permute-start(bf16[16,4224]{1,0:T(8,128)(2,1)S(1)} %get-tuple-element.25.rows_ref.refs_0_), channel_id=1, source_target_pairs={{0,2},{1,3},{2,0},{3,1},{4,6},{5,7},{6,4},{7,5},{8,10},{9,11},{10,... | collective-permute-start | bytes 405512 | tf_op jit(solution)/shard_map/ppermute | solution.py:376
  8.3 2.4 %collective-permute-start.11 = (bf16[128,4096]{1,0:T(8,128)(2,1)}, bf16[128,4096]{1,0:T(8,128)(2,1)S(1)}, u32[]{:S(2)}, u32[]{:S(2)}) collective-permute-start(bf16[128,4096]{1,0:T(8,128)(2,1)} %bitcast.21), channel_id=1, source_target_pairs={{8,0},{9,1},{10,2},{11,3},{12,4},{13,5},{14,6},{15,7},{16,8},{17,9... | collective-permute-start | bytes 3145736 | tf_op jit(solution)/shard_map/ppermute | solution.py:387
  10.8 2.6 %collective-permute-done.refs_1_.far_ref = bf16[16,4224]{1,0:T(8,128)(2,1)S(1)} collective-permute-done((bf16[16,4224]{1,0:T(8,128)(2,1)S(1)}, bf16[16,4224]{1,0:T(8,128)(2,1)S(1)}, u32[]{:S(2)}, u32[]{:S(2)}) %collective-permute-start) | collective-permute-done | bytes 135200 | tf_op jit(solution)/shard_map/ppermute | solution.py:376
  13.3 0.6 %collective-permute-start.2 = (bf16[16,4224]{1,0:T(8,128)(2,1)S(1)}, bf16[16,4224]{1,0:T(8,128)(2,1)S(1)}, u32[]{:S(2)}, u32[]{:S(2)}) collective-permute-start(bf16[16,4224]{1,0:T(8,128)(2,1)S(1)} %collective-permute-done.refs_1_.far_ref), channel_id=1, source_target_pairs={{0,2},{1,3},{2,0},{3,1},{4,6},{5,7},{6,4},{7,5},{8,10},{9,11},{10,... | collective-permute-start | bytes 405512 | tf_op jit(solution)/shard_map/ppermute | solution.py:376
  13.9 2.4 %shard_map.103 = (bf16[384,4096]{1,0:T(8,128)(2,1)S(1)}, bf16[192,4096]{1,0:T(8,128)(2,1)S(1)}, bf16[16,4224]{1,0:T(8,128)(2,1)S(1)}) custom-call(bf16[384,4096]{1,0:T(8,128)(2,1)} %bitcast.23, bf16[192,4096]{1,0:T(8,128)(2,1)} %bitcast.24, bf16[16,4224]{1,0:T(8,128)(2,1)S(1)} %get-tuple-element.25.rows_ref.refs_0_), custom_call_target="tpu_custom_call" | custom-call | flops 30000001024 | bytes 4718592 | tf_op jit(solution)/shard_map/pallas_call | solution.py:408
  16.3 0.1 collective-permute-start.3
  16.4 0.5 %collective-permute-start.4 = (bf16[16,4224]{1,0:T(8,128)(2,1)S(1)}, bf16[16,4224]{1,0:T(8,128)(2,1)S(1)}, u32[]{:S(2)}, u32[]{:S(2)}) collective-permute-start(bf16[16,4224]{1,0:T(8,128)(2,1)S(1)} %collective-permute-done.refs_1_.far_ref), channel_id=1, source_target_pairs={{0,1},{1,0},{2,3},{3,2},{4,5},{5,4},{6,7},{7,6},{8,9},{9,8},{10,11... | collective-permute-start | bytes 405512 | tf_op jit(solution)/shard_map/ppermute | solution.py:379
  16.9 0.0 collective-permute-done.1.refs_2_
  16.9 0.1 collective-permute-start.5
  17.0 1.4 %collective-permute-done.2.refs_3_ = bf16[16,4224]{1,0:T(8,128)(2,1)S(1)} collective-permute-done((bf16[16,4224]{1,0:T(8,128)(2,1)S(1)}, bf16[16,4224]{1,0:T(8,128)(2,1)S(1)}, u32[]{:S(2)}, u32[]{:S(2)}) %collective-permute-start.2) | collective-permute-done | bytes 135200 | tf_op jit(solution)/shard_map/ppermute | solution.py:376
  18.3 0.0 collective-permute-start.6
  18.3 0.0 collective-permute-done.3.refs_4_
  18.3 0.0 collective-permute-done.4.refs_5_
  18.3 0.0 collective-permute-done.5.refs_6_
  18.4 1.3 %collective-permute-done.6.refs_7_ = bf16[16,4224]{1,0:T(8,128)(2,1)S(1)} collective-permute-done((bf16[16,4224]{1,0:T(8,128)(2,1)S(1)}, bf16[16,4224]{1,0:T(8,128)(2,1)S(1)}, u32[]{:S(2)}, u32[]{:S(2)}) %collective-permute-start.6) | collective-permute-done | bytes 135200 | tf_op jit(solution)/shard_map/ppermute | solution.py:379
  19.7 2.4 %shard_map.104 = (bf16[32,4224]{1,0:T(8,128)(2,1)S(1)}, bf16[32,4224]{1,0:T(8,128)(2,1)S(1)}, bf16[128,4096]{1,0:T(8,128)(2,1)S(1)}, bf16[384,128]{1,0:T(8,128)(2,1)S(1)}, bf16[192,128]{1,0:T(8,128)(2,1)S(1)}) custom-call(bf16[16,4224]{1,0:T(8,128)(2,1)S(1)} %get-tuple-element.25.rows_ref.refs_0_, bf16[16,4224]{1,0:T(8,128)(2,1)S(1)} %collective-permute-done.refs_1_.far_ref, ...), custom_call_target="tpu_custom_call" | custom-call | flops 503316480 | bytes 4718592 | tf_op jit(solution)/shard_map/pallas_call | solution.py:418
  22.1 0.0 copy-start.1
  22.1 0.2 collective-permute-start.7
  22.3 1.4 %collective-permute-done.7.got_ref = bf16[32,4224]{1,0:T(8,128)(2,1)S(1)} collective-permute-done((bf16[32,4224]{1,0:T(8,128)(2,1)S(1)}, bf16[32,4224]{1,0:T(8,128)(2,1)S(1)}, u32[]{:S(2)}, u32[]{:S(2)}) %collective-permute-start.7) | collective-permute-done | bytes 270368 | tf_op jit(solution)/shard_map/ppermute | solution.py:379
  23.7 0.1 shard_map.105
  23.8 1.2 %collective-permute-start.8 = (bf16[16,4224]{1,0:T(8,128)(2,1)S(1)}, bf16[16,4224]{1,0:T(8,128)(2,1)S(1)}, u32[]{:S(2)}, u32[]{:S(2)}) collective-permute-start(bf16[16,4224]{1,0:T(8,128)(2,1)S(1)} %get-tuple-element.32), channel_id=1, source_target_pairs={{0,2},{1,3},{2,0},{3,1},{4,6},{5,7},{6,4},{7,5},{8,10},{9,11},{10,... | collective-permute-start | bytes 405512 | tf_op jit(solution)/shard_map/ppermute | solution.py:376
  24.9 3.2 %shard_map.106 = (bf16[384,4096]{1,0:T(8,128)(2,1)}, bf16[192,4096]{1,0:T(8,128)(2,1)}) custom-call(bf16[128,4096]{1,0:T(8,128)(2,1)S(1)} %get-tuple-element.34.rows_ref, bf16[384,128]{1,0:T(8,128)(2,1)S(1)} %get-tuple-element.35.both_ref, bf16[192,128]{1,0:T(8,128)(2,1)S(1)} %get-tuple-element.36.act_ref, ...), custom_call_target="tpu_custom_call" | custom-call | flops 603979776 | bytes 4718592 | tf_op jit(solution)/shard_map/pallas_call | solution.py:326
  28.1 1.3 %collective-permute-done.8.got_ref = bf16[16,4224]{1,0:T(8,128)(2,1)S(1)} collective-permute-done((bf16[16,4224]{1,0:T(8,128)(2,1)S(1)}, bf16[16,4224]{1,0:T(8,128)(2,1)S(1)}, u32[]{:S(2)}, u32[]{:S(2)}) %collective-permute-start.8) | collective-permute-done | bytes 135200 | tf_op jit(solution)/shard_map/ppermute | solution.py:376
  29.5 0.2 shard_map.107
  29.7 4.7 %collective-permute-start.9 = (bf16[8,4224]{1,0:T(8,128)(2,1)S(1)}, bf16[8,4224]{1,0:T(8,128)(2,1)S(1)}, u32[]{:S(2)}, u32[]{:S(2)}) collective-permute-start(bf16[8,4224]{1,0:T(8,128)(2,1)S(1)} %get-tuple-element.38), channel_id=1, source_target_pairs={{8,4},{9,5},{10,6},{11,7},{12,0},{13,1},{14,2},{15,3},{16,12},{17,... | collective-permute-start | bytes 202760 | tf_op jit(solution)/shard_map/ppermute | solution.py:387
  34.4 0.5 %collective-permute-start.10 = (bf16[8,4096]{1,0:T(8,128)(2,1)S(1)}, bf16[8,4096]{1,0:T(8,128)(2,1)S(1)}, u32[]{:S(2)}, u32[]{:S(2)}) collective-permute-start(bf16[8,4096]{1,0:T(8,128)(2,1)S(1)} %get-tuple-element.39), channel_id=1, source_target_pairs={{8,0},{9,1},{10,2},{11,3},{12,4},{13,5},{14,6},{15,7},{16,8},{17,9... | collective-permute-start | bytes 196616 | tf_op jit(solution)/shard_map/ppermute | solution.py:387
  34.9 0.2 collective-permute-start.12
  35.2 4.3 %collective-permute-done.12.other_comb_ref = f32[8,128]{1,0:T(8,128)S(1)} collective-permute-done((f32[8,128]{1,0:T(8,128)S(1)}, f32[8,128]{1,0:T(8,128)S(1)}, u32[]{:S(2)}, u32[]{:S(2)}) %collective-permute-start.12) | collective-permute-done | bytes 4128 | tf_op jit(solution)/shard_map/ppermute | solution.py:376
  39.4 0.0 collective-permute-done.11.grad_ref
  39.5 1.5 %shard_map.108 = (bf16[128,4096]{1,0:T(8,128)(2,1)}, f32[8,128]{1,0:T(8,128)}) custom-call(bf16[8,4224]{1,0:T(8,128)(2,1)S(1)} %collective-permute-done.9.other_ref, bf16[8,4096]{1,0:T(8,128)(2,1)S(1)} %collective-permute-done.10.own_ref, bf16[128,4096]{1,0:T(8,128)(2,1)S(1)} %collective-permute-done.11.grad_ref, ...), custom_call_target="tpu_custom_call" | custom-call | flops 16777216 | bytes 2097152 | tf_op jit(solution)/shard_map/pallas_call | solution.py:441
  (5 shorter events, 0.0 us)
Async XLA Ops:
  2.6 10.7 %collective-permute-start = (bf16[16,4224]{1,0:T(8,128)(2,1)S(1)}, bf16[16,4224]{1,0:T(8,128)(2,1)S(1)}, u32[]{:S(2)}, u32[]{:S(2)}) collective-permute-start(bf16[16,4224]{1,0:T(8,128)(2,1)S(1)} %get-tuple-element.25.rows_ref.refs_0_), channel_id=1, source_target_pairs={{0,4},{1,5},{2,6},{3,7},{4,0},{5,1},{6,2},{7,3},{8,12},{9,13},{10,... | collective-permute-start | bytes 405512 | tf_op jit(solution)/shard_map/ppermute | solution.py:376
  6.7 10.2 %collective-permute-start.1 = (bf16[16,4224]{1,0:T(8,128)(2,1)S(1)}, bf16[16,4224]{1,0:T(8,128)(2,1)S(1)}, u32[]{:S(2)}, u32[]{:S(2)}) collective-permute-start(bf16[16,4224]{1,0:T(8,128)(2,1)S(1)} %get-tuple-element.25.rows_ref.refs_0_), channel_id=1, source_target_pairs={{0,2},{1,3},{2,0},{3,1},{4,6},{5,7},{6,4},{7,5},{8,10},{9,11},{10,... | collective-permute-start | bytes 405512 | tf_op jit(solution)/shard_map/ppermute | solution.py:376
  8.3 31.1 %collective-permute-start.11 = (bf16[128,4096]{1,0:T(8,128)(2,1)}, bf16[128,4096]{1,0:T(8,128)(2,1)S(1)}, u32[]{:S(2)}, u32[]{:S(2)}) collective-permute-start(bf16[128,4096]{1,0:T(8,128)(2,1)} %bitcast.21), channel_id=1, source_target_pairs={{8,0},{9,1},{10,2},{11,3},{12,4},{13,5},{14,6},{15,7},{16,8},{17,9... | collective-permute-start | bytes 3145736 | tf_op jit(solution)/shard_map/ppermute | solution.py:387
  13.3 5.0 %collective-permute-start.2 = (bf16[16,4224]{1,0:T(8,128)(2,1)S(1)}, bf16[16,4224]{1,0:T(8,128)(2,1)S(1)}, u32[]{:S(2)}, u32[]{:S(2)}) collective-permute-start(bf16[16,4224]{1,0:T(8,128)(2,1)S(1)} %collective-permute-done.refs_1_.far_ref), channel_id=1, source_target_pairs={{0,2},{1,3},{2,0},{3,1},{4,6},{5,7},{6,4},{7,5},{8,10},{9,11},{10,... | collective-permute-start | bytes 405512 | tf_op jit(solution)/shard_map/ppermute | solution.py:376
  16.3 2.0 %collective-permute-start.3 = (bf16[16,4224]{1,0:T(8,128)(2,1)S(1)}, bf16[16,4224]{1,0:T(8,128)(2,1)S(1)}, u32[]{:S(2)}, u32[]{:S(2)}) collective-permute-start(bf16[16,4224]{1,0:T(8,128)(2,1)S(1)} %get-tuple-element.26), channel_id=1, source_target_pairs={{0,1},{1,0},{2,3},{3,2},{4,5},{5,4},{6,7},{7,6},{8,9},{9,8},{10,11... | collective-permute-start | bytes 405512 | tf_op jit(solution)/shard_map/ppermute | solution.py:379
  16.4 1.9 %collective-permute-start.4 = (bf16[16,4224]{1,0:T(8,128)(2,1)S(1)}, bf16[16,4224]{1,0:T(8,128)(2,1)S(1)}, u32[]{:S(2)}, u32[]{:S(2)}) collective-permute-start(bf16[16,4224]{1,0:T(8,128)(2,1)S(1)} %collective-permute-done.refs_1_.far_ref), channel_id=1, source_target_pairs={{0,1},{1,0},{2,3},{3,2},{4,5},{5,4},{6,7},{7,6},{8,9},{9,8},{10,11... | collective-permute-start | bytes 405512 | tf_op jit(solution)/shard_map/ppermute | solution.py:379
  16.9 1.5 %collective-permute-start.5 = (bf16[16,4224]{1,0:T(8,128)(2,1)S(1)}, bf16[16,4224]{1,0:T(8,128)(2,1)S(1)}, u32[]{:S(2)}, u32[]{:S(2)}) collective-permute-start(bf16[16,4224]{1,0:T(8,128)(2,1)S(1)} %collective-permute-done.1.refs_2_), channel_id=1, source_target_pairs={{0,1},{1,0},{2,3},{3,2},{4,5},{5,4},{6,7},{7,6},{8,9},{9,8},{10,11... | collective-permute-start | bytes 405512 | tf_op jit(solution)/shard_map/ppermute | solution.py:379
  18.3 1.4 %collective-permute-start.6 = (bf16[16,4224]{1,0:T(8,128)(2,1)S(1)}, bf16[16,4224]{1,0:T(8,128)(2,1)S(1)}, u32[]{:S(2)}, u32[]{:S(2)}) collective-permute-start(bf16[16,4224]{1,0:T(8,128)(2,1)S(1)} %collective-permute-done.2.refs_3_), channel_id=1, source_target_pairs={{0,1},{1,0},{2,3},{3,2},{4,5},{5,4},{6,7},{7,6},{8,9},{9,8},{10,11... | collective-permute-start | bytes 405512 | tf_op jit(solution)/shard_map/ppermute | solution.py:379
  19.7 9.8 %copy-start = (f32[1,4096]{1,0:T(1,128)S(1)}, f32[1,4096]{1,0:T(1,128)}, u32[]{:S(2)}) copy-start(f32[1,4096]{1,0:T(1,128)} %gain_ref.1) | copy-start | bytes 49156
  22.1 17.4 %copy-start.1 = (s32[1,128,8]{1,2,0:T(8,128)S(1)}, s32[1,128,8]{1,2,0:T(8,128)}, u32[]{:S(2)}) copy-start(s32[1,128,8]{1,2,0:T(8,128)} %param.9) | copy-start | bytes 12292
  22.1 1.6 %collective-permute-start.7 = (bf16[32,4224]{1,0:T(8,128)(2,1)S(1)}, bf16[32,4224]{1,0:T(8,128)(2,1)S(1)}, u32[]{:S(2)}, u32[]{:S(2)}) collective-permute-start(bf16[32,4224]{1,0:T(8,128)(2,1)S(1)} %get-tuple-element.30), channel_id=1, source_target_pairs={{0,1},{1,0},{2,3},{3,2},{4,5},{5,4},{6,7},{7,6},{8,9},{9,8},{10,11... | collective-permute-start | bytes 811016 | tf_op jit(solution)/shard_map/ppermute | solution.py:379
  23.8 5.7 %collective-permute-start.8 = (bf16[16,4224]{1,0:T(8,128)(2,1)S(1)}, bf16[16,4224]{1,0:T(8,128)(2,1)S(1)}, u32[]{:S(2)}, u32[]{:S(2)}) collective-permute-start(bf16[16,4224]{1,0:T(8,128)(2,1)S(1)} %get-tuple-element.32), channel_id=1, source_target_pairs={{0,2},{1,3},{2,0},{3,1},{4,6},{5,7},{6,4},{7,5},{8,10},{9,11},{10,... | collective-permute-start | bytes 405512 | tf_op jit(solution)/shard_map/ppermute | solution.py:376
  29.7 9.7 %collective-permute-start.9 = (bf16[8,4224]{1,0:T(8,128)(2,1)S(1)}, bf16[8,4224]{1,0:T(8,128)(2,1)S(1)}, u32[]{:S(2)}, u32[]{:S(2)}) collective-permute-start(bf16[8,4224]{1,0:T(8,128)(2,1)S(1)} %get-tuple-element.38), channel_id=1, source_target_pairs={{8,4},{9,5},{10,6},{11,7},{12,0},{13,1},{14,2},{15,3},{16,12},{17,... | collective-permute-start | bytes 202760 | tf_op jit(solution)/shard_map/ppermute | solution.py:387
  34.4 5.0 %collective-permute-start.10 = (bf16[8,4096]{1,0:T(8,128)(2,1)S(1)}, bf16[8,4096]{1,0:T(8,128)(2,1)S(1)}, u32[]{:S(2)}, u32[]{:S(2)}) collective-permute-start(bf16[8,4096]{1,0:T(8,128)(2,1)S(1)} %get-tuple-element.39), channel_id=1, source_target_pairs={{8,0},{9,1},{10,2},{11,3},{12,4},{13,5},{14,6},{15,7},{16,8},{17,9... | collective-permute-start | bytes 196616 | tf_op jit(solution)/shard_map/ppermute | solution.py:387
  34.9 4.5 %collective-permute-start.12 = (f32[8,128]{1,0:T(8,128)S(1)}, f32[8,128]{1,0:T(8,128)S(1)}, u32[]{:S(2)}, u32[]{:S(2)}) collective-permute-start(f32[8,128]{1,0:T(8,128)S(1)} %get-tuple-element.40), channel_id=1, source_target_pairs={{0,4},{1,5},{2,6},{3,7},{4,0},{5,1},{6,2},{7,3},{8,12},{9,13},{10,... | collective-permute-start | bytes 12296 | tf_op jit(solution)/shard_map/ppermute | solution.py:376

commit v6 on v5

--- a/solution.py
+++ b/solution.py
@@ -151,6 +151,8 @@
     )
 
 
+FETCH_FLOPS = 1_000_000_000
+HIDDEN_FLOPS = 6_400_000_000
 IN_HBM = pl.BlockSpec(memory_space=pltpu.HBM)
 IN_VMEM = pl.BlockSpec(memory_space=pltpu.VMEM)
 
@@ -170,8 +172,8 @@
     return high, middle, values - high - middle
 
 
-def rows_kernel(ids_hbm, weight_hbm, gain_hbm, hidden_hbm, grad_hbm, rows_ref, normed_ref, place_ref,
-                ids_ref, weight_ref, gain_ref, hidden_ref, grad_ref, sems):
+def rows_kernel(ids_hbm, weight_hbm, gain_hbm, hidden_hbm, grad_hbm, in_ref, out_ref, both_ref,
+                normed_ref, place_ref, ids_ref, weight_ref, gain_ref, hidden_ref, grad_ref, sems):
     tokens, width = hidden_ref.shape
     cap = SPECIALIST_CAP
     copies = [
@@ -202,6 +204,7 @@
     normed_ref[...] = normed
     copies[2].wait()
     normed_in = normed * gain_ref[...]
+    in_ref[:, :width] = normed_in.astype(BF16)
     copies[3].wait()
     weight = jnp.sum(
         jnp.where(hit, weight_ref[...].astype(F32), 0.0), axis=0, keepdims=True
@@ -211,98 +214,108 @@
     extra = jnp.broadcast_to(taken, (cap, LANES))
     for number, part in enumerate(in_parts(rms)):
         extra = jnp.where(lane == number + 1, part, extra)
-    rows_ref[:, width:] = jnp.concatenate([extra, place], axis=0).astype(BF16)
+    in_ref[:, width:] = extra.astype(BF16)
+    out_ref[:, width:] = place.astype(BF16)
+    both_ref[:, width:] = jnp.concatenate([extra, place], axis=0).astype(BF16)
     copies[4].wait()
     grad = take_rows(place.astype(BF16), grad_ref[...])
-    rows_ref[:, :width] = jnp.concatenate([normed_in, grad], axis=0).astype(BF16)
-
-
-def fetch_kernel(slab_hbm, down_hbm, rows_ref, slab_ref, down_ref, again_ref, sems):
+    out_ref[:, :width] = grad.astype(BF16)
+    both_ref[:, :width] = jnp.concatenate([normed_in, grad], axis=0).astype(BF16)
+
+
+def fetch_kernel(slab_hbm, down_hbm, after_ref, slab_ref, down_ref, sems):
+    del after_ref
     first = pltpu.make_async_copy(slab_hbm, slab_ref, sems.at[0])
     second = pltpu.make_async_copy(down_hbm, down_ref, sems.at[1])
     first.start()
     second.start()
-    again_ref[...] = rows_ref[...]
     first.wait()
     second.wait()
 
 
-def halves(rows, cap):
-    blocks = range(rows.shape[0] // (2 * cap))
-    return [
-        jnp.concatenate([rows[(2 * b + h) * cap : (2 * b + h + 1) * cap] for b in blocks], axis=0)
-        for h in (0, 1)
-    ]
-
-
-def padded(rows, half, cap):
-    blank = jnp.zeros((cap, rows.shape[1]), rows.dtype)
+def pass_kernel(block_ref, *refs):
+    *after_refs, out_ref = refs
+    del after_refs
+    out_ref[...] = block_ref[...]
+
+
+def stacked(refs, half, start, stop):
+    cap = SPECIALIST_CAP
     pieces = []
-    for b in range(rows.shape[0] // cap):
-        own = rows[b * cap : (b + 1) * cap]
-        pieces += [own, blank] if half == 0 else [blank, own]
+    for ref in refs:
+        block = ref[:, start:stop].astype(F32)
+        pieces.append(block if ref.shape[0] == cap else block[half * cap : (half + 1) * cap])
     return jnp.concatenate(pieces, axis=0)
 
 
+def project_kernel(*refs):
+    *blocks, slab_ref, slab_two_ref, pre_ref, pre_two_ref, first_ref, last_ref = refs
+    width = slab_ref.shape[1]
+    rows = stacked(blocks, 0, 0, width).astype(BF16)
+    half = first_ref.shape[0]
+    pre_ref[...] = rows_product(rows, slab_ref[...])
+    pre_two_ref[...] = rows_product(rows, slab_two_ref[...])
+    first_ref[...] = rows[:half]
+    last_ref[...] = rows[half:]
+
+
 def hidden_kernel(*refs):
-    *blocks, slab_ref, down_ref, keep_ref, send_ref, rows_ref, both_ref, act_ref = refs
+    in_blocks, blocks, refs = refs[:4], refs[4:8], refs[8:]
+    pre_ref, pre_two_ref, slab_ref, down_ref, slab_two_ref, down_two_ref, *refs = refs
+    own_ref, other_ref, first_ref, last_ref, keep_ref, send_ref = refs
     hidden, width = down_ref.shape
-    half = keep_ref.shape[0]
-    cap = SPECIALIST_CAP
-    rows = jnp.concatenate([r[:, :width] for r in blocks], axis=0)
-    rows_ref[...] = rows
-    pre, _ = halves(rows_product(rows, slab_ref[...]), cap)
-    _, back = halves(rows_product(rows, down_ref[...]), cap)
-    weight = jnp.concatenate([r[:, width:].astype(F32)[:cap, :1] for r in blocks], axis=0)
-    gate = pre[:, :hidden]
-    up = pre[:, hidden:]
-    sig = jax.nn.sigmoid(gate)
-    active = gate * sig
-    act = active * up
-    into = weight * back
-    both = jnp.concatenate(
-        [into * up * sig * (1.0 + gate * (1.0 - sig)), into * active], axis=1
-    )
-    part = take_rows(both.astype(BF16), slab_ref[...]).astype(BF16)
-    send_ref[:, :width] = part[half:]
-    keep_ref[:, :width] = part[:half]
-    comb = jnp.sum(act * back, axis=1, keepdims=True)
-    comb = jnp.broadcast_to(comb, (2 * half, LANES)).astype(BF16)
-    send_ref[:, width:] = comb[half:]
-    keep_ref[:, width:] = comb[:half]
-    both_ref[...] = padded(both, 0, cap).T.astype(BF16)
-    act_ref[...] = padded(weight * act, 1, cap).T.astype(BF16)
-
-
-def halve_kernel(keep_ref, got_ref, own_ref, other_ref):
-    total = keep_ref[...].astype(F32) + got_ref[...].astype(F32)
     half = own_ref.shape[0]
-    width = own_ref.shape[1] - LANES
-    other_ref[:, :width] = total[half:, :width].astype(BF16)
-    own_ref[:, :width] = total[:half, :width].astype(BF16)
-    comb = total[:, width:]
+    rows = stacked(blocks, 1, 0, width).astype(BF16)
+    weight = stacked(in_blocks, 0, width, width + LANES)[:, :1]
+    total, comb = 0.0, 0.0
+    for slab, down, pre, left_ref in (
+        (slab_ref[...], down_ref[...], pre_ref[...], keep_ref),
+        (slab_two_ref[...], down_two_ref[...], pre_two_ref[...], send_ref),
+    ):
+        back = rows_product(rows, down)
+        gate = pre[:, :hidden]
+        up = pre[:, hidden:]
+        sig = jax.nn.sigmoid(gate)
+        active = gate * sig
+        act = active * up
+        into = weight * back
+        both = jnp.concatenate(
+            [into * up * sig * (1.0 + gate * (1.0 - sig)), into * active], axis=1
+        )
+        total = total + take_rows(both.astype(BF16), slab)
+        part = jnp.sum(act * back, axis=1, keepdims=True)
+        comb = comb + part.astype(BF16).astype(F32)
+        left_ref[:, : 2 * hidden] = both.astype(BF16)
+        left_ref[:, 2 * hidden : 3 * hidden] = (weight * act).astype(BF16)
+        left_ref[:, 3 * hidden :] = jnp.zeros(
+            (left_ref.shape[0], left_ref.shape[1] - 3 * hidden), BF16
+        )
+    other_ref[:, :width] = total[half:].astype(BF16)
+    own_ref[:, :width] = total[:half].astype(BF16)
+    comb = jnp.broadcast_to(comb, (2 * half, LANES))
     high = comb.astype(BF16).astype(F32)
     lane = lax.broadcasted_iota(jnp.int32, comb.shape, 1)
     comb = jnp.where(lane < LANES // 2, high, comb - high).astype(BF16)
     other_ref[:, width:] = comb[half:]
     own_ref[:, width:] = comb[:half]
-
-
-def split_kernel(keep_ref, got_ref, normed_ref, rows_ref, far_ref, gain_ref, after_ref,
+    first_ref[...] = rows[:half]
+    last_ref[...] = rows[half:]
+
+
+def split_kernel(keep_ref, got_ref, normed_ref, in_ref, far_in_ref, far_grad_ref, gain_ref,
                  own_ref, other_ref, own_comb_ref, other_comb_ref):
-    del after_ref
     cap, width = own_ref.shape
     total = keep_ref[...].astype(F32) + got_ref[...].astype(F32)
     gain = gain_ref[...]
-    far = far_ref[...].astype(F32)
-    extra = jnp.concatenate([rows_ref[:, width:].astype(F32)[:cap], far[:cap, width:]], axis=0)
+    far = far_in_ref[...].astype(F32)
+    extra = jnp.concatenate([in_ref[:, width:].astype(F32), far[:, width:]], axis=0)
     rms = extra[:, 1:2] + extra[:, 2:3] + extra[:, 3:4]
-    normed = jnp.concatenate([normed_ref[...], far[:cap, :width] / gain], axis=0)
+    normed = jnp.concatenate([normed_ref[...], far[:, :width] / gain], axis=0)
     scaled = total[:, :width] * gain
     inner = jnp.mean(scaled * normed, axis=-1, keepdims=True)
     change = (scaled - normed * inner) / rms
     other_ref[:, :width] = change[cap:].astype(BF16)
-    other_ref[:, width:] = far[cap:, width:].astype(BF16)
+    other_ref[:, width:] = far_grad_ref[:, width:]
     own_ref[...] = change[:cap].astype(BF16)
     comb = total[:, width:]
     comb = comb + pltpu.roll(comb, LANES // 2, 1)
@@ -310,35 +323,52 @@
     own_comb_ref[...] = comb[:cap]
 
 
-def weights_kernel(rows_ref, both_ref, act_ref, after_ref, both_out, act_out):
+def weights_kernel(chunks, *refs):
+    ins, grads, refs = refs[:4], refs[4:8], refs[8:]
+    keep_ref, got_ref, after_ref, both_hbm, act_hbm, both_ref, act_ref, sems = refs
     del after_ref
-    chunk = both_out.shape[1]
-    rows = rows_ref[:, pl.ds(pl.multiple_of(pl.program_id(0) * chunk, chunk), chunk)]
-    both_out[...] = take_rows(both_ref[...], rows).astype(BF16)
-    act_out[...] = take_rows(act_ref[...], rows).astype(BF16)
-
-
-def weight_grads(rows, both, act, after):
-    width = rows.shape[1]
-    hidden = act.shape[0]
-    chunk = min(width, 1024)
-    across = lambda count: pl.BlockSpec((count, chunk), lambda i: (0, i))
+    hidden, width = act_ref.shape
+    left = jnp.concatenate([keep_ref[...], got_ref[...]], axis=0).astype(F32).T
+    both = left[: 2 * hidden].astype(BF16)
+    act = left[2 * hidden : 3 * hidden].astype(BF16)
+    chunk = width // chunks
+    copies = []
+    for number in range(chunks):
+        columns = slice(number * chunk, (number + 1) * chunk)
+        for which, (left_rows, blocks, ref, hbm) in enumerate(
+            ((both, ins, both_ref, both_hbm), (act, grads, act_ref, act_hbm))
+        ):
+            rows = jnp.concatenate([r[:, columns] for r in blocks], axis=0)
+            ref[:, columns] = take_rows(left_rows, rows).astype(BF16)
+            copy = pltpu.make_async_copy(
+                ref.at[:, columns], hbm.at[:, columns], sems.at[2 * number + which]
+            )
+            copy.start()
+            copies.append(copy)
+    for copy in copies:
+        copy.wait()
+
+
+def weight_grads(blocks, keep, got, after, hidden, width):
+    chunks = 4
     return pl.pallas_call(
-        weights_kernel,
-        grid=(width // chunk,),
-        in_specs=[IN_VMEM, IN_VMEM, IN_VMEM, pl.BlockSpec(memory_space=pl.ANY)],
-        out_specs=[across(2 * hidden), across(hidden)],
+        functools.partial(weights_kernel, chunks),
+        in_specs=[IN_VMEM] * (len(blocks) + 2) + [pl.BlockSpec(memory_space=pl.ANY)],
+        out_specs=[IN_HBM] * 2,
         out_shape=[
             jax.ShapeDtypeStruct((2 * hidden, width), BF16),
             jax.ShapeDtypeStruct((hidden, width), BF16),
         ],
+        scratch_shapes=[
+            pltpu.VMEM((2 * hidden, width), BF16),
+            pltpu.VMEM((hidden, width), BF16),
+            pltpu.SemaphoreType.DMA((2 * chunks,)),
+        ],
         compiler_params=pltpu.CompilerParams(vmem_limit_bytes=24 << 20),
         cost_estimate=pl.CostEstimate(
-            flops=6 * rows.shape[0] * hidden * width,
-            bytes_accessed=6 * hidden * width,
-            transcendentals=0,
+            flops=6 * 64 * hidden * width, bytes_accessed=6 * hidden * width, transcendentals=0
         ),
-    )(rows, both, act, after)
+    )(*blocks, keep, got, after)
 
 
 def finish_kernel(other_ref, own_ref, grad_ref, other_comb_ref, own_comb_ref, ids_ref, place_ref,
@@ -387,9 +417,10 @@
         return lax.ppermute(block, ("pipe", "expert"), route)
 
     next_grad = handed(out_grad[0], 0)
-    rows, normed, place = call(
+    row_in, row_grad, row_both, normed, place = call(
         rows_kernel,
-        [((2 * cap, wide), BF16), ((cap, width), F32), ((cap, tokens), F32)],
+        [((cap, wide), BF16)] * 2
+        + [((2 * cap, wide), BF16), ((cap, width), F32), ((cap, tokens), F32)],
         4 * tokens * width * cap,
         4 * tokens * width,
         in_specs=[IN_HBM] * 5,
@@ -402,42 +433,55 @@
             pltpu.SemaphoreType.DMA((5,)),
         ],
     )(*map(in_hbm, (ids, weights, norm_gain, hidden_in[0], out_grad[0])))
-    far = across(rows, 2)
-    near = across(rows, 1)
-    farthest = across(far, 1)
-    slab_near, down_near, rows_again = call(
+    far_in = across(row_in, 2)
+    far_grad = across(row_grad, 2)
+    slab_two, down_two = beside(slab), beside(down)
+    (passed,) = call(
+        pass_kernel,
+        [(row_both.shape, BF16)],
+        0,
+        4 * cap * wide,
+        in_specs=[IN_VMEM] + [pl.BlockSpec(memory_space=pl.ANY)] * 2,
+    )(row_both, slab_two, down_two)
+    near = across(passed, 1)
+    slab_near, down_near = call(
         fetch_kernel,
-        [(slab.shape, BF16), (down.shape, BF16), (rows.shape, BF16)],
-        30_000_000_000,
+        [(slab.shape, BF16), (down.shape, BF16)],
+        FETCH_FLOPS,
         6 * hidden * width,
-        in_specs=[IN_HBM, IN_HBM, IN_VMEM],
+        in_specs=[IN_HBM] * 2 + [pl.BlockSpec(memory_space=pl.ANY)],
         scratch=[pltpu.SemaphoreType.DMA((2,))],
-    )(in_hbm(slab), in_hbm(down), rows)
-    lane = [rows, far, near, farthest]
-    blocks = lane + [beside(b) for b in (rows_again, far, near, farthest)]
-    keep, send, all_rows, both, act = call(
+    )(in_hbm(slab), in_hbm(down), far_grad)
+    farthest_in = across(far_in, 1)
+    farthest_grad = across(far_grad, 1)
+    ins = [row_in, far_in, near, farthest_in]
+    grads = [row_grad, far_grad, near, farthest_grad]
+    half_rows = ((2 * cap, width), BF16)
+    pre, pre_two, *in_halves = call(
+        project_kernel,
+        [((total_rows // 2, 2 * hidden), F32)] * 2 + [half_rows] * 2,
+        0,
+        4 * hidden * width,
+    )(*ins, slab_near, slab_two)
+    left_width = -(-3 * hidden // LANES) * LANES
+    own_half, other_half, *rest = call(
         hidden_kernel,
-        [
-            ((total_rows // 2, wide), BF16),
-            ((total_rows // 2, wide), BF16),
-            ((2 * total_rows, width), BF16),
-            ((2 * hidden, 2 * total_rows), BF16),
-            ((hidden, 2 * total_rows), BF16),
-        ],
-        10 * total_rows * hidden * width,
+        [((2 * cap, wide), BF16)] * 2
+        + [half_rows] * 2
+        + [((total_rows // 2, left_width), BF16)] * 2,
+        HIDDEN_FLOPS,
         6 * hidden * width,
-    )(*blocks, slab_near, down_near)
-    own_half, other_half = call(
-        halve_kernel, [((2 * cap, wide), BF16)] * 2, 4 * cap * width, 16 * cap * width
-    )(keep, beside(send))
-    gate_up_out, down_out = weight_grads(all_rows, both, act, own_half)
+    )(*ins, *grads, pre, pre_two, slab_near, down_near, slab_two, down_two)
+    *grad_halves, left_keep, left_send = rest
     own, other, own_comb, other_comb = call(
         split_kernel,
         [((cap, width), BF16), ((cap, wide), BF16)] + [((cap, LANES), F32)] * 2,
         2 * cap * width,
         8 * cap * width,
-        in_specs=[IN_VMEM] * 6 + [IN_HBM],
-    )(own_half, across(other_half, 1), normed, rows, far, norm_gain, in_hbm(down_out))
+    )(own_half, across(other_half, 1), normed, row_in, far_in, far_grad, norm_gain)
+    blocks = in_halves + [beside(b) for b in in_halves]
+    blocks += grad_halves + [beside(b) for b in grad_halves]
+    gate_up_out, down_out = weight_grads(blocks, left_keep, beside(left_send), own, hidden, width)
     out, combined = call(
         finish_kernel,
         [((tokens, width), BF16), ((SPLIT, tokens), F32)],

time: 41.2 us -> 39.5 us (0.959)
  waiting for transfers between devices: 12.3 us -> 6.67 us
  starting transfers between devices: 16.2 us -> 18.9 us
  Pallas kernels: 11.7 us -> 13 us
    ppermute x5 -> x7, waiting for transfers between devices: 9.55 us -> 5.95 us  [across(): lax.ppermute(block, 'expert', [(i, i ^ 2 * offset) for i in range(devices)])]
    ppermute x5 -> x7, waiting for transfers between devices: 2.73 us -> 0.72 us  [beside(): return lax.ppermute(block, 'expert', [(i, i ^ 1) for i in range(devices)])]
    ppermute x5 -> x7, starting transfers between devices: 7.7 us -> 9.69 us  [across(): lax.ppermute(block, 'expert', [(i, i ^ 2 * offset) for i in range(devices)])]
    pallas_call x5 -> x6, Pallas kernels: 9.99 us -> 11.3 us  [the longest x1 2.65 us: weight_grads(): pl.pallas_call(functools.partial(weights_kernel, chunks), in_specs=[IN_VM...]
    ppermute x5 -> x7, starting transfers between devices: 0.87 us -> 1.28 us  [beside(): return lax.ppermute(block, 'expert', [(i, i ^ 1) for i in range(devices)])]
  transfers between devices with their start and end apart: 13 -> 17, of which waited for: 6 -> 5; matrix products, arithmetic and copies ran while one was open for 0% -> 0% of each run, Pallas kernels for 20% -> 29%
where the time goes in v6:
time: 39.5 us; the launch traced here: 39.4 us
  starting transfers between devices  18.9 us (48%)
  Pallas kernels  13 us (33%)
  waiting for transfers between devices  6.67 us (17%)
  between operations  0.73 us (2%)
    ppermute x7, starting transfers between devices, across(): lax.ppermute(block, 'expert', [(i, i ^ 2 * offset) for i in range(devices)])  9.69 us
    ppermute x3, starting transfers between devices, handed(): return lax.ppermute(block, ('pipe', 'expert'), route)  7.98 us
    ppermute x7, waiting for transfers between devices, across(): lax.ppermute(block, 'expert', [(i, i ^ 2 * offset) for i in range(devices)])  5.95 us
    pallas_call x1, Pallas kernels, weight_grads(): pl.pallas_call(functools.partial(weights_kernel, chunks), in_specs=[IN_VM...  2.65 us
    pallas_call x1, Pallas kernels, on_one(): call(fetch_kernel, [(slab.shape, BF16), (down.shape, BF16)], FETCH_FLOPS,...  2.37 us
    pallas_call x1, Pallas kernels, on_one(): call(hidden_kernel, [((2 * cap, wide), BF16)] * 2 + [half_rows] * 2 + [((...  2.32 us
    pallas_call x1, Pallas kernels, on_one(): call(rows_kernel, [((cap, wide), BF16)] * 2 + [((2 * cap, wide), BF16), (...  2 us
    pallas_call x1, Pallas kernels, on_one(): call(project_kernel, [((total_rows // 2, 2 * hidden), F32)] * 2 + [half_r...  1.93 us
  transfers between devices with their start and end apart: 17, of which 5 were waited for; matrix products, arithmetic and copies ran while one was open for 0% of the time, Pallas kernels for 29%

profile of v6, /device:TPU:0, one launch (start us, length us, event | category | flops | bytes accessed | tf_op | source)
XLA Modules:
  0.0 39.4 jit_solution(8819254203886122507)
XLA Ops:
  0.6 0.5 %collective-permute-start.1 = (bf16[384,4096]{1,0:T(8,128)(2,1)}, bf16[384,4096]{1,0:T(8,128)(2,1)S(1)}, u32[]{:S(2)}, u32[]{:S(2)}) collective-permute-start(bf16[384,4096]{1,0:T(8,128)(2,1)} %bitcast.18), channel_id=1, source_target_pairs={{0,1},{1,0},{2,3},{3,2},{4,5},{5,4},{6,7},{7,6},{8,9},{9,8},{10,11... | collective-permute-start | bytes 9437192 | tf_op jit(solution)/shard_map/ppermute | solution.py:409
  1.1 0.1 collective-permute-start.2
  1.2 2.0 %shard_map.102 = (bf16[8,4224]{1,0:T(8,128)(2,1)S(1)}, bf16[8,4224]{1,0:T(8,128)(2,1)S(1)}, bf16[16,4224]{1,0:T(8,128)(2,1)S(1)}, f32[8,4096]{1,0:T(8,128)S(1)}, f32[8,128]{1,0:T(8,128)S(1)}) custom-call(s32[8,128]{1,0:T(8,128)} %bitcast.16, bf16[8,128]{1,0:T(8,128)(2,1)} %bitcast.25, f32[1,4096]{1,0:T(1,128)} %gain_ref.1, bf16[128,4096]{1,0:T(8,128)(2,1)} %bitcast.22, ...), custom_call_target="tpu_custom_call" | custom-call | flops 16777216 | bytes 2097152 | tf_op jit(solution)/shard_map/pallas_call | solution.py:420
  3.2 4.1 %collective-permute-start = (bf16[8,4224]{1,0:T(8,128)(2,1)S(1)}, bf16[8,4224]{1,0:T(8,128)(2,1)S(1)}, u32[]{:S(2)}, u32[]{:S(2)}) collective-permute-start(bf16[8,4224]{1,0:T(8,128)(2,1)S(1)} %get-tuple-element.29.refs_0_.in_ref), channel_id=1, source_target_pairs={{0,4},{1,5},{2,6},{3,7},{4,0},{5,1},{6,2},{7,3},{8,12},{9,13},{10,... | collective-permute-start | bytes 202760 | tf_op jit(solution)/shard_map/ppermute | solution.py:406
  7.3 0.1 collective-permute-start.5
  7.4 2.7 %collective-permute-start.10 = (bf16[128,4096]{1,0:T(8,128)(2,1)}, bf16[128,4096]{1,0:T(8,128)(2,1)S(1)}, u32[]{:S(2)}, u32[]{:S(2)}) collective-permute-start(bf16[128,4096]{1,0:T(8,128)(2,1)} %bitcast.24), channel_id=1, source_target_pairs={{8,0},{9,1},{10,2},{11,3},{12,4},{13,5},{14,6},{15,7},{16,8},{17,9... | collective-permute-start | bytes 3145736 | tf_op jit(solution)/shard_map/ppermute | solution.py:417
  10.1 1.8 %collective-permute-start.3 = (bf16[16,4224]{1,0:T(8,128)(2,1)S(1)}, bf16[16,4224]{1,0:T(8,128)(2,1)S(1)}, u32[]{:S(2)}, u32[]{:S(2)}) collective-permute-start(bf16[16,4224]{1,0:T(8,128)(2,1)S(1)} %shard_map.103), channel_id=1, source_target_pairs={{0,2},{1,3},{2,0},{3,1},{4,6},{5,7},{6,4},{7,5},{8,10},{9,11},{10,... | collective-permute-start | bytes 405512 | tf_op jit(solution)/shard_map/ppermute | solution.py:406
  11.9 0.0 collective-permute-done.refs_1_.far_in_ref
  11.9 1.5 %collective-permute-start.4 = (bf16[8,4224]{1,0:T(8,128)(2,1)S(1)}, bf16[8,4224]{1,0:T(8,128)(2,1)S(1)}, u32[]{:S(2)}, u32[]{:S(2)}) collective-permute-start(bf16[8,4224]{1,0:T(8,128)(2,1)S(1)} %collective-permute-done.refs_1_.far_in_ref), channel_id=1, source_target_pairs={{0,2},{1,3},{2,0},{3,1},{4,6},{5,7},{6,4},{7,5},{8,10},{9,11},{10,... | collective-permute-start | bytes 202760 | tf_op jit(solution)/shard_map/ppermute | solution.py:406
  13.4 0.8 %collective-permute-done.5.after_ref.refs_5_.far_grad_ref = bf16[8,4224]{1,0:T(8,128)(2,1)S(1)} collective-permute-done((bf16[8,4224]{1,0:T(8,128)(2,1)S(1)}, bf16[8,4224]{1,0:T(8,128)(2,1)S(1)}, u32[]{:S(2)}, u32[]{:S(2)}) %collective-permute-start.5) | collective-permute-done | bytes 67616 | tf_op jit(solution)/shard_map/ppermute | solution.py:406
  14.1 0.6 %collective-permute-start.6 = (bf16[8,4224]{1,0:T(8,128)(2,1)S(1)}, bf16[8,4224]{1,0:T(8,128)(2,1)S(1)}, u32[]{:S(2)}, u32[]{:S(2)}) collective-permute-start(bf16[8,4224]{1,0:T(8,128)(2,1)S(1)} %collective-permute-done.5.after_ref.refs_5_.far_grad_ref), channel_id=1, source_target_pairs={{0,2},{1,3},{2,0},{3,1},{4,6},{5,7},{6,4},{7,5},{8,10},{9,11},{10,... | collective-permute-start | bytes 202760 | tf_op jit(solution)/shard_map/ppermute | solution.py:406
  14.8 2.4 %shard_map.104 = (bf16[384,4096]{1,0:T(8,128)(2,1)S(1)}, bf16[192,4096]{1,0:T(8,128)(2,1)S(1)}) custom-call(bf16[384,4096]{1,0:T(8,128)(2,1)} %bitcast.19, bf16[192,4096]{1,0:T(8,128)(2,1)} %bitcast.21, bf16[8,4224]{1,0:T(8,128)(2,1)S(1)} %collective-permute-done.5.after_ref.refs_5_.far_grad_ref), custom_call_target="tpu_custom_call" | custom-call | flops 1000000000 | bytes 4718592 | tf_op jit(solution)/shard_map/pallas_call | solution.py:447
  17.1 1.3 %collective-permute-done.4.refs_3_ = bf16[8,4224]{1,0:T(8,128)(2,1)S(1)} collective-permute-done((bf16[8,4224]{1,0:T(8,128)(2,1)S(1)}, bf16[8,4224]{1,0:T(8,128)(2,1)S(1)}, u32[]{:S(2)}, u32[]{:S(2)}) %collective-permute-start.4) | collective-permute-done | bytes 67616 | tf_op jit(solution)/shard_map/ppermute | solution.py:406
  18.5 1.9 %shard_map.105 = (f32[32,384]{1,0:T(8,128)S(1)}, f32[32,384]{1,0:T(8,128)S(1)}, bf16[16,4096]{1,0:T(8,128)(2,1)S(1)}, bf16[16,4096]{1,0:T(8,128)(2,1)S(1)}) custom-call(bf16[8,4224]{1,0:T(8,128)(2,1)S(1)} %get-tuple-element.29.refs_0_.in_ref, bf16[8,4224]{1,0:T(8,128)(2,1)S(1)} %collective-permute-done.refs_1_.far_in_ref, ...), custom_call_target="tpu_custom_call" | custom-call | bytes 3145728 | tf_op jit(solution)/shard_map/pallas_call | solution.py:460
  20.4 0.0 collective-permute-done.6.refs_7_
  20.4 0.0 copy-start
  20.4 0.0 copy-start.1
  20.4 2.3 %shard_map.106 = (bf16[16,4224]{1,0:T(8,128)(2,1)S(1)}, bf16[16,4224]{1,0:T(8,128)(2,1)S(1)}, bf16[16,4096]{1,0:T(8,128)(2,1)S(1)}, bf16[16,4096]{1,0:T(8,128)(2...) custom-call(bf16[8,4224]{1,0:T(8,128)(2,1)S(1)} %get-tuple-element.29.refs_0_.in_ref, ...), custom_call_target="tpu_custom_call" | custom-call | flops 6400000000 | bytes 4718592 | tf_op jit(solution)/shard_map/pallas_call | solution.py:467
  22.7 1.3 %collective-permute-start.7 = (bf16[16,4224]{1,0:T(8,128)(2,1)S(1)}, bf16[16,4224]{1,0:T(8,128)(2,1)S(1)}, u32[]{:S(2)}, u32[]{:S(2)}) collective-permute-start(bf16[16,4224]{1,0:T(8,128)(2,1)S(1)} %get-tuple-element.37), channel_id=1, source_target_pairs={{0,2},{1,3},{2,0},{3,1},{4,6},{5,7},{6,4},{7,5},{8,10},{9,11},{10,... | collective-permute-start | bytes 405512 | tf_op jit(solution)/shard_map/ppermute | solution.py:406
  24.1 0.5 %collective-permute-start.14 = (bf16[16,4096]{1,0:T(8,128)(2,1)S(1)}, bf16[16,4096]{1,0:T(8,128)(2,1)S(1)}, u32[]{:S(2)}, u32[]{:S(2)}) collective-permute-start(bf16[16,4096]{1,0:T(8,128)(2,1)S(1)} %get-tuple-element.47.refs_4_), channel_id=1, source_target_pairs={{0,1},{1,0},{2,3},{3,2},{4,5},{5,4},{6,7},{7,6},{8,9},{9,8},{10,11... | collective-permute-start | bytes 393224 | tf_op jit(solution)/shard_map/ppermute | solution.py:409
  24.6 0.0 collective-permute-start.15
  24.6 0.7 %collective-permute-done.16.refs_9_ = bf16[32,640]{1,0:T(8,128)(2,1)S(1)} collective-permute-done((bf16[32,640]{1,0:T(8,128)(2,1)S(1)}, bf16[32,640]{1,0:T(8,128)(2,1)S(1)}, u32[]{:S(2)}, u32[]{:S(2)}) %collective-permute-start.16) | collective-permute-done | bytes 40992 | tf_op jit(solution)/shard_map/ppermute | solution.py:409
  25.3 0.2 collective-permute-start.12
  25.4 2.4 %collective-permute-done.7.got_ref = bf16[16,4224]{1,0:T(8,128)(2,1)S(1)} collective-permute-done((bf16[16,4224]{1,0:T(8,128)(2,1)S(1)}, bf16[16,4224]{1,0:T(8,128)(2,1)S(1)}, u32[]{:S(2)}, u32[]{:S(2)}) %collective-permute-start.7) | collective-permute-done | bytes 135200 | tf_op jit(solution)/shard_map/ppermute | solution.py:406
  27.8 0.0 collective-permute-start.13
  27.8 0.2 shard_map.107
  28.0 4.7 %collective-permute-start.8 = (bf16[8,4224]{1,0:T(8,128)(2,1)S(1)}, bf16[8,4224]{1,0:T(8,128)(2,1)S(1)}, u32[]{:S(2)}, u32[]{:S(2)}) collective-permute-start(bf16[8,4224]{1,0:T(8,128)(2,1)S(1)} %get-tuple-element.39), channel_id=1, source_target_pairs={{8,4},{9,5},{10,6},{11,7},{12,0},{13,1},{14,2},{15,3},{16,12},{17,... | collective-permute-start | bytes 202760 | tf_op jit(solution)/shard_map/ppermute | solution.py:417
  32.8 0.5 %collective-permute-start.9 = (bf16[8,4096]{1,0:T(8,128)(2,1)S(1)}, bf16[8,4096]{1,0:T(8,128)(2,1)S(1)}, u32[]{:S(2)}, u32[]{:S(2)}) collective-permute-start(bf16[8,4096]{1,0:T(8,128)(2,1)S(1)} %get-tuple-element.40.refs_10_), channel_id=1, source_target_pairs={{8,0},{9,1},{10,2},{11,3},{12,4},{13,5},{14,6},{15,7},{16,8},{17,9... | collective-permute-start | bytes 196616 | tf_op jit(solution)/shard_map/ppermute | solution.py:417
  33.3 0.3 collective-permute-start.11
  33.7 2.7 %shard_map.109 = (bf16[384,4096]{1,0:T(8,128)(2,1)}, bf16[192,4096]{1,0:T(8,128)(2,1)}) custom-call(bf16[16,4096]{1,0:T(8,128)(2,1)S(1)} %get-tuple-element.45.refs_0_, bf16[16,4096]{1,0:T(8,128)(2,1)S(1)} %get-tuple-element.46.refs_1_, bf16[16,4096]{1,0:T(8,128)(2,1)S(1)} %collective-permute-done.12.refs_2_, ...), custom_call_target="tpu_custom_call" | custom-call | flops 301989888 | bytes 4718592 | tf_op jit(solution)/shard_map/pallas_call | solution.py:354
  36.3 1.5 %collective-permute-done.11.other_comb_ref = f32[8,128]{1,0:T(8,128)S(1)} collective-permute-done((f32[8,128]{1,0:T(8,128)S(1)}, f32[8,128]{1,0:T(8,128)S(1)}, u32[]{:S(2)}, u32[]{:S(2)}) %collective-permute-start.11) | collective-permute-done | bytes 4128 | tf_op jit(solution)/shard_map/ppermute | solution.py:406
  37.8 1.5 %shard_map.108 = (bf16[128,4096]{1,0:T(8,128)(2,1)}, f32[8,128]{1,0:T(8,128)}) custom-call(bf16[8,4224]{1,0:T(8,128)(2,1)S(1)} %collective-permute-done.8.other_ref, bf16[8,4096]{1,0:T(8,128)(2,1)S(1)} %collective-permute-done.9.own_ref, bf16[128,4096]{1,0:T(8,128)(2,1)S(1)} %collective-permute-done.10.grad_ref, ...), custom_call_target="tpu_custom_call" | custom-call | flops 16777216 | bytes 2097152 | tf_op jit(solution)/shard_map/pallas_call | solution.py:485
  (14 shorter events, 0.0 us)
Async XLA Ops:
  0.6 9.5 %collective-permute-start.1 = (bf16[384,4096]{1,0:T(8,128)(2,1)}, bf16[384,4096]{1,0:T(8,128)(2,1)S(1)}, u32[]{:S(2)}, u32[]{:S(2)}) collective-permute-start(bf16[384,4096]{1,0:T(8,128)(2,1)} %bitcast.18), channel_id=1, source_target_pairs={{0,1},{1,0},{2,3},{3,2},{4,5},{5,4},{6,7},{7,6},{8,9},{9,8},{10,11... | collective-permute-start | bytes 9437192 | tf_op jit(solution)/shard_map/ppermute | solution.py:409
  1.1 8.9 %collective-permute-start.2 = (bf16[192,4096]{1,0:T(8,128)(2,1)}, bf16[192,4096]{1,0:T(8,128)(2,1)S(1)}, u32[]{:S(2)}, u32[]{:S(2)}) collective-permute-start(bf16[192,4096]{1,0:T(8,128)(2,1)} %bitcast.20), channel_id=1, source_target_pairs={{0,1},{1,0},{2,3},{3,2},{4,5},{5,4},{6,7},{7,6},{8,9},{9,8},{10,11... | collective-permute-start | bytes 4718600 | tf_op jit(solution)/shard_map/ppermute | solution.py:409
  3.2 8.7 %collective-permute-start = (bf16[8,4224]{1,0:T(8,128)(2,1)S(1)}, bf16[8,4224]{1,0:T(8,128)(2,1)S(1)}, u32[]{:S(2)}, u32[]{:S(2)}) collective-permute-start(bf16[8,4224]{1,0:T(8,128)(2,1)S(1)} %get-tuple-element.29.refs_0_.in_ref), channel_id=1, source_target_pairs={{0,4},{1,5},{2,6},{3,7},{4,0},{5,1},{6,2},{7,3},{8,12},{9,13},{10,... | collective-permute-start | bytes 202760 | tf_op jit(solution)/shard_map/ppermute | solution.py:406
  7.3 6.8 %collective-permute-start.5 = (bf16[8,4224]{1,0:T(8,128)(2,1)S(1)}, bf16[8,4224]{1,0:T(8,128)(2,1)S(1)}, u32[]{:S(2)}, u32[]{:S(2)}) collective-permute-start(bf16[8,4224]{1,0:T(8,128)(2,1)S(1)} %get-tuple-element.31.refs_4_), channel_id=1, source_target_pairs={{0,4},{1,5},{2,6},{3,7},{4,0},{5,1},{6,2},{7,3},{8,12},{9,13},{10,... | collective-permute-start | bytes 202760 | tf_op jit(solution)/shard_map/ppermute | solution.py:406
  7.4 28.9 %collective-permute-start.10 = (bf16[128,4096]{1,0:T(8,128)(2,1)}, bf16[128,4096]{1,0:T(8,128)(2,1)S(1)}, u32[]{:S(2)}, u32[]{:S(2)}) collective-permute-start(bf16[128,4096]{1,0:T(8,128)(2,1)} %bitcast.24), channel_id=1, source_target_pairs={{8,0},{9,1},{10,2},{11,3},{12,4},{13,5},{14,6},{15,7},{16,8},{17,9... | collective-permute-start | bytes 3145736 | tf_op jit(solution)/shard_map/ppermute | solution.py:417
  10.1 8.3 %collective-permute-start.3 = (bf16[16,4224]{1,0:T(8,128)(2,1)S(1)}, bf16[16,4224]{1,0:T(8,128)(2,1)S(1)}, u32[]{:S(2)}, u32[]{:S(2)}) collective-permute-start(bf16[16,4224]{1,0:T(8,128)(2,1)S(1)} %shard_map.103), channel_id=1, source_target_pairs={{0,2},{1,3},{2,0},{3,1},{4,6},{5,7},{6,4},{7,5},{8,10},{9,11},{10,... | collective-permute-start | bytes 405512 | tf_op jit(solution)/shard_map/ppermute | solution.py:406
  11.9 6.5 %collective-permute-start.4 = (bf16[8,4224]{1,0:T(8,128)(2,1)S(1)}, bf16[8,4224]{1,0:T(8,128)(2,1)S(1)}, u32[]{:S(2)}, u32[]{:S(2)}) collective-permute-start(bf16[8,4224]{1,0:T(8,128)(2,1)S(1)} %collective-permute-done.refs_1_.far_in_ref), channel_id=1, source_target_pairs={{0,2},{1,3},{2,0},{3,1},{4,6},{5,7},{6,4},{7,5},{8,10},{9,11},{10,... | collective-permute-start | bytes 202760 | tf_op jit(solution)/shard_map/ppermute | solution.py:406
  14.1 6.3 %collective-permute-start.6 = (bf16[8,4224]{1,0:T(8,128)(2,1)S(1)}, bf16[8,4224]{1,0:T(8,128)(2,1)S(1)}, u32[]{:S(2)}, u32[]{:S(2)}) collective-permute-start(bf16[8,4224]{1,0:T(8,128)(2,1)S(1)} %collective-permute-done.5.after_ref.refs_5_.far_grad_ref), channel_id=1, source_target_pairs={{0,2},{1,3},{2,0},{3,1},{4,6},{5,7},{6,4},{7,5},{8,10},{9,11},{10,... | collective-permute-start | bytes 202760 | tf_op jit(solution)/shard_map/ppermute | solution.py:406
  20.4 7.4 %copy-start = (f32[1,4096]{1,0:T(1,128)S(1)}, f32[1,4096]{1,0:T(1,128)}, u32[]{:S(2)}) copy-start(f32[1,4096]{1,0:T(1,128)} %gain_ref.1) | copy-start | bytes 49156
  20.4 17.4 %copy-start.1 = (s32[1,128,8]{1,2,0:T(8,128)S(1)}, s32[1,128,8]{1,2,0:T(8,128)}, u32[]{:S(2)}) copy-start(s32[1,128,8]{1,2,0:T(8,128)} %param.9) | copy-start | bytes 12292
  22.7 5.1 %collective-permute-start.7 = (bf16[16,4224]{1,0:T(8,128)(2,1)S(1)}, bf16[16,4224]{1,0:T(8,128)(2,1)S(1)}, u32[]{:S(2)}, u32[]{:S(2)}) collective-permute-start(bf16[16,4224]{1,0:T(8,128)(2,1)S(1)} %get-tuple-element.37), channel_id=1, source_target_pairs={{0,2},{1,3},{2,0},{3,1},{4,6},{5,7},{6,4},{7,5},{8,10},{9,11},{10,... | collective-permute-start | bytes 405512 | tf_op jit(solution)/shard_map/ppermute | solution.py:406
  24.1 1.2 %collective-permute-start.16 = (bf16[32,640]{1,0:T(8,128)(2,1)S(1)}, bf16[32,640]{1,0:T(8,128)(2,1)S(1)}, u32[]{:S(2)}, u32[]{:S(2)}) collective-permute-start(bf16[32,640]{1,0:T(8,128)(2,1)S(1)} %get-tuple-element.50), channel_id=1, source_target_pairs={{0,1},{1,0},{2,3},{3,2},{4,5},{5,4},{6,7},{7,6},{8,9},{9,8},{10,11... | collective-permute-start | bytes 122888 | tf_op jit(solution)/shard_map/ppermute | solution.py:409
  24.1 4.0 %collective-permute-start.14 = (bf16[16,4096]{1,0:T(8,128)(2,1)S(1)}, bf16[16,4096]{1,0:T(8,128)(2,1)S(1)}, u32[]{:S(2)}, u32[]{:S(2)}) collective-permute-start(bf16[16,4096]{1,0:T(8,128)(2,1)S(1)} %get-tuple-element.47.refs_4_), channel_id=1, source_target_pairs={{0,1},{1,0},{2,3},{3,2},{4,5},{5,4},{6,7},{7,6},{8,9},{9,8},{10,11... | collective-permute-start | bytes 393224 | tf_op jit(solution)/shard_map/ppermute | solution.py:409
  24.6 8.2 %collective-permute-start.15 = (bf16[16,4096]{1,0:T(8,128)(2,1)S(1)}, bf16[16,4096]{1,0:T(8,128)(2,1)S(1)}, u32[]{:S(2)}, u32[]{:S(2)}) collective-permute-start(bf16[16,4096]{1,0:T(8,128)(2,1)S(1)} %get-tuple-element.48.refs_5_), channel_id=1, source_target_pairs={{0,1},{1,0},{2,3},{3,2},{4,5},{5,4},{6,7},{7,6},{8,9},{9,8},{10,11... | collective-permute-start | bytes 393224 | tf_op jit(solution)/shard_map/ppermute | solution.py:409
  25.3 8.0 %collective-permute-start.12 = (bf16[16,4096]{1,0:T(8,128)(2,1)S(1)}, bf16[16,4096]{1,0:T(8,128)(2,1)S(1)}, u32[]{:S(2)}, u32[]{:S(2)}) collective-permute-start(bf16[16,4096]{1,0:T(8,128)(2,1)S(1)} %get-tuple-element.45.refs_0_), channel_id=1, source_target_pairs={{0,1},{1,0},{2,3},{3,2},{4,5},{5,4},{6,7},{7,6},{8,9},{9,8},{10,11... | collective-permute-start | bytes 393224 | tf_op jit(solution)/shard_map/ppermute | solution.py:409
  27.8 5.9 %collective-permute-start.13 = (bf16[16,4096]{1,0:T(8,128)(2,1)S(1)}, bf16[16,4096]{1,0:T(8,128)(2,1)S(1)}, u32[]{:S(2)}, u32[]{:S(2)}) collective-permute-start(bf16[16,4096]{1,0:T(8,128)(2,1)S(1)} %get-tuple-element.46.refs_1_), channel_id=1, source_target_pairs={{0,1},{1,0},{2,3},{3,2},{4,5},{5,4},{6,7},{7,6},{8,9},{9,8},{10,11... | collective-permute-start | bytes 393224 | tf_op jit(solution)/shard_map/ppermute | solution.py:409
  28.0 9.8 %collective-permute-start.8 = (bf16[8,4224]{1,0:T(8,128)(2,1)S(1)}, bf16[8,4224]{1,0:T(8,128)(2,1)S(1)}, u32[]{:S(2)}, u32[]{:S(2)}) collective-permute-start(bf16[8,4224]{1,0:T(8,128)(2,1)S(1)} %get-tuple-element.39), channel_id=1, source_target_pairs={{8,4},{9,5},{10,6},{11,7},{12,0},{13,1},{14,2},{15,3},{16,12},{17,... | collective-permute-start | bytes 202760 | tf_op jit(solution)/shard_map/ppermute | solution.py:417
  32.8 5.1 %collective-permute-start.9 = (bf16[8,4096]{1,0:T(8,128)(2,1)S(1)}, bf16[8,4096]{1,0:T(8,128)(2,1)S(1)}, u32[]{:S(2)}, u32[]{:S(2)}) collective-permute-start(bf16[8,4096]{1,0:T(8,128)(2,1)S(1)} %get-tuple-element.40.refs_10_), channel_id=1, source_target_pairs={{8,0},{9,1},{10,2},{11,3},{12,4},{13,5},{14,6},{15,7},{16,8},{17,9... | collective-permute-start | bytes 196616 | tf_op jit(solution)/shard_map/ppermute | solution.py:417
  33.3 4.5 %collective-permute-start.11 = (f32[8,128]{1,0:T(8,128)S(1)}, f32[8,128]{1,0:T(8,128)S(1)}, u32[]{:S(2)}, u32[]{:S(2)}) collective-permute-start(f32[8,128]{1,0:T(8,128)S(1)} %get-tuple-element.41), channel_id=1, source_target_pairs={{0,4},{1,5},{2,6},{3,7},{4,0},{5,1},{6,2},{7,3},{8,12},{9,13},{10,... | collective-permute-start | bytes 12296 | tf_op jit(solution)/shard_map/ppermute | solution.py:406

commit v7 on v6

--- a/solution.py
+++ b/solution.py
@@ -152,7 +152,7 @@
 
 
 FETCH_FLOPS = 1_000_000_000
-HIDDEN_FLOPS = 6_400_000_000
+HIDDEN_FLOPS = 7_000_000_000
 IN_HBM = pl.BlockSpec(memory_space=pltpu.HBM)
 IN_VMEM = pl.BlockSpec(memory_space=pltpu.VMEM)
 
@@ -231,12 +231,6 @@
     second.start()
     first.wait()
     second.wait()
-
-
-def pass_kernel(block_ref, *refs):
-    *after_refs, out_ref = refs
-    del after_refs
-    out_ref[...] = block_ref[...]
 
 
 def stacked(refs, half, start, stop):
@@ -416,7 +410,6 @@
         ]
         return lax.ppermute(block, ("pipe", "expert"), route)
 
-    next_grad = handed(out_grad[0], 0)
     row_in, row_grad, row_both, normed, place = call(
         rows_kernel,
         [((cap, wide), BF16)] * 2
@@ -436,14 +429,9 @@
     far_in = across(row_in, 2)
     far_grad = across(row_grad, 2)
     slab_two, down_two = beside(slab), beside(down)
-    (passed,) = call(
-        pass_kernel,
-        [(row_both.shape, BF16)],
-        0,
-        4 * cap * wide,
-        in_specs=[IN_VMEM] + [pl.BlockSpec(memory_space=pl.ANY)] * 2,
-    )(row_both, slab_two, down_two)
-    near = across(passed, 1)
+    near = across(row_both, 1)
+    grad_after, _ = lax.optimization_barrier((out_grad[0], slab_two))
+    next_grad = handed(grad_after, 0)
     slab_near, down_near = call(
         fetch_kernel,
         [(slab.shape, BF16), (down.shape, BF16)],

time: 39.5 us -> 39.1 us (0.990)
  waiting for transfers between devices: 6.67 us -> 5.78 us
  starting transfers between devices: 18.9 us -> 19.4 us
    ppermute x7, waiting for transfers between devices: 5.95 us -> 5.06 us  [across(): lax.ppermute(block, 'expert', [(i, i ^ 2 * offset) for i in range(devices)])]
  transfers between devices with their start and end apart: 17 -> 17, of which waited for: 5 -> 4; matrix products, arithmetic and copies ran while one was open for 0% -> 0% of each run, Pallas kernels for 29% -> 30%
where the time goes in v7:
time: 39.1 us; the launch traced here: 38.9 us
  starting transfers between devices  19.4 us (50%)
  Pallas kernels  13 us (33%)
  waiting for transfers between devices  5.78 us (15%)
  between operations  0.75 us (2%)
    ppermute x7, starting transfers between devices, across(): lax.ppermute(block, 'expert', [(i, i ^ 2 * offset) for i in range(devices)])  9.82 us
    ppermute x3, starting transfers between devices, handed(): return lax.ppermute(block, ('pipe', 'expert'), route)  8.3 us
    ppermute x7, waiting for transfers between devices, across(): lax.ppermute(block, 'expert', [(i, i ^ 2 * offset) for i in range(devices)])  5.06 us
    pallas_call x1, Pallas kernels, weight_grads(): pl.pallas_call(functools.partial(weights_kernel, chunks), in_specs=[IN_VM...  2.65 us
    pallas_call x1, Pallas kernels, on_one(): call(fetch_kernel, [(slab.shape, BF16), (down.shape, BF16)], FETCH_FLOPS,...  2.37 us
    pallas_call x1, Pallas kernels, on_one(): call(hidden_kernel, [((2 * cap, wide), BF16)] * 2 + [half_rows] * 2 + [((...  2.32 us
    pallas_call x1, Pallas kernels, on_one(): call(rows_kernel, [((cap, wide), BF16)] * 2 + [((2 * cap, wide), BF16), (...  2 us
    pallas_call x1, Pallas kernels, on_one(): call(project_kernel, [((total_rows // 2, 2 * hidden), F32)] * 2 + [half_r...  1.93 us
  transfers between devices with their start and end apart: 17, of which 4 were waited for; matrix products, arithmetic and copies ran while one was open for 0% of the time, Pallas kernels for 30%

profile of v7, /device:TPU:0, one launch (start us, length us, event | category | flops | bytes accessed | tf_op | source)
XLA Modules:
  0.0 38.9 jit_solution(17490617811072140769)
XLA Ops:
  0.6 0.5 %collective-permute-start.5 = (bf16[384,4096]{1,0:T(8,128)(2,1)}, bf16[384,4096]{1,0:T(8,128)(2,1)S(1)}, u32[]{:S(2)}, u32[]{:S(2)}) collective-permute-start(bf16[384,4096]{1,0:T(8,128)(2,1)} %bitcast.18), channel_id=1, source_target_pairs={{0,1},{1,0},{2,3},{3,2},{4,5},{5,4},{6,7},{7,6},{8,9},{9,8},{10,11... | collective-permute-start | bytes 9437192 | tf_op jit(solution)/shard_map/ppermute | solution.py:403
  1.1 0.1 collective-permute-start.6
  1.2 2.0 %shard_map.102 = (bf16[8,4224]{1,0:T(8,128)(2,1)S(1)}, bf16[8,4224]{1,0:T(8,128)(2,1)S(1)}, bf16[16,4224]{1,0:T(8,128)(2,1)S(1)}, f32[8,4096]{1,0:T(8,128)S(1)}, f32[8,128]{1,0:T(8,128)S(1)}) custom-call(s32[8,128]{1,0:T(8,128)} %bitcast.16, bf16[8,128]{1,0:T(8,128)(2,1)} %bitcast.25, f32[1,4096]{1,0:T(1,128)} %gain_ref.1, bf16[128,4096]{1,0:T(8,128)(2,1)} %bitcast.22, ...), custom_call_target="tpu_custom_call" | custom-call | flops 16777216 | bytes 2097152 | tf_op jit(solution)/shard_map/pallas_call | solution.py:413
  3.2 4.1 %collective-permute-start = (bf16[8,4224]{1,0:T(8,128)(2,1)S(1)}, bf16[8,4224]{1,0:T(8,128)(2,1)S(1)}, u32[]{:S(2)}, u32[]{:S(2)}) collective-permute-start(bf16[8,4224]{1,0:T(8,128)(2,1)S(1)} %get-tuple-element.30.refs_0_.in_ref), channel_id=1, source_target_pairs={{0,4},{1,5},{2,6},{3,7},{4,0},{5,1},{6,2},{7,3},{8,12},{9,13},{10,... | collective-permute-start | bytes 202760 | tf_op jit(solution)/shard_map/ppermute | solution.py:400
  7.3 0.1 collective-permute-start.3
  7.4 1.8 %collective-permute-start.1 = (bf16[16,4224]{1,0:T(8,128)(2,1)S(1)}, bf16[16,4224]{1,0:T(8,128)(2,1)S(1)}, u32[]{:S(2)}, u32[]{:S(2)}) collective-permute-start(bf16[16,4224]{1,0:T(8,128)(2,1)S(1)} %get-tuple-element.31), channel_id=1, source_target_pairs={{0,2},{1,3},{2,0},{3,1},{4,6},{5,7},{6,4},{7,5},{8,10},{9,11},{10,... | collective-permute-start | bytes 405512 | tf_op jit(solution)/shard_map/ppermute | solution.py:400
  9.2 2.4 %collective-permute-start.10 = (bf16[128,4096]{1,0:T(8,128)(2,1)}, bf16[128,4096]{1,0:T(8,128)(2,1)S(1)}, u32[]{:S(2)}, u32[]{:S(2)}) collective-permute-start(bf16[128,4096]{1,0:T(8,128)(2,1)} %bitcast.24), channel_id=1, source_target_pairs={{8,0},{9,1},{10,2},{11,3},{12,4},{13,5},{14,6},{15,7},{16,8},{17,9... | collective-permute-start | bytes 3145736 | tf_op jit(solution)/shard_map/ppermute | solution.py:411
  11.7 0.0 collective-permute-done.refs_1_.far_in_ref
  11.7 1.7 %collective-permute-start.2 = (bf16[8,4224]{1,0:T(8,128)(2,1)S(1)}, bf16[8,4224]{1,0:T(8,128)(2,1)S(1)}, u32[]{:S(2)}, u32[]{:S(2)}) collective-permute-start(bf16[8,4224]{1,0:T(8,128)(2,1)S(1)} %collective-permute-done.refs_1_.far_in_ref), channel_id=1, source_target_pairs={{0,2},{1,3},{2,0},{3,1},{4,6},{5,7},{6,4},{7,5},{8,10},{9,11},{10,... | collective-permute-start | bytes 202760 | tf_op jit(solution)/shard_map/ppermute | solution.py:400
  13.3 0.5 %collective-permute-done.3.after_ref.refs_5_.far_grad_ref = bf16[8,4224]{1,0:T(8,128)(2,1)S(1)} collective-permute-done((bf16[8,4224]{1,0:T(8,128)(2,1)S(1)}, bf16[8,4224]{1,0:T(8,128)(2,1)S(1)}, u32[]{:S(2)}, u32[]{:S(2)}) %collective-permute-start.3) | collective-permute-done | bytes 67616 | tf_op jit(solution)/shard_map/ppermute | solution.py:400
  13.8 1.0 %collective-permute-start.4 = (bf16[8,4224]{1,0:T(8,128)(2,1)S(1)}, bf16[8,4224]{1,0:T(8,128)(2,1)S(1)}, u32[]{:S(2)}, u32[]{:S(2)}) collective-permute-start(bf16[8,4224]{1,0:T(8,128)(2,1)S(1)} %collective-permute-done.3.after_ref.refs_5_.far_grad_ref), channel_id=1, source_target_pairs={{0,2},{1,3},{2,0},{3,1},{4,6},{5,7},{6,4},{7,5},{8,10},{9,11},{10,... | collective-permute-start | bytes 202760 | tf_op jit(solution)/shard_map/ppermute | solution.py:400
  14.8 2.4 %shard_map.103 = (bf16[384,4096]{1,0:T(8,128)(2,1)S(1)}, bf16[192,4096]{1,0:T(8,128)(2,1)S(1)}) custom-call(bf16[384,4096]{1,0:T(8,128)(2,1)} %bitcast.19, bf16[192,4096]{1,0:T(8,128)(2,1)} %bitcast.21, bf16[8,4224]{1,0:T(8,128)(2,1)S(1)} %collective-permute-done.3.after_ref.refs_5_.far_grad_ref), custom_call_target="tpu_custom_call" | custom-call | flops 1000000000 | bytes 4718592 | tf_op jit(solution)/shard_map/pallas_call | solution.py:435
  17.2 0.0 collective-permute-done.1.refs_2_.refs_6_
  17.2 1.9 %shard_map.104 = (f32[32,384]{1,0:T(8,128)S(1)}, f32[32,384]{1,0:T(8,128)S(1)}, bf16[16,4096]{1,0:T(8,128)(2,1)S(1)}, bf16[16,4096]{1,0:T(8,128)(2,1)S(1)}) custom-call(bf16[8,4224]{1,0:T(8,128)(2,1)S(1)} %get-tuple-element.30.refs_0_.in_ref, bf16[8,4224]{1,0:T(8,128)(2,1)S(1)} %collective-permute-done.refs_1_.far_in_ref, ...), custom_call_target="tpu_custom_call" | custom-call | bytes 3145728 | tf_op jit(solution)/shard_map/pallas_call | solution.py:448
  19.1 0.0 collective-permute-done.4.refs_7_
  19.2 0.0 collective-permute-done.6.refs_13_
  19.2 0.0 copy-start
  19.2 0.0 copy-start.1
  19.2 2.3 %shard_map.105 = (bf16[16,4224]{1,0:T(8,128)(2,1)S(1)}, bf16[16,4224]{1,0:T(8,128)(2,1)S(1)}, bf16[16,4096]{1,0:T(8,128)(2,1)S(1)}, bf16[16,4096]{1,0:T(8,128)(2...) custom-call(bf16[8,4224]{1,0:T(8,128)(2,1)S(1)} %get-tuple-element.30.refs_0_.in_ref, ...), custom_call_target="tpu_custom_call" | custom-call | flops 7000000000 | bytes 4718592 | tf_op jit(solution)/shard_map/pallas_call | solution.py:455
  21.5 1.1 %collective-permute-start.7 = (bf16[16,4224]{1,0:T(8,128)(2,1)S(1)}, bf16[16,4224]{1,0:T(8,128)(2,1)S(1)}, u32[]{:S(2)}, u32[]{:S(2)}) collective-permute-start(bf16[16,4224]{1,0:T(8,128)(2,1)S(1)} %get-tuple-element.38), channel_id=1, source_target_pairs={{0,2},{1,3},{2,0},{3,1},{4,6},{5,7},{6,4},{7,5},{8,10},{9,11},{10,... | collective-permute-start | bytes 405512 | tf_op jit(solution)/shard_map/ppermute | solution.py:400
  22.6 0.0 collective-permute-start.16
  22.6 0.5 %collective-permute-start.14 = (bf16[16,4096]{1,0:T(8,128)(2,1)S(1)}, bf16[16,4096]{1,0:T(8,128)(2,1)S(1)}, u32[]{:S(2)}, u32[]{:S(2)}) collective-permute-start(bf16[16,4096]{1,0:T(8,128)(2,1)S(1)} %get-tuple-element.49.refs_4_), channel_id=1, source_target_pairs={{0,1},{1,0},{2,3},{3,2},{4,5},{5,4},{6,7},{7,6},{8,9},{9,8},{10,11... | collective-permute-start | bytes 393224 | tf_op jit(solution)/shard_map/ppermute | solution.py:403
  23.1 0.7 %collective-permute-done.16.refs_9_ = bf16[32,640]{1,0:T(8,128)(2,1)S(1)} collective-permute-done((bf16[32,640]{1,0:T(8,128)(2,1)S(1)}, bf16[32,640]{1,0:T(8,128)(2,1)S(1)}, u32[]{:S(2)}, u32[]{:S(2)}) %collective-permute-start.16) | collective-permute-done | bytes 40992 | tf_op jit(solution)/shard_map/ppermute | solution.py:403
  23.8 0.2 collective-permute-start.12
  24.0 2.8 %collective-permute-done.7.got_ref = bf16[16,4224]{1,0:T(8,128)(2,1)S(1)} collective-permute-done((bf16[16,4224]{1,0:T(8,128)(2,1)S(1)}, bf16[16,4224]{1,0:T(8,128)(2,1)S(1)}, u32[]{:S(2)}, u32[]{:S(2)}) %collective-permute-start.7) | collective-permute-done | bytes 135200 | tf_op jit(solution)/shard_map/ppermute | solution.py:400
  26.8 0.2 shard_map.106
  27.0 5.3 %collective-permute-start.8 = (bf16[8,4224]{1,0:T(8,128)(2,1)S(1)}, bf16[8,4224]{1,0:T(8,128)(2,1)S(1)}, u32[]{:S(2)}, u32[]{:S(2)}) collective-permute-start(bf16[8,4224]{1,0:T(8,128)(2,1)S(1)} %get-tuple-element.40), channel_id=1, source_target_pairs={{8,4},{9,5},{10,6},{11,7},{12,0},{13,1},{14,2},{15,3},{16,12},{17,... | collective-permute-start | bytes 202760 | tf_op jit(solution)/shard_map/ppermute | solution.py:411
  32.4 0.5 %collective-permute-start.9 = (bf16[8,4096]{1,0:T(8,128)(2,1)S(1)}, bf16[8,4096]{1,0:T(8,128)(2,1)S(1)}, u32[]{:S(2)}, u32[]{:S(2)}) collective-permute-start(bf16[8,4096]{1,0:T(8,128)(2,1)S(1)} %get-tuple-element.41.refs_10_), channel_id=1, source_target_pairs={{8,0},{9,1},{10,2},{11,3},{12,4},{13,5},{14,6},{15,7},{16,8},{17,9... | collective-permute-start | bytes 196616 | tf_op jit(solution)/shard_map/ppermute | solution.py:411
  32.9 0.1 collective-permute-start.11
  33.0 2.7 %shard_map.108 = (bf16[384,4096]{1,0:T(8,128)(2,1)}, bf16[192,4096]{1,0:T(8,128)(2,1)}) custom-call(bf16[16,4096]{1,0:T(8,128)(2,1)S(1)} %get-tuple-element.47.refs_0_, bf16[16,4096]{1,0:T(8,128)(2,1)S(1)} %get-tuple-element.48.refs_1_, bf16[16,4096]{1,0:T(8,128)(2,1)S(1)} %collective-permute-done.12.refs_2_, ...), custom_call_target="tpu_custom_call" | custom-call | flops 301989888 | bytes 4718592 | tf_op jit(solution)/shard_map/pallas_call | solution.py:348
  35.7 1.7 %collective-permute-done.11.other_comb_ref = f32[8,128]{1,0:T(8,128)S(1)} collective-permute-done((f32[8,128]{1,0:T(8,128)S(1)}, f32[8,128]{1,0:T(8,128)S(1)}, u32[]{:S(2)}, u32[]{:S(2)}) %collective-permute-start.11) | collective-permute-done | bytes 4128 | tf_op jit(solution)/shard_map/ppermute | solution.py:400
  37.4 1.5 %shard_map.107 = (bf16[128,4096]{1,0:T(8,128)(2,1)}, f32[8,128]{1,0:T(8,128)}) custom-call(bf16[8,4224]{1,0:T(8,128)(2,1)S(1)} %collective-permute-done.8.other_ref, bf16[8,4096]{1,0:T(8,128)(2,1)S(1)} %collective-permute-done.9.own_ref, bf16[128,4096]{1,0:T(8,128)(2,1)S(1)} %collective-permute-done.10.grad_ref, ...), custom_call_target="tpu_custom_call" | custom-call | flops 16777216 | bytes 2097152 | tf_op jit(solution)/shard_map/pallas_call | solution.py:473
  (13 shorter events, 0.0 us)
Async XLA Ops:
  0.6 8.6 %collective-permute-start.5 = (bf16[384,4096]{1,0:T(8,128)(2,1)}, bf16[384,4096]{1,0:T(8,128)(2,1)S(1)}, u32[]{:S(2)}, u32[]{:S(2)}) collective-permute-start(bf16[384,4096]{1,0:T(8,128)(2,1)} %bitcast.18), channel_id=1, source_target_pairs={{0,1},{1,0},{2,3},{3,2},{4,5},{5,4},{6,7},{7,6},{8,9},{9,8},{10,11... | collective-permute-start | bytes 9437192 | tf_op jit(solution)/shard_map/ppermute | solution.py:403
  1.1 18.0 %collective-permute-start.6 = (bf16[192,4096]{1,0:T(8,128)(2,1)}, bf16[192,4096]{1,0:T(8,128)(2,1)S(1)}, u32[]{:S(2)}, u32[]{:S(2)}) collective-permute-start(bf16[192,4096]{1,0:T(8,128)(2,1)} %bitcast.20), channel_id=1, source_target_pairs={{0,1},{1,0},{2,3},{3,2},{4,5},{5,4},{6,7},{7,6},{8,9},{9,8},{10,11... | collective-permute-start | bytes 4718600 | tf_op jit(solution)/shard_map/ppermute | solution.py:403
  3.2 8.4 %collective-permute-start = (bf16[8,4224]{1,0:T(8,128)(2,1)S(1)}, bf16[8,4224]{1,0:T(8,128)(2,1)S(1)}, u32[]{:S(2)}, u32[]{:S(2)}) collective-permute-start(bf16[8,4224]{1,0:T(8,128)(2,1)S(1)} %get-tuple-element.30.refs_0_.in_ref), channel_id=1, source_target_pairs={{0,4},{1,5},{2,6},{3,7},{4,0},{5,1},{6,2},{7,3},{8,12},{9,13},{10,... | collective-permute-start | bytes 202760 | tf_op jit(solution)/shard_map/ppermute | solution.py:400
  7.3 6.5 %collective-permute-start.3 = (bf16[8,4224]{1,0:T(8,128)(2,1)S(1)}, bf16[8,4224]{1,0:T(8,128)(2,1)S(1)}, u32[]{:S(2)}, u32[]{:S(2)}) collective-permute-start(bf16[8,4224]{1,0:T(8,128)(2,1)S(1)} %get-tuple-element.32.refs_4_), channel_id=1, source_target_pairs={{0,4},{1,5},{2,6},{3,7},{4,0},{5,1},{6,2},{7,3},{8,12},{9,13},{10,... | collective-permute-start | bytes 202760 | tf_op jit(solution)/shard_map/ppermute | solution.py:400
  7.4 9.8 %collective-permute-start.1 = (bf16[16,4224]{1,0:T(8,128)(2,1)S(1)}, bf16[16,4224]{1,0:T(8,128)(2,1)S(1)}, u32[]{:S(2)}, u32[]{:S(2)}) collective-permute-start(bf16[16,4224]{1,0:T(8,128)(2,1)S(1)} %get-tuple-element.31), channel_id=1, source_target_pairs={{0,2},{1,3},{2,0},{3,1},{4,6},{5,7},{6,4},{7,5},{8,10},{9,11},{10,... | collective-permute-start | bytes 405512 | tf_op jit(solution)/shard_map/ppermute | solution.py:400
  9.2 28.2 %collective-permute-start.10 = (bf16[128,4096]{1,0:T(8,128)(2,1)}, bf16[128,4096]{1,0:T(8,128)(2,1)S(1)}, u32[]{:S(2)}, u32[]{:S(2)}) collective-permute-start(bf16[128,4096]{1,0:T(8,128)(2,1)} %bitcast.24), channel_id=1, source_target_pairs={{8,0},{9,1},{10,2},{11,3},{12,4},{13,5},{14,6},{15,7},{16,8},{17,9... | collective-permute-start | bytes 3145736 | tf_op jit(solution)/shard_map/ppermute | solution.py:411
  11.7 5.5 %collective-permute-start.2 = (bf16[8,4224]{1,0:T(8,128)(2,1)S(1)}, bf16[8,4224]{1,0:T(8,128)(2,1)S(1)}, u32[]{:S(2)}, u32[]{:S(2)}) collective-permute-start(bf16[8,4224]{1,0:T(8,128)(2,1)S(1)} %collective-permute-done.refs_1_.far_in_ref), channel_id=1, source_target_pairs={{0,2},{1,3},{2,0},{3,1},{4,6},{5,7},{6,4},{7,5},{8,10},{9,11},{10,... | collective-permute-start | bytes 202760 | tf_op jit(solution)/shard_map/ppermute | solution.py:400
  13.8 5.3 %collective-permute-start.4 = (bf16[8,4224]{1,0:T(8,128)(2,1)S(1)}, bf16[8,4224]{1,0:T(8,128)(2,1)S(1)}, u32[]{:S(2)}, u32[]{:S(2)}) collective-permute-start(bf16[8,4224]{1,0:T(8,128)(2,1)S(1)} %collective-permute-done.3.after_ref.refs_5_.far_grad_ref), channel_id=1, source_target_pairs={{0,2},{1,3},{2,0},{3,1},{4,6},{5,7},{6,4},{7,5},{8,10},{9,11},{10,... | collective-permute-start | bytes 202760 | tf_op jit(solution)/shard_map/ppermute | solution.py:400
  19.2 7.6 %copy-start = (f32[1,4096]{1,0:T(1,128)S(1)}, f32[1,4096]{1,0:T(1,128)}, u32[]{:S(2)}) copy-start(f32[1,4096]{1,0:T(1,128)} %gain_ref.1) | copy-start | bytes 49156
  19.2 18.2 %copy-start.1 = (s32[1,128,8]{1,2,0:T(8,128)S(1)}, s32[1,128,8]{1,2,0:T(8,128)}, u32[]{:S(2)}) copy-start(s32[1,128,8]{1,2,0:T(8,128)} %param.9) | copy-start | bytes 12292
  21.5 5.3 %collective-permute-start.7 = (bf16[16,4224]{1,0:T(8,128)(2,1)S(1)}, bf16[16,4224]{1,0:T(8,128)(2,1)S(1)}, u32[]{:S(2)}, u32[]{:S(2)}) collective-permute-start(bf16[16,4224]{1,0:T(8,128)(2,1)S(1)} %get-tuple-element.38), channel_id=1, source_target_pairs={{0,2},{1,3},{2,0},{3,1},{4,6},{5,7},{6,4},{7,5},{8,10},{9,11},{10,... | collective-permute-start | bytes 405512 | tf_op jit(solution)/shard_map/ppermute | solution.py:400
  22.6 1.2 %collective-permute-start.16 = (bf16[32,640]{1,0:T(8,128)(2,1)S(1)}, bf16[32,640]{1,0:T(8,128)(2,1)S(1)}, u32[]{:S(2)}, u32[]{:S(2)}) collective-permute-start(bf16[32,640]{1,0:T(8,128)(2,1)S(1)} %get-tuple-element.52), channel_id=1, source_target_pairs={{0,1},{1,0},{2,3},{3,2},{4,5},{5,4},{6,7},{7,6},{8,9},{9,8},{10,11... | collective-permute-start | bytes 122888 | tf_op jit(solution)/shard_map/ppermute | solution.py:403
  22.6 4.4 %collective-permute-start.14 = (bf16[16,4096]{1,0:T(8,128)(2,1)S(1)}, bf16[16,4096]{1,0:T(8,128)(2,1)S(1)}, u32[]{:S(2)}, u32[]{:S(2)}) collective-permute-start(bf16[16,4096]{1,0:T(8,128)(2,1)S(1)} %get-tuple-element.49.refs_4_), channel_id=1, source_target_pairs={{0,1},{1,0},{2,3},{3,2},{4,5},{5,4},{6,7},{7,6},{8,9},{9,8},{10,11... | collective-permute-start | bytes 393224 | tf_op jit(solution)/shard_map/ppermute | solution.py:403
  23.1 9.3 %collective-permute-start.15 = (bf16[16,4096]{1,0:T(8,128)(2,1)S(1)}, bf16[16,4096]{1,0:T(8,128)(2,1)S(1)}, u32[]{:S(2)}, u32[]{:S(2)}) collective-permute-start(bf16[16,4096]{1,0:T(8,128)(2,1)S(1)} %get-tuple-element.50.refs_5_), channel_id=1, source_target_pairs={{0,1},{1,0},{2,3},{3,2},{4,5},{5,4},{6,7},{7,6},{8,9},{9,8},{10,11... | collective-permute-start | bytes 393224 | tf_op jit(solution)/shard_map/ppermute | solution.py:403
  23.8 9.1 %collective-permute-start.12 = (bf16[16,4096]{1,0:T(8,128)(2,1)S(1)}, bf16[16,4096]{1,0:T(8,128)(2,1)S(1)}, u32[]{:S(2)}, u32[]{:S(2)}) collective-permute-start(bf16[16,4096]{1,0:T(8,128)(2,1)S(1)} %get-tuple-element.47.refs_0_), channel_id=1, source_target_pairs={{0,1},{1,0},{2,3},{3,2},{4,5},{5,4},{6,7},{7,6},{8,9},{9,8},{10,11... | collective-permute-start | bytes 393224 | tf_op jit(solution)/shard_map/ppermute | solution.py:403
  26.8 6.2 %collective-permute-start.13 = (bf16[16,4096]{1,0:T(8,128)(2,1)S(1)}, bf16[16,4096]{1,0:T(8,128)(2,1)S(1)}, u32[]{:S(2)}, u32[]{:S(2)}) collective-permute-start(bf16[16,4096]{1,0:T(8,128)(2,1)S(1)} %get-tuple-element.48.refs_1_), channel_id=1, source_target_pairs={{0,1},{1,0},{2,3},{3,2},{4,5},{5,4},{6,7},{7,6},{8,9},{9,8},{10,11... | collective-permute-start | bytes 393224 | tf_op jit(solution)/shard_map/ppermute | solution.py:403
  27.0 10.4 %collective-permute-start.8 = (bf16[8,4224]{1,0:T(8,128)(2,1)S(1)}, bf16[8,4224]{1,0:T(8,128)(2,1)S(1)}, u32[]{:S(2)}, u32[]{:S(2)}) collective-permute-start(bf16[8,4224]{1,0:T(8,128)(2,1)S(1)} %get-tuple-element.40), channel_id=1, source_target_pairs={{8,4},{9,5},{10,6},{11,7},{12,0},{13,1},{14,2},{15,3},{16,12},{17,... | collective-permute-start | bytes 202760 | tf_op jit(solution)/shard_map/ppermute | solution.py:411
  32.4 5.1 %collective-permute-start.9 = (bf16[8,4096]{1,0:T(8,128)(2,1)S(1)}, bf16[8,4096]{1,0:T(8,128)(2,1)S(1)}, u32[]{:S(2)}, u32[]{:S(2)}) collective-permute-start(bf16[8,4096]{1,0:T(8,128)(2,1)S(1)} %get-tuple-element.41.refs_10_), channel_id=1, source_target_pairs={{8,0},{9,1},{10,2},{11,3},{12,4},{13,5},{14,6},{15,7},{16,8},{17,9... | collective-permute-start | bytes 196616 | tf_op jit(solution)/shard_map/ppermute | solution.py:411
  32.9 4.5 %collective-permute-start.11 = (f32[8,128]{1,0:T(8,128)S(1)}, f32[8,128]{1,0:T(8,128)S(1)}, u32[]{:S(2)}, u32[]{:S(2)}) collective-permute-start(f32[8,128]{1,0:T(8,128)S(1)} %get-tuple-element.43), channel_id=1, source_target_pairs={{0,4},{1,5},{2,6},{3,7},{4,0},{5,1},{6,2},{7,3},{8,12},{9,13},{10,... | collective-permute-start | bytes 12296 | tf_op jit(solution)/shard_map/ppermute | solution.py:400

commit v8 on v6

--- a/solution.py
+++ b/solution.py
@@ -151,7 +151,7 @@
     )
 
 
-FETCH_FLOPS = 1_000_000_000
+TOKEN_FLOPS = 1_000_000_000
 HIDDEN_FLOPS = 6_400_000_000
 IN_HBM = pl.BlockSpec(memory_space=pltpu.HBM)
 IN_VMEM = pl.BlockSpec(memory_space=pltpu.VMEM)
@@ -223,19 +223,13 @@
     both_ref[:, :width] = jnp.concatenate([normed_in, grad], axis=0).astype(BF16)
 
 
-def fetch_kernel(slab_hbm, down_hbm, after_ref, slab_ref, down_ref, sems):
+def token_kernel(after_ref, token_ref):
     del after_ref
-    first = pltpu.make_async_copy(slab_hbm, slab_ref, sems.at[0])
-    second = pltpu.make_async_copy(down_hbm, down_ref, sems.at[1])
-    first.start()
-    second.start()
-    first.wait()
-    second.wait()
-
-
-def pass_kernel(block_ref, *refs):
-    *after_refs, out_ref = refs
-    del after_refs
+    token_ref[...] = jnp.zeros_like(token_ref)
+
+
+def pass_kernel(block_ref, after_ref, out_ref):
+    del after_ref
     out_ref[...] = block_ref[...]
 
 
@@ -249,7 +243,8 @@
 
 
 def project_kernel(*refs):
-    *blocks, slab_ref, slab_two_ref, pre_ref, pre_two_ref, first_ref, last_ref = refs
+    *blocks, token_ref, slab_ref, slab_two_ref, pre_ref, pre_two_ref, first_ref, last_ref = refs
+    del token_ref
     width = slab_ref.shape[1]
     rows = stacked(blocks, 0, 0, width).astype(BF16)
     half = first_ref.shape[0]
@@ -371,12 +366,8 @@
     )(*blocks, keep, got, after)
 
 
-def finish_kernel(other_ref, own_ref, grad_ref, other_comb_ref, own_comb_ref, ids_ref, place_ref,
-                  out_ref, comb_ref):
+def finish_kernel(other_ref, own_ref, grad_ref, out_ref):
     width = grad_ref.shape[1]
-    comb = own_comb_ref[...] + other_comb_ref[...]
-    comb = jnp.sum(place_ref[...] * comb, axis=0, keepdims=True)
-    comb_ref[...] = jnp.where(ids_ref[...] == 0, comb, 0.0)
     place = other_ref[:, width:]
     grad = grad_ref[...]
     own = take_rows(place, grad)
@@ -386,6 +377,13 @@
     spread = take_rows(back.astype(BF16), rows)
     named = jnp.sum(back, axis=1, keepdims=True) > 0.0
     out_ref[...] = jnp.where(named, spread, grad.astype(F32)).astype(BF16)
+
+
+def combine_kernel(own_comb_ref, other_comb_ref, ids_ref, place_ref, after_ref, comb_ref):
+    del after_ref
+    comb = own_comb_ref[...] + other_comb_ref[...]
+    comb = jnp.sum(place_ref[...] * comb, axis=0, keepdims=True)
+    comb_ref[...] = jnp.where(ids_ref[...] == 0, comb, 0.0)
 
 
 def on_one(hidden_in, out_grad, expert_ids, route_weight, norm_gain, w_gate_up, w_down):
@@ -441,17 +439,16 @@
         [(row_both.shape, BF16)],
         0,
         4 * cap * wide,
-        in_specs=[IN_VMEM] + [pl.BlockSpec(memory_space=pl.ANY)] * 2,
-    )(row_both, slab_two, down_two)
+        in_specs=[IN_VMEM] + [pl.BlockSpec(memory_space=pl.ANY)],
+    )(row_both, slab_two)
     near = across(passed, 1)
-    slab_near, down_near = call(
-        fetch_kernel,
-        [(slab.shape, BF16), (down.shape, BF16)],
-        FETCH_FLOPS,
-        6 * hidden * width,
-        in_specs=[IN_HBM] * 2 + [pl.BlockSpec(memory_space=pl.ANY)],
-        scratch=[pltpu.SemaphoreType.DMA((2,))],
-    )(in_hbm(slab), in_hbm(down), far_grad)
+    (token,) = call(
+        token_kernel,
+        [((cap, LANES), F32)],
+        TOKEN_FLOPS,
+        0,
+        in_specs=[pl.BlockSpec(memory_space=pl.ANY)],
+    )(far_grad)
     farthest_in = across(far_in, 1)
     farthest_grad = across(far_grad, 1)
     ins = [row_in, far_in, near, farthest_in]
@@ -462,7 +459,7 @@
         [((total_rows // 2, 2 * hidden), F32)] * 2 + [half_rows] * 2,
         0,
         4 * hidden * width,
-    )(*ins, slab_near, slab_two)
+    )(*ins, token, slab, slab_two)
     left_width = -(-3 * hidden // LANES) * LANES
     own_half, other_half, *rest = call(
         hidden_kernel,
@@ -471,7 +468,7 @@
         + [((total_rows // 2, left_width), BF16)] * 2,
         HIDDEN_FLOPS,
         6 * hidden * width,
-    )(*ins, *grads, pre, pre_two, slab_near, down_near, slab_two, down_two)
+    )(*ins, *grads, pre, pre_two, slab, down, slab_two, down_two)
     *grad_halves, left_keep, left_send = rest
     own, other, own_comb, other_comb = call(
         split_kernel,
@@ -482,12 +479,16 @@
     blocks = in_halves + [beside(b) for b in in_halves]
     blocks += grad_halves + [beside(b) for b in grad_halves]
     gate_up_out, down_out = weight_grads(blocks, left_keep, beside(left_send), own, hidden, width)
-    out, combined = call(
-        finish_kernel,
-        [((tokens, width), BF16), ((SPLIT, tokens), F32)],
-        4 * tokens * width * cap,
-        4 * tokens * width,
-    )(handed(other, 2), handed(own, 0), next_grad, across(other_comb, 2), own_comb, ids, place)
+    (out,) = call(
+        finish_kernel, [((tokens, width), BF16)], 4 * tokens * width * cap, 4 * tokens * width
+    )(handed(other, 2), handed(own, 0), next_grad)
+    (combined,) = call(
+        combine_kernel,
+        [((SPLIT, tokens), F32)],
+        0,
+        4 * SPLIT * tokens,
+        in_specs=[IN_VMEM] * 4 + [IN_HBM],
+    )(own_comb, across(other_comb, 2), ids, place, in_hbm(out))
     return (
         out[None],
         gate_up_out.reshape(1, 1, 2, hidden, width),

time: 39.5 us -> 38.7 us (0.980)
  Pallas kernels: 13 us -> 11.3 us
  waiting for transfers between devices: 6.67 us -> 8.08 us
  starting transfers between devices: 18.9 us -> 18.5 us
    pallas_call x2 -> x3, Pallas kernels: 3.89 us -> 2.12 us  [the longest x1 1.51 us: on_one(): call(finish_kernel, [((tokens, width), BF16)], 4 * tokens * width * cap,...]
    ppermute x3, waiting for transfers between devices: 0.01 us -> 0.75 us  [handed(): return lax.ppermute(block, ('pipe', 'expert'), route)]
    ppermute x7, waiting for transfers between devices: 5.95 us -> 6.61 us  [across(): lax.ppermute(block, 'expert', [(i, i ^ 2 * offset) for i in range(devices)])]
    ppermute x7, starting transfers between devices: 9.69 us -> 9.12 us  [across(): lax.ppermute(block, 'expert', [(i, i ^ 2 * offset) for i in range(devices)])]
  transfers between devices with their start and end apart: 17 -> 17, of which waited for: 5 -> 5; matrix products, arithmetic and copies ran while one was open for 0% -> 0% of each run, Pallas kernels for 29% -> 28%
where the time goes in v8:
time: 38.7 us; the launch traced here: 38.5 us
  starting transfers between devices  18.5 us (48%)
  Pallas kernels  11.3 us (29%)
  waiting for transfers between devices  8.08 us (21%)
  between operations  0.74 us (2%)
    ppermute x7, starting transfers between devices, across(): lax.ppermute(block, 'expert', [(i, i ^ 2 * offset) for i in range(devices)])  9.12 us
    ppermute x3, starting transfers between devices, handed(): return lax.ppermute(block, ('pipe', 'expert'), route)  8.05 us
    ppermute x7, waiting for transfers between devices, across(): lax.ppermute(block, 'expert', [(i, i ^ 2 * offset) for i in range(devices)])  6.61 us
    pallas_call x1, Pallas kernels, weight_grads(): pl.pallas_call(functools.partial(weights_kernel, chunks), in_specs=[IN_VM...  2.66 us
    pallas_call x1, Pallas kernels, on_one(): call(hidden_kernel, [((2 * cap, wide), BF16)] * 2 + [half_rows] * 2 + [((...  2.32 us
    pallas_call x1, Pallas kernels, on_one(): call(rows_kernel, [((cap, wide), BF16)] * 2 + [((2 * cap, wide), BF16), (...  2 us
    pallas_call x1, Pallas kernels, on_one(): call(project_kernel, [((total_rows // 2, 2 * hidden), F32)] * 2 + [half_r...  1.93 us
    pallas_call x1, Pallas kernels, on_one(): call(finish_kernel, [((tokens, width), BF16)], 4 * tokens * width * cap,...  1.51 us
  transfers between devices with their start and end apart: 17, of which 5 were waited for; matrix products, arithmetic and copies ran while one was open for 0% of the time, Pallas kernels for 28%

profile of v8, /device:TPU:0, one launch (start us, length us, event | category | flops | bytes accessed | tf_op | source)
XLA Modules:
  0.0 38.5 jit_solution(15179164954180311738)
XLA Ops:
  0.6 0.5 %collective-permute-start.1 = (bf16[384,4096]{1,0:T(8,128)(2,1)}, bf16[384,4096]{1,0:T(8,128)(2,1)S(1)}, u32[]{:S(2)}, u32[]{:S(2)}) collective-permute-start(bf16[384,4096]{1,0:T(8,128)(2,1)} %bitcast.16), channel_id=1, source_target_pairs={{0,1},{1,0},{2,3},{3,2},{4,5},{5,4},{6,7},{7,6},{8,9},{9,8},{10,11... | collective-permute-start | bytes 9437192 | tf_op jit(solution)/shard_map/ppermute | solution.py:407
  1.1 0.1 collective-permute-start.6
  1.2 2.0 %shard_map.102 = (bf16[8,4224]{1,0:T(8,128)(2,1)S(1)}, bf16[8,4224]{1,0:T(8,128)(2,1)S(1)}, bf16[16,4224]{1,0:T(8,128)(2,1)S(1)}, f32[8,4096]{1,0:T(8,128)S(1)}, f32[8,128]{1,0:T(8,128)S(1)}) custom-call(s32[8,128]{1,0:T(8,128)} %bitcast.19, bf16[8,128]{1,0:T(8,128)(2,1)} %bitcast.28, f32[1,4096]{1,0:T(1,128)} %gain_ref.1, bf16[128,4096]{1,0:T(8,128)(2,1)} %bitcast.24, ...), custom_call_target="tpu_custom_call" | custom-call | flops 16777216 | bytes 2097152 | tf_op jit(solution)/shard_map/pallas_call | solution.py:418
  3.2 4.1 %collective-permute-start = (bf16[8,4224]{1,0:T(8,128)(2,1)S(1)}, bf16[8,4224]{1,0:T(8,128)(2,1)S(1)}, u32[]{:S(2)}, u32[]{:S(2)}) collective-permute-start(bf16[8,4224]{1,0:T(8,128)(2,1)S(1)} %get-tuple-element.25.refs_0_.in_ref), channel_id=1, source_target_pairs={{0,4},{1,5},{2,6},{3,7},{4,0},{5,1},{6,2},{7,3},{8,12},{9,13},{10,... | collective-permute-start | bytes 202760 | tf_op jit(solution)/shard_map/ppermute | solution.py:404
  7.3 0.1 collective-permute-start.4
  7.4 2.7 %collective-permute-start.10 = (bf16[128,4096]{1,0:T(8,128)(2,1)}, bf16[128,4096]{1,0:T(8,128)(2,1)S(1)}, u32[]{:S(2)}, u32[]{:S(2)}) collective-permute-start(bf16[128,4096]{1,0:T(8,128)(2,1)} %bitcast.26), channel_id=1, source_target_pairs={{8,0},{9,1},{10,2},{11,3},{12,4},{13,5},{14,6},{15,7},{16,8},{17,9... | collective-permute-start | bytes 3145736 | tf_op jit(solution)/shard_map/ppermute | solution.py:415
  10.1 1.6 %collective-permute-start.2 = (bf16[16,4224]{1,0:T(8,128)(2,1)S(1)}, bf16[16,4224]{1,0:T(8,128)(2,1)S(1)}, u32[]{:S(2)}, u32[]{:S(2)}) collective-permute-start(bf16[16,4224]{1,0:T(8,128)(2,1)S(1)} %shard_map.103), channel_id=1, source_target_pairs={{0,2},{1,3},{2,0},{3,1},{4,6},{5,7},{6,4},{7,5},{8,10},{9,11},{10,... | collective-permute-start | bytes 405512 | tf_op jit(solution)/shard_map/ppermute | solution.py:404
  11.8 1.6 %collective-permute-start.3 = (bf16[8,4224]{1,0:T(8,128)(2,1)S(1)}, bf16[8,4224]{1,0:T(8,128)(2,1)S(1)}, u32[]{:S(2)}, u32[]{:S(2)}) collective-permute-start(bf16[8,4224]{1,0:T(8,128)(2,1)S(1)} %collective-permute-done.refs_1_.far_in_ref), channel_id=1, source_target_pairs={{0,2},{1,3},{2,0},{3,1},{4,6},{5,7},{6,4},{7,5},{8,10},{9,11},{10,... | collective-permute-start | bytes 202760 | tf_op jit(solution)/shard_map/ppermute | solution.py:404
  13.4 0.7 %collective-permute-done.4.after_ref.refs_5_.far_grad_ref = bf16[8,4224]{1,0:T(8,128)(2,1)S(1)} collective-permute-done((bf16[8,4224]{1,0:T(8,128)(2,1)S(1)}, bf16[8,4224]{1,0:T(8,128)(2,1)S(1)}, u32[]{:S(2)}, u32[]{:S(2)}) %collective-permute-start.4) | collective-permute-done | bytes 67616 | tf_op jit(solution)/shard_map/ppermute | solution.py:404
  14.1 0.7 %collective-permute-start.5 = (bf16[8,4224]{1,0:T(8,128)(2,1)S(1)}, bf16[8,4224]{1,0:T(8,128)(2,1)S(1)}, u32[]{:S(2)}, u32[]{:S(2)}) collective-permute-start(bf16[8,4224]{1,0:T(8,128)(2,1)S(1)} %collective-permute-done.4.after_ref.refs_5_.far_grad_ref), channel_id=1, source_target_pairs={{0,2},{1,3},{2,0},{3,1},{4,6},{5,7},{6,4},{7,5},{8,10},{9,11},{10,... | collective-permute-start | bytes 202760 | tf_op jit(solution)/shard_map/ppermute | solution.py:404
  14.8 3.2 %collective-permute-done.3.refs_3_ = bf16[8,4224]{1,0:T(8,128)(2,1)S(1)} collective-permute-done((bf16[8,4224]{1,0:T(8,128)(2,1)S(1)}, bf16[8,4224]{1,0:T(8,128)(2,1)S(1)}, u32[]{:S(2)}, u32[]{:S(2)}) %collective-permute-start.3) | collective-permute-done | bytes 67616 | tf_op jit(solution)/shard_map/ppermute | solution.py:404
  18.0 0.0 collective-permute-done.2.refs_2_.refs_6_
  18.0 1.9 %shard_map.105 = (f32[32,384]{1,0:T(8,128)S(1)}, f32[32,384]{1,0:T(8,128)S(1)}, bf16[16,4096]{1,0:T(8,128)(2,1)S(1)}, bf16[16,4096]{1,0:T(8,128)(2,1)S(1)}) custom-call(bf16[8,4224]{1,0:T(8,128)(2,1)S(1)} %get-tuple-element.25.refs_0_.in_ref, bf16[8,4224]{1,0:T(8,128)(2,1)S(1)} %collective-permute-done.refs_1_.far_in_ref, ...), custom_call_target="tpu_custom_call" | custom-call | bytes 3145728 | tf_op jit(solution)/shard_map/pallas_call | solution.py:457
  19.9 0.0 collective-permute-done.5.refs_7_
  19.9 0.0 collective-permute-done.6.refs_13_
  20.0 0.0 copy-start.1
  20.0 2.3 %shard_map.106 = (bf16[16,4224]{1,0:T(8,128)(2,1)S(1)}, bf16[16,4224]{1,0:T(8,128)(2,1)S(1)}, bf16[16,4096]{1,0:T(8,128)(2,1)S(1)}, bf16[16,4096]{1,0:T(8,128)(2...) custom-call(bf16[8,4224]{1,0:T(8,128)(2,1)S(1)} %get-tuple-element.25.refs_0_.in_ref, ...), custom_call_target="tpu_custom_call" | custom-call | flops 6400000000 | bytes 4718592 | tf_op jit(solution)/shard_map/pallas_call | solution.py:464
  22.3 0.0 copy-start.2
  22.3 1.0 %collective-permute-start.7 = (bf16[16,4224]{1,0:T(8,128)(2,1)S(1)}, bf16[16,4224]{1,0:T(8,128)(2,1)S(1)}, u32[]{:S(2)}, u32[]{:S(2)}) collective-permute-start(bf16[16,4224]{1,0:T(8,128)(2,1)S(1)} %get-tuple-element.31), channel_id=1, source_target_pairs={{0,2},{1,3},{2,0},{3,1},{4,6},{5,7},{6,4},{7,5},{8,10},{9,11},{10,... | collective-permute-start | bytes 405512 | tf_op jit(solution)/shard_map/ppermute | solution.py:404
  23.3 0.0 collective-permute-start.15
  23.3 0.5 %collective-permute-start.13 = (bf16[16,4096]{1,0:T(8,128)(2,1)S(1)}, bf16[16,4096]{1,0:T(8,128)(2,1)S(1)}, u32[]{:S(2)}, u32[]{:S(2)}) collective-permute-start(bf16[16,4096]{1,0:T(8,128)(2,1)S(1)} %get-tuple-element.37.refs_4_), channel_id=1, source_target_pairs={{0,1},{1,0},{2,3},{3,2},{4,5},{5,4},{6,7},{7,6},{8,9},{9,8},{10,11... | collective-permute-start | bytes 393224 | tf_op jit(solution)/shard_map/ppermute | solution.py:407
  23.8 0.7 %collective-permute-done.15.refs_9_ = bf16[32,640]{1,0:T(8,128)(2,1)S(1)} collective-permute-done((bf16[32,640]{1,0:T(8,128)(2,1)S(1)}, bf16[32,640]{1,0:T(8,128)(2,1)S(1)}, u32[]{:S(2)}, u32[]{:S(2)}) %collective-permute-start.15) | collective-permute-done | bytes 40992 | tf_op jit(solution)/shard_map/ppermute | solution.py:407
  24.6 0.2 collective-permute-start.11
  24.7 2.7 %collective-permute-done.7.got_ref = bf16[16,4224]{1,0:T(8,128)(2,1)S(1)} collective-permute-done((bf16[16,4224]{1,0:T(8,128)(2,1)S(1)}, bf16[16,4224]{1,0:T(8,128)(2,1)S(1)}, u32[]{:S(2)}, u32[]{:S(2)}) %collective-permute-start.7) | collective-permute-done | bytes 135200 | tf_op jit(solution)/shard_map/ppermute | solution.py:404
  27.4 0.0 collective-permute-start.12
  27.4 0.2 shard_map.107
  27.6 4.5 %collective-permute-start.8 = (bf16[8,4224]{1,0:T(8,128)(2,1)S(1)}, bf16[8,4224]{1,0:T(8,128)(2,1)S(1)}, u32[]{:S(2)}, u32[]{:S(2)}) collective-permute-start(bf16[8,4224]{1,0:T(8,128)(2,1)S(1)} %get-tuple-element.33), channel_id=1, source_target_pairs={{8,4},{9,5},{10,6},{11,7},{12,0},{13,1},{14,2},{15,3},{16,12},{17,... | collective-permute-start | bytes 202760 | tf_op jit(solution)/shard_map/ppermute | solution.py:415
  32.1 0.8 %collective-permute-start.9 = (bf16[8,4096]{1,0:T(8,128)(2,1)S(1)}, bf16[8,4096]{1,0:T(8,128)(2,1)S(1)}, u32[]{:S(2)}, u32[]{:S(2)}) collective-permute-start(bf16[8,4096]{1,0:T(8,128)(2,1)S(1)} %get-tuple-element.34.refs_10_), channel_id=1, source_target_pairs={{8,0},{9,1},{10,2},{11,3},{12,4},{13,5},{14,6},{15,7},{16,8},{17,9... | collective-permute-start | bytes 196616 | tf_op jit(solution)/shard_map/ppermute | solution.py:415
  33.0 2.7 %shard_map.109 = (bf16[384,4096]{1,0:T(8,128)(2,1)}, bf16[192,4096]{1,0:T(8,128)(2,1)}) custom-call(bf16[16,4096]{1,0:T(8,128)(2,1)S(1)} %get-tuple-element.35.refs_0_, bf16[16,4096]{1,0:T(8,128)(2,1)S(1)} %get-tuple-element.36.refs_1_, bf16[16,4096]{1,0:T(8,128)(2,1)S(1)} %collective-permute-done.11.refs_2_, ...), custom_call_target="tpu_custom_call" | custom-call | flops 301989888 | bytes 4718592 | tf_op jit(solution)/shard_map/pallas_call | solution.py:349
  35.7 0.7 %collective-permute-done.9.own_ref = bf16[8,4096]{1,0:T(8,128)(2,1)S(1)} collective-permute-done((bf16[8,4096]{1,0:T(8,128)(2,1)S(1)}, bf16[8,4096]{1,0:T(8,128)(2,1)S(1)}, u32[]{:S(2)}, u32[]{:S(2)}) %collective-permute-start.9) | collective-permute-done | bytes 65568 | tf_op jit(solution)/shard_map/ppermute | solution.py:415
  36.4 1.5 %shard_map.108.after_ref = bf16[128,4096]{1,0:T(8,128)(2,1)} custom-call(bf16[8,4224]{1,0:T(8,128)(2,1)S(1)} %collective-permute-done.8.other_ref, bf16[8,4096]{1,0:T(8,128)(2,1)S(1)} %collective-permute-done.9.own_ref, bf16[128,4096]{1,0:T(8,128)(2,1)S(1)} %collective-permute-done.10.grad_ref), custom_call_target="tpu_custom_call" | custom-call | flops 16777216 | bytes 2097152 | tf_op jit(solution)/shard_map/pallas_call | solution.py:482
  37.9 0.6 %shard_map.110 = f32[8,128]{1,0:T(8,128)} custom-call(f32[8,128]{1,0:T(8,128)S(1)} %get-tuple-element.43.own_comb_ref, f32[8,128]{1,0:T(8,128)S(1)} %collective-permute-done.16.other_comb_ref, s32[8,128]{1,0:T(8,128)S(1)} %bitcast.20, f32[8,128]{1,0:T(8,128)S(1)} %get-tuple-element.45.place_ref, bf16[128,4096]{1,0:T(8,128)(2,1)} %shard_map.108.after_ref), custom_call_target="tpu_custom_call" | custom-call | bytes 4096 | tf_op jit(solution)/shard_map/pallas_call | solution.py:485
  (19 shorter events, 0.1 us)
Async XLA Ops:
  0.6 9.5 %collective-permute-start.1 = (bf16[384,4096]{1,0:T(8,128)(2,1)}, bf16[384,4096]{1,0:T(8,128)(2,1)S(1)}, u32[]{:S(2)}, u32[]{:S(2)}) collective-permute-start(bf16[384,4096]{1,0:T(8,128)(2,1)} %bitcast.16), channel_id=1, source_target_pairs={{0,1},{1,0},{2,3},{3,2},{4,5},{5,4},{6,7},{7,6},{8,9},{9,8},{10,11... | collective-permute-start | bytes 9437192 | tf_op jit(solution)/shard_map/ppermute | solution.py:407
  1.1 18.8 %collective-permute-start.6 = (bf16[192,4096]{1,0:T(8,128)(2,1)}, bf16[192,4096]{1,0:T(8,128)(2,1)S(1)}, u32[]{:S(2)}, u32[]{:S(2)}) collective-permute-start(bf16[192,4096]{1,0:T(8,128)(2,1)} %bitcast.21), channel_id=1, source_target_pairs={{0,1},{1,0},{2,3},{3,2},{4,5},{5,4},{6,7},{7,6},{8,9},{9,8},{10,11... | collective-permute-start | bytes 4718600 | tf_op jit(solution)/shard_map/ppermute | solution.py:407
  3.2 8.5 %collective-permute-start = (bf16[8,4224]{1,0:T(8,128)(2,1)S(1)}, bf16[8,4224]{1,0:T(8,128)(2,1)S(1)}, u32[]{:S(2)}, u32[]{:S(2)}) collective-permute-start(bf16[8,4224]{1,0:T(8,128)(2,1)S(1)} %get-tuple-element.25.refs_0_.in_ref), channel_id=1, source_target_pairs={{0,4},{1,5},{2,6},{3,7},{4,0},{5,1},{6,2},{7,3},{8,12},{9,13},{10,... | collective-permute-start | bytes 202760 | tf_op jit(solution)/shard_map/ppermute | solution.py:404
  7.3 6.8 %collective-permute-start.4 = (bf16[8,4224]{1,0:T(8,128)(2,1)S(1)}, bf16[8,4224]{1,0:T(8,128)(2,1)S(1)}, u32[]{:S(2)}, u32[]{:S(2)}) collective-permute-start(bf16[8,4224]{1,0:T(8,128)(2,1)S(1)} %get-tuple-element.27.refs_4_), channel_id=1, source_target_pairs={{0,4},{1,5},{2,6},{3,7},{4,0},{5,1},{6,2},{7,3},{8,12},{9,13},{10,... | collective-permute-start | bytes 202760 | tf_op jit(solution)/shard_map/ppermute | solution.py:404
  7.4 28.3 %collective-permute-start.10 = (bf16[128,4096]{1,0:T(8,128)(2,1)}, bf16[128,4096]{1,0:T(8,128)(2,1)S(1)}, u32[]{:S(2)}, u32[]{:S(2)}) collective-permute-start(bf16[128,4096]{1,0:T(8,128)(2,1)} %bitcast.26), channel_id=1, source_target_pairs={{8,0},{9,1},{10,2},{11,3},{12,4},{13,5},{14,6},{15,7},{16,8},{17,9... | collective-permute-start | bytes 3145736 | tf_op jit(solution)/shard_map/ppermute | solution.py:415
  10.1 7.9 %copy-start = (bf16[1,1,2,192,4096]{4,3,2,1,0:T(8,128)(2,1)S(1)}, bf16[1,1,2,192,4096]{4,3,2,1,0:T(8,128)(2,1)}, u32[]{:S(2)}) copy-start(bf16[1,1,2,192,4096]{4,3,2,1,0:T(8,128)(2,1)} %param.12) | copy-start | bytes 9437188
  10.1 7.9 %collective-permute-start.2 = (bf16[16,4224]{1,0:T(8,128)(2,1)S(1)}, bf16[16,4224]{1,0:T(8,128)(2,1)S(1)}, u32[]{:S(2)}, u32[]{:S(2)}) collective-permute-start(bf16[16,4224]{1,0:T(8,128)(2,1)S(1)} %shard_map.103), channel_id=1, source_target_pairs={{0,2},{1,3},{2,0},{3,1},{4,6},{5,7},{6,4},{7,5},{8,10},{9,11},{10,... | collective-permute-start | bytes 405512 | tf_op jit(solution)/shard_map/ppermute | solution.py:404
  11.8 6.2 %collective-permute-start.3 = (bf16[8,4224]{1,0:T(8,128)(2,1)S(1)}, bf16[8,4224]{1,0:T(8,128)(2,1)S(1)}, u32[]{:S(2)}, u32[]{:S(2)}) collective-permute-start(bf16[8,4224]{1,0:T(8,128)(2,1)S(1)} %collective-permute-done.refs_1_.far_in_ref), channel_id=1, source_target_pairs={{0,2},{1,3},{2,0},{3,1},{4,6},{5,7},{6,4},{7,5},{8,10},{9,11},{10,... | collective-permute-start | bytes 202760 | tf_op jit(solution)/shard_map/ppermute | solution.py:404
  14.1 5.8 %collective-permute-start.5 = (bf16[8,4224]{1,0:T(8,128)(2,1)S(1)}, bf16[8,4224]{1,0:T(8,128)(2,1)S(1)}, u32[]{:S(2)}, u32[]{:S(2)}) collective-permute-start(bf16[8,4224]{1,0:T(8,128)(2,1)S(1)} %collective-permute-done.4.after_ref.refs_5_.far_grad_ref), channel_id=1, source_target_pairs={{0,2},{1,3},{2,0},{3,1},{4,6},{5,7},{6,4},{7,5},{8,10},{9,11},{10,... | collective-permute-start | bytes 202760 | tf_op jit(solution)/shard_map/ppermute | solution.py:404
  14.8 5.1 %copy-start.3 = (bf16[1,1,192,4096]{3,2,1,0:T(8,128)(2,1)S(1)}, bf16[1,1,192,4096]{3,2,1,0:T(8,128)(2,1)}, u32[]{:S(2)}) copy-start(bf16[1,1,192,4096]{3,2,1,0:T(8,128)(2,1)} %param.13) | copy-start | bytes 4718596
  20.0 7.4 %copy-start.1 = (f32[1,4096]{1,0:T(1,128)S(1)}, f32[1,4096]{1,0:T(1,128)}, u32[]{:S(2)}) copy-start(f32[1,4096]{1,0:T(1,128)} %gain_ref.1) | copy-start | bytes 49156
  22.3 15.6 %copy-start.2 = (s32[1,128,8]{1,2,0:T(8,128)S(1)}, s32[1,128,8]{1,2,0:T(8,128)}, u32[]{:S(2)}) copy-start(s32[1,128,8]{1,2,0:T(8,128)} %param.9) | copy-start | bytes 12292
  22.3 5.1 %collective-permute-start.7 = (bf16[16,4224]{1,0:T(8,128)(2,1)S(1)}, bf16[16,4224]{1,0:T(8,128)(2,1)S(1)}, u32[]{:S(2)}, u32[]{:S(2)}) collective-permute-start(bf16[16,4224]{1,0:T(8,128)(2,1)S(1)} %get-tuple-element.31), channel_id=1, source_target_pairs={{0,2},{1,3},{2,0},{3,1},{4,6},{5,7},{6,4},{7,5},{8,10},{9,11},{10,... | collective-permute-start | bytes 405512 | tf_op jit(solution)/shard_map/ppermute | solution.py:404
  23.3 1.2 %collective-permute-start.15 = (bf16[32,640]{1,0:T(8,128)(2,1)S(1)}, bf16[32,640]{1,0:T(8,128)(2,1)S(1)}, u32[]{:S(2)}, u32[]{:S(2)}) collective-permute-start(bf16[32,640]{1,0:T(8,128)(2,1)S(1)} %get-tuple-element.40), channel_id=1, source_target_pairs={{0,1},{1,0},{2,3},{3,2},{4,5},{5,4},{6,7},{7,6},{8,9},{9,8},{10,11... | collective-permute-start | bytes 122888 | tf_op jit(solution)/shard_map/ppermute | solution.py:407
  23.3 4.3 %collective-permute-start.13 = (bf16[16,4096]{1,0:T(8,128)(2,1)S(1)}, bf16[16,4096]{1,0:T(8,128)(2,1)S(1)}, u32[]{:S(2)}, u32[]{:S(2)}) collective-permute-start(bf16[16,4096]{1,0:T(8,128)(2,1)S(1)} %get-tuple-element.37.refs_4_), channel_id=1, source_target_pairs={{0,1},{1,0},{2,3},{3,2},{4,5},{5,4},{6,7},{7,6},{8,9},{9,8},{10,11... | collective-permute-start | bytes 393224 | tf_op jit(solution)/shard_map/ppermute | solution.py:407
  23.8 8.3 %collective-permute-start.14 = (bf16[16,4096]{1,0:T(8,128)(2,1)S(1)}, bf16[16,4096]{1,0:T(8,128)(2,1)S(1)}, u32[]{:S(2)}, u32[]{:S(2)}) collective-permute-start(bf16[16,4096]{1,0:T(8,128)(2,1)S(1)} %get-tuple-element.38.refs_5_), channel_id=1, source_target_pairs={{0,1},{1,0},{2,3},{3,2},{4,5},{5,4},{6,7},{7,6},{8,9},{9,8},{10,11... | collective-permute-start | bytes 393224 | tf_op jit(solution)/shard_map/ppermute | solution.py:407
  24.6 8.4 %collective-permute-start.11 = (bf16[16,4096]{1,0:T(8,128)(2,1)S(1)}, bf16[16,4096]{1,0:T(8,128)(2,1)S(1)}, u32[]{:S(2)}, u32[]{:S(2)}) collective-permute-start(bf16[16,4096]{1,0:T(8,128)(2,1)S(1)} %get-tuple-element.35.refs_0_), channel_id=1, source_target_pairs={{0,1},{1,0},{2,3},{3,2},{4,5},{5,4},{6,7},{7,6},{8,9},{9,8},{10,11... | collective-permute-start | bytes 393224 | tf_op jit(solution)/shard_map/ppermute | solution.py:407
  27.4 5.6 %collective-permute-start.12 = (bf16[16,4096]{1,0:T(8,128)(2,1)S(1)}, bf16[16,4096]{1,0:T(8,128)(2,1)S(1)}, u32[]{:S(2)}, u32[]{:S(2)}) collective-permute-start(bf16[16,4096]{1,0:T(8,128)(2,1)S(1)} %get-tuple-element.36.refs_1_), channel_id=1, source_target_pairs={{0,1},{1,0},{2,3},{3,2},{4,5},{5,4},{6,7},{7,6},{8,9},{9,8},{10,11... | collective-permute-start | bytes 393224 | tf_op jit(solution)/shard_map/ppermute | solution.py:407
  27.6 8.8 %collective-permute-start.8 = (bf16[8,4224]{1,0:T(8,128)(2,1)S(1)}, bf16[8,4224]{1,0:T(8,128)(2,1)S(1)}, u32[]{:S(2)}, u32[]{:S(2)}) collective-permute-start(bf16[8,4224]{1,0:T(8,128)(2,1)S(1)} %get-tuple-element.33), channel_id=1, source_target_pairs={{8,4},{9,5},{10,6},{11,7},{12,0},{13,1},{14,2},{15,3},{16,12},{17,... | collective-permute-start | bytes 202760 | tf_op jit(solution)/shard_map/ppermute | solution.py:415
  32.1 4.3 %collective-permute-start.9 = (bf16[8,4096]{1,0:T(8,128)(2,1)S(1)}, bf16[8,4096]{1,0:T(8,128)(2,1)S(1)}, u32[]{:S(2)}, u32[]{:S(2)}) collective-permute-start(bf16[8,4096]{1,0:T(8,128)(2,1)S(1)} %get-tuple-element.34.refs_10_), channel_id=1, source_target_pairs={{8,0},{9,1},{10,2},{11,3},{12,4},{13,5},{14,6},{15,7},{16,8},{17,9... | collective-permute-start | bytes 196616 | tf_op jit(solution)/shard_map/ppermute | solution.py:415
  33.0 5.0 %collective-permute-start.16 = (f32[8,128]{1,0:T(8,128)S(1)}, f32[8,128]{1,0:T(8,128)S(1)}, u32[]{:S(2)}, u32[]{:S(2)}) collective-permute-start(f32[8,128]{1,0:T(8,128)S(1)} %get-tuple-element.44), channel_id=1, source_target_pairs={{0,4},{1,5},{2,6},{3,7},{4,0},{5,1},{6,2},{7,3},{8,12},{9,13},{10,... | collective-permute-start | bytes 12296 | tf_op jit(solution)/shard_map/ppermute | solution.py:404

commit v9 on v8

--- a/solution.py
+++ b/solution.py
@@ -172,8 +172,8 @@
     return high, middle, values - high - middle
 
 
-def rows_kernel(ids_hbm, weight_hbm, gain_hbm, hidden_hbm, grad_hbm, in_ref, out_ref, both_ref,
-                normed_ref, place_ref, ids_ref, weight_ref, gain_ref, hidden_ref, grad_ref, sems):
+def rows_kernel(ids_hbm, weight_ref, gain_hbm, hidden_hbm, grad_hbm, in_ref, out_ref, both_ref,
+                normed_ref, place_ref, ids_ref, gain_ref, hidden_ref, grad_ref, sems):
     tokens, width = hidden_ref.shape
     cap = SPECIALIST_CAP
     copies = [
@@ -182,7 +182,6 @@
             (ids_hbm, ids_ref),
             (hidden_hbm, hidden_ref),
             (gain_hbm, gain_ref),
-            (weight_hbm, weight_ref),
             (grad_hbm, grad_ref),
         ])
     ]
@@ -205,7 +204,6 @@
     copies[2].wait()
     normed_in = normed * gain_ref[...]
     in_ref[:, :width] = normed_in.astype(BF16)
-    copies[3].wait()
     weight = jnp.sum(
         jnp.where(hit, weight_ref[...].astype(F32), 0.0), axis=0, keepdims=True
     )
@@ -217,7 +215,7 @@
     in_ref[:, width:] = extra.astype(BF16)
     out_ref[:, width:] = place.astype(BF16)
     both_ref[:, width:] = jnp.concatenate([extra, place], axis=0).astype(BF16)
-    copies[4].wait()
+    copies[3].wait()
     grad = take_rows(place.astype(BF16), grad_ref[...])
     out_ref[:, :width] = grad.astype(BF16)
     both_ref[:, :width] = jnp.concatenate([normed_in, grad], axis=0).astype(BF16)
@@ -421,16 +419,15 @@
         + [((2 * cap, wide), BF16), ((cap, width), F32), ((cap, tokens), F32)],
         4 * tokens * width * cap,
         4 * tokens * width,
-        in_specs=[IN_HBM] * 5,
+        in_specs=[IN_HBM, IN_VMEM] + [IN_HBM] * 3,
         scratch=[
             pltpu.VMEM(ids.shape, ids.dtype),
-            pltpu.VMEM(weights.shape, weights.dtype),
             pltpu.VMEM(norm_gain.shape, norm_gain.dtype),
             pltpu.VMEM((tokens, width), BF16),
             pltpu.VMEM((tokens, width), BF16),
-            pltpu.SemaphoreType.DMA((5,)),
+            pltpu.SemaphoreType.DMA((4,)),
         ],
-    )(*map(in_hbm, (ids, weights, norm_gain, hidden_in[0], out_grad[0])))
+    )(in_hbm(ids), weights, *map(in_hbm, (norm_gain, hidden_in[0], out_grad[0])))
     far_in = across(row_in, 2)
     far_grad = across(row_grad, 2)
     slab_two, down_two = beside(slab), beside(down)

time: 38.7 us -> 39.3 us (1.016)
  local copies, waits for them, and re-layouts: 0.02 us -> 0.7 us
    unnamed x8 -> x10, local copies, waits for them, and re-layouts: 0.02 us -> 0.7 us
  transfers between devices with their start and end apart: 17 -> 17, of which waited for: 5 -> 5; matrix products, arithmetic and copies ran while one was open for 0% -> 0% of each run, Pallas kernels for 28% -> 27%
where the time goes in v9:
time: 39.3 us; the launch traced here: 39.1 us
  starting transfers between devices  18.5 us (47%)
  Pallas kernels  11.2 us (28%)
  waiting for transfers between devices  7.96 us (20%)
  between operations  0.74 us (2%)
  local copies, waits for them, and re-layouts  0.7 us (2%)
    ppermute x7, starting transfers between devices, across(): lax.ppermute(block, 'expert', [(i, i ^ 2 * offset) for i in range(devices)])  9.12 us
    ppermute x3, starting transfers between devices, handed(): return lax.ppermute(block, ('pipe', 'expert'), route)  8.05 us
    ppermute x7, waiting for transfers between devices, across(): lax.ppermute(block, 'expert', [(i, i ^ 2 * offset) for i in range(devices)])  6.61 us
    pallas_call x1, Pallas kernels, weight_grads(): pl.pallas_call(functools.partial(weights_kernel, chunks), in_specs=[IN_VM...  2.66 us
    pallas_call x1, Pallas kernels, on_one(): call(hidden_kernel, [((2 * cap, wide), BF16)] * 2 + [half_rows] * 2 + [((...  2.32 us
    pallas_call x1, Pallas kernels, on_one(): call(rows_kernel, [((cap, wide), BF16)] * 2 + [((2 * cap, wide), BF16), (...  1.98 us
    pallas_call x1, Pallas kernels, on_one(): call(project_kernel, [((total_rows // 2, 2 * hidden), F32)] * 2 + [half_r...  1.93 us
    pallas_call x1, Pallas kernels, on_one(): call(finish_kernel, [((tokens, width), BF16)], 4 * tokens * width * cap,...  1.51 us
  transfers between devices with their start and end apart: 17, of which 5 were waited for; matrix products, arithmetic and copies ran while one was open for 0% of the time, Pallas kernels for 27%

profile of v9, /device:TPU:0, one launch (start us, length us, event | category | flops | bytes accessed | tf_op | source)
XLA Modules:
  0.0 39.1 jit_solution(7229761916233671304)
XLA Ops:
  0.6 0.5 %collective-permute-start.1 = (bf16[384,4096]{1,0:T(8,128)(2,1)}, bf16[384,4096]{1,0:T(8,128)(2,1)S(1)}, u32[]{:S(2)}, u32[]{:S(2)}) collective-permute-start(bf16[384,4096]{1,0:T(8,128)(2,1)} %bitcast.16), channel_id=1, source_target_pairs={{0,1},{1,0},{2,3},{3,2},{4,5},{5,4},{6,7},{7,6},{8,9},{9,8},{10,11... | collective-permute-start | bytes 9437192 | tf_op jit(solution)/shard_map/ppermute | solution.py:405
  1.1 0.1 collective-permute-start.6
  1.2 0.7 %copy-done.3 = bf16[1,128,8]{1,2,0:T(8,128)(2,1)S(1)} copy-done((bf16[1,128,8]{1,2,0:T(8,128)(2,1)S(1)}, bf16[1,128,8]{1,2,0:T(8,128)(2,1)}, u32[]{:S(2)}) %copy-start.3) | copy-done | bytes 2072
  1.9 2.0 %shard_map.102 = (bf16[8,4224]{1,0:T(8,128)(2,1)S(1)}, bf16[8,4224]{1,0:T(8,128)(2,1)S(1)}, bf16[16,4224]{1,0:T(8,128)(2,1)S(1)}, f32[8,4096]{1,0:T(8,128)S(1)}, f32[8,128]{1,0:T(8,128)S(1)}) custom-call(s32[8,128]{1,0:T(8,128)} %bitcast.19, bf16[8,128]{1,0:T(8,128)(2,1)S(1)} %bitcast.21, f32[1,4096]{1,0:T(1,128)} %gain_ref.1, bf16[128,4096]{1,0:T(8,128)(2,1)} %bitcast.25, ...), custom_call_target="tpu_custom_call" | custom-call | flops 16777216 | bytes 2097152 | tf_op jit(solution)/shard_map/pallas_call | solution.py:416
  3.9 4.1 %collective-permute-start = (bf16[8,4224]{1,0:T(8,128)(2,1)S(1)}, bf16[8,4224]{1,0:T(8,128)(2,1)S(1)}, u32[]{:S(2)}, u32[]{:S(2)}) collective-permute-start(bf16[8,4224]{1,0:T(8,128)(2,1)S(1)} %get-tuple-element.25.refs_0_.in_ref), channel_id=1, source_target_pairs={{0,4},{1,5},{2,6},{3,7},{4,0},{5,1},{6,2},{7,3},{8,12},{9,13},{10,... | collective-permute-start | bytes 202760 | tf_op jit(solution)/shard_map/ppermute | solution.py:402
  8.0 0.1 collective-permute-start.4
  8.1 2.7 %collective-permute-start.10 = (bf16[128,4096]{1,0:T(8,128)(2,1)}, bf16[128,4096]{1,0:T(8,128)(2,1)S(1)}, u32[]{:S(2)}, u32[]{:S(2)}) collective-permute-start(bf16[128,4096]{1,0:T(8,128)(2,1)} %bitcast.27), channel_id=1, source_target_pairs={{8,0},{9,1},{10,2},{11,3},{12,4},{13,5},{14,6},{15,7},{16,8},{17,9... | collective-permute-start | bytes 3145736 | tf_op jit(solution)/shard_map/ppermute | solution.py:413
  10.8 1.6 %collective-permute-start.2 = (bf16[16,4224]{1,0:T(8,128)(2,1)S(1)}, bf16[16,4224]{1,0:T(8,128)(2,1)S(1)}, u32[]{:S(2)}, u32[]{:S(2)}) collective-permute-start(bf16[16,4224]{1,0:T(8,128)(2,1)S(1)} %shard_map.103), channel_id=1, source_target_pairs={{0,2},{1,3},{2,0},{3,1},{4,6},{5,7},{6,4},{7,5},{8,10},{9,11},{10,... | collective-permute-start | bytes 405512 | tf_op jit(solution)/shard_map/ppermute | solution.py:402
  12.4 1.6 %collective-permute-start.3 = (bf16[8,4224]{1,0:T(8,128)(2,1)S(1)}, bf16[8,4224]{1,0:T(8,128)(2,1)S(1)}, u32[]{:S(2)}, u32[]{:S(2)}) collective-permute-start(bf16[8,4224]{1,0:T(8,128)(2,1)S(1)} %collective-permute-done.refs_1_.far_in_ref), channel_id=1, source_target_pairs={{0,2},{1,3},{2,0},{3,1},{4,6},{5,7},{6,4},{7,5},{8,10},{9,11},{10,... | collective-permute-start | bytes 202760 | tf_op jit(solution)/shard_map/ppermute | solution.py:402
  14.1 0.7 %collective-permute-done.4.after_ref.refs_5_.far_grad_ref = bf16[8,4224]{1,0:T(8,128)(2,1)S(1)} collective-permute-done((bf16[8,4224]{1,0:T(8,128)(2,1)S(1)}, bf16[8,4224]{1,0:T(8,128)(2,1)S(1)}, u32[]{:S(2)}, u32[]{:S(2)}) %collective-permute-start.4) | collective-permute-done | bytes 67616 | tf_op jit(solution)/shard_map/ppermute | solution.py:402
  14.8 0.7 %collective-permute-start.5 = (bf16[8,4224]{1,0:T(8,128)(2,1)S(1)}, bf16[8,4224]{1,0:T(8,128)(2,1)S(1)}, u32[]{:S(2)}, u32[]{:S(2)}) collective-permute-start(bf16[8,4224]{1,0:T(8,128)(2,1)S(1)} %collective-permute-done.4.after_ref.refs_5_.far_grad_ref), channel_id=1, source_target_pairs={{0,2},{1,3},{2,0},{3,1},{4,6},{5,7},{6,4},{7,5},{8,10},{9,11},{10,... | collective-permute-start | bytes 202760 | tf_op jit(solution)/shard_map/ppermute | solution.py:402
  15.5 3.2 %collective-permute-done.3.refs_3_ = bf16[8,4224]{1,0:T(8,128)(2,1)S(1)} collective-permute-done((bf16[8,4224]{1,0:T(8,128)(2,1)S(1)}, bf16[8,4224]{1,0:T(8,128)(2,1)S(1)}, u32[]{:S(2)}, u32[]{:S(2)}) %collective-permute-start.3) | collective-permute-done | bytes 67616 | tf_op jit(solution)/shard_map/ppermute | solution.py:402
  18.7 1.9 %shard_map.105 = (f32[32,384]{1,0:T(8,128)S(1)}, f32[32,384]{1,0:T(8,128)S(1)}, bf16[16,4096]{1,0:T(8,128)(2,1)S(1)}, bf16[16,4096]{1,0:T(8,128)(2,1)S(1)}) custom-call(bf16[8,4224]{1,0:T(8,128)(2,1)S(1)} %get-tuple-element.25.refs_0_.in_ref, bf16[8,4224]{1,0:T(8,128)(2,1)S(1)} %collective-permute-done.refs_1_.far_in_ref, ...), custom_call_target="tpu_custom_call" | custom-call | bytes 3145728 | tf_op jit(solution)/shard_map/pallas_call | solution.py:454
  20.6 0.0 collective-permute-done.5.refs_7_
  20.6 0.0 collective-permute-done.6.refs_13_
  20.6 0.0 copy-start.1
  20.6 2.3 %shard_map.106 = (bf16[16,4224]{1,0:T(8,128)(2,1)S(1)}, bf16[16,4224]{1,0:T(8,128)(2,1)S(1)}, bf16[16,4096]{1,0:T(8,128)(2,1)S(1)}, bf16[16,4096]{1,0:T(8,128)(2...) custom-call(bf16[8,4224]{1,0:T(8,128)(2,1)S(1)} %get-tuple-element.25.refs_0_.in_ref, ...), custom_call_target="tpu_custom_call" | custom-call | flops 6400000000 | bytes 4718592 | tf_op jit(solution)/shard_map/pallas_call | solution.py:461
  23.0 0.0 copy-start.2
  23.0 1.0 %collective-permute-start.7 = (bf16[16,4224]{1,0:T(8,128)(2,1)S(1)}, bf16[16,4224]{1,0:T(8,128)(2,1)S(1)}, u32[]{:S(2)}, u32[]{:S(2)}) collective-permute-start(bf16[16,4224]{1,0:T(8,128)(2,1)S(1)} %get-tuple-element.31), channel_id=1, source_target_pairs={{0,2},{1,3},{2,0},{3,1},{4,6},{5,7},{6,4},{7,5},{8,10},{9,11},{10,... | collective-permute-start | bytes 405512 | tf_op jit(solution)/shard_map/ppermute | solution.py:402
  24.0 0.0 collective-permute-start.15
  24.0 0.5 %collective-permute-start.13 = (bf16[16,4096]{1,0:T(8,128)(2,1)S(1)}, bf16[16,4096]{1,0:T(8,128)(2,1)S(1)}, u32[]{:S(2)}, u32[]{:S(2)}) collective-permute-start(bf16[16,4096]{1,0:T(8,128)(2,1)S(1)} %get-tuple-element.37.refs_4_), channel_id=1, source_target_pairs={{0,1},{1,0},{2,3},{3,2},{4,5},{5,4},{6,7},{7,6},{8,9},{9,8},{10,11... | collective-permute-start | bytes 393224 | tf_op jit(solution)/shard_map/ppermute | solution.py:405
  24.5 0.7 %collective-permute-done.15.refs_9_ = bf16[32,640]{1,0:T(8,128)(2,1)S(1)} collective-permute-done((bf16[32,640]{1,0:T(8,128)(2,1)S(1)}, bf16[32,640]{1,0:T(8,128)(2,1)S(1)}, u32[]{:S(2)}, u32[]{:S(2)}) %collective-permute-start.15) | collective-permute-done | bytes 40992 | tf_op jit(solution)/shard_map/ppermute | solution.py:405
  25.2 0.2 collective-permute-start.11
  25.4 2.7 %collective-permute-done.7.got_ref = bf16[16,4224]{1,0:T(8,128)(2,1)S(1)} collective-permute-done((bf16[16,4224]{1,0:T(8,128)(2,1)S(1)}, bf16[16,4224]{1,0:T(8,128)(2,1)S(1)}, u32[]{:S(2)}, u32[]{:S(2)}) %collective-permute-start.7) | collective-permute-done | bytes 135200 | tf_op jit(solution)/shard_map/ppermute | solution.py:402
  28.0 0.0 collective-permute-start.12
  28.1 0.2 shard_map.107
  28.3 4.0 %collective-permute-start.8 = (bf16[8,4224]{1,0:T(8,128)(2,1)S(1)}, bf16[8,4224]{1,0:T(8,128)(2,1)S(1)}, u32[]{:S(2)}, u32[]{:S(2)}) collective-permute-start(bf16[8,4224]{1,0:T(8,128)(2,1)S(1)} %get-tuple-element.33), channel_id=1, source_target_pairs={{8,4},{9,5},{10,6},{11,7},{12,0},{13,1},{14,2},{15,3},{16,12},{17,... | collective-permute-start | bytes 202760 | tf_op jit(solution)/shard_map/ppermute | solution.py:413
  32.3 1.3 %collective-permute-start.9 = (bf16[8,4096]{1,0:T(8,128)(2,1)S(1)}, bf16[8,4096]{1,0:T(8,128)(2,1)S(1)}, u32[]{:S(2)}, u32[]{:S(2)}) collective-permute-start(bf16[8,4096]{1,0:T(8,128)(2,1)S(1)} %get-tuple-element.34.refs_10_), channel_id=1, source_target_pairs={{8,0},{9,1},{10,2},{11,3},{12,4},{13,5},{14,6},{15,7},{16,8},{17,9... | collective-permute-start | bytes 196616 | tf_op jit(solution)/shard_map/ppermute | solution.py:413
  33.7 2.7 %shard_map.109 = (bf16[384,4096]{1,0:T(8,128)(2,1)}, bf16[192,4096]{1,0:T(8,128)(2,1)}) custom-call(bf16[16,4096]{1,0:T(8,128)(2,1)S(1)} %get-tuple-element.35.refs_0_, bf16[16,4096]{1,0:T(8,128)(2,1)S(1)} %get-tuple-element.36.refs_1_, bf16[16,4096]{1,0:T(8,128)(2,1)S(1)} %collective-permute-done.11.refs_2_, ...), custom_call_target="tpu_custom_call" | custom-call | flops 301989888 | bytes 4718592 | tf_op jit(solution)/shard_map/pallas_call | solution.py:347
  36.3 0.6 %collective-permute-done.9.own_ref = bf16[8,4096]{1,0:T(8,128)(2,1)S(1)} collective-permute-done((bf16[8,4096]{1,0:T(8,128)(2,1)S(1)}, bf16[8,4096]{1,0:T(8,128)(2,1)S(1)}, u32[]{:S(2)}, u32[]{:S(2)}) %collective-permute-start.9) | collective-permute-done | bytes 65568 | tf_op jit(solution)/shard_map/ppermute | solution.py:413
  37.0 1.5 %shard_map.108.after_ref = bf16[128,4096]{1,0:T(8,128)(2,1)} custom-call(bf16[8,4224]{1,0:T(8,128)(2,1)S(1)} %collective-permute-done.8.other_ref, bf16[8,4096]{1,0:T(8,128)(2,1)S(1)} %collective-permute-done.9.own_ref, bf16[128,4096]{1,0:T(8,128)(2,1)S(1)} %collective-permute-done.10.grad_ref), custom_call_target="tpu_custom_call" | custom-call | flops 16777216 | bytes 2097152 | tf_op jit(solution)/shard_map/pallas_call | solution.py:479
  38.5 0.6 %shard_map.110 = f32[8,128]{1,0:T(8,128)} custom-call(f32[8,128]{1,0:T(8,128)S(1)} %get-tuple-element.43.own_comb_ref, f32[8,128]{1,0:T(8,128)S(1)} %collective-permute-done.16.other_comb_ref, s32[8,128]{1,0:T(8,128)S(1)} %bitcast.20, f32[8,128]{1,0:T(8,128)S(1)} %get-tuple-element.45.place_ref, bf16[128,4096]{1,0:T(8,128)(2,1)} %shard_map.108.after_ref), custom_call_target="tpu_custom_call" | custom-call | bytes 4096 | tf_op jit(solution)/shard_map/pallas_call | solution.py:482
  (21 shorter events, 0.1 us)
Async XLA Ops:
  0.6 10.1 %collective-permute-start.1 = (bf16[384,4096]{1,0:T(8,128)(2,1)}, bf16[384,4096]{1,0:T(8,128)(2,1)S(1)}, u32[]{:S(2)}, u32[]{:S(2)}) collective-permute-start(bf16[384,4096]{1,0:T(8,128)(2,1)} %bitcast.16), channel_id=1, source_target_pairs={{0,1},{1,0},{2,3},{3,2},{4,5},{5,4},{6,7},{7,6},{8,9},{9,8},{10,11... | collective-permute-start | bytes 9437192 | tf_op jit(solution)/shard_map/ppermute | solution.py:405
  1.1 19.5 %collective-permute-start.6 = (bf16[192,4096]{1,0:T(8,128)(2,1)}, bf16[192,4096]{1,0:T(8,128)(2,1)S(1)}, u32[]{:S(2)}, u32[]{:S(2)}) collective-permute-start(bf16[192,4096]{1,0:T(8,128)(2,1)} %bitcast.22), channel_id=1, source_target_pairs={{0,1},{1,0},{2,3},{3,2},{4,5},{5,4},{6,7},{7,6},{8,9},{9,8},{10,11... | collective-permute-start | bytes 4718600 | tf_op jit(solution)/shard_map/ppermute | solution.py:405
  1.2 0.7 %copy-start.3 = (bf16[1,128,8]{1,2,0:T(8,128)(2,1)S(1)}, bf16[1,128,8]{1,2,0:T(8,128)(2,1)}, u32[]{:S(2)}) copy-start(bf16[1,128,8]{1,2,0:T(8,128)(2,1)} %param.10) | copy-start | bytes 6148
  3.9 8.5 %collective-permute-start = (bf16[8,4224]{1,0:T(8,128)(2,1)S(1)}, bf16[8,4224]{1,0:T(8,128)(2,1)S(1)}, u32[]{:S(2)}, u32[]{:S(2)}) collective-permute-start(bf16[8,4224]{1,0:T(8,128)(2,1)S(1)} %get-tuple-element.25.refs_0_.in_ref), channel_id=1, source_target_pairs={{0,4},{1,5},{2,6},{3,7},{4,0},{5,1},{6,2},{7,3},{8,12},{9,13},{10,... | collective-permute-start | bytes 202760 | tf_op jit(solution)/shard_map/ppermute | solution.py:402
  8.0 6.8 %collective-permute-start.4 = (bf16[8,4224]{1,0:T(8,128)(2,1)S(1)}, bf16[8,4224]{1,0:T(8,128)(2,1)S(1)}, u32[]{:S(2)}, u32[]{:S(2)}) collective-permute-start(bf16[8,4224]{1,0:T(8,128)(2,1)S(1)} %get-tuple-element.27.refs_4_), channel_id=1, source_target_pairs={{0,4},{1,5},{2,6},{3,7},{4,0},{5,1},{6,2},{7,3},{8,12},{9,13},{10,... | collective-permute-start | bytes 202760 | tf_op jit(solution)/shard_map/ppermute | solution.py:402
  8.1 28.3 %collective-permute-start.10 = (bf16[128,4096]{1,0:T(8,128)(2,1)}, bf16[128,4096]{1,0:T(8,128)(2,1)S(1)}, u32[]{:S(2)}, u32[]{:S(2)}) collective-permute-start(bf16[128,4096]{1,0:T(8,128)(2,1)} %bitcast.27), channel_id=1, source_target_pairs={{8,0},{9,1},{10,2},{11,3},{12,4},{13,5},{14,6},{15,7},{16,8},{17,9... | collective-permute-start | bytes 3145736 | tf_op jit(solution)/shard_map/ppermute | solution.py:413
  10.8 7.9 %copy-start = (bf16[1,1,2,192,4096]{4,3,2,1,0:T(8,128)(2,1)S(1)}, bf16[1,1,2,192,4096]{4,3,2,1,0:T(8,128)(2,1)}, u32[]{:S(2)}) copy-start(bf16[1,1,2,192,4096]{4,3,2,1,0:T(8,128)(2,1)} %param.12) | copy-start | bytes 9437188
  10.8 7.9 %collective-permute-start.2 = (bf16[16,4224]{1,0:T(8,128)(2,1)S(1)}, bf16[16,4224]{1,0:T(8,128)(2,1)S(1)}, u32[]{:S(2)}, u32[]{:S(2)}) collective-permute-start(bf16[16,4224]{1,0:T(8,128)(2,1)S(1)} %shard_map.103), channel_id=1, source_target_pairs={{0,2},{1,3},{2,0},{3,1},{4,6},{5,7},{6,4},{7,5},{8,10},{9,11},{10,... | collective-permute-start | bytes 405512 | tf_op jit(solution)/shard_map/ppermute | solution.py:402
  12.4 6.2 %collective-permute-start.3 = (bf16[8,4224]{1,0:T(8,128)(2,1)S(1)}, bf16[8,4224]{1,0:T(8,128)(2,1)S(1)}, u32[]{:S(2)}, u32[]{:S(2)}) collective-permute-start(bf16[8,4224]{1,0:T(8,128)(2,1)S(1)} %collective-permute-done.refs_1_.far_in_ref), channel_id=1, source_target_pairs={{0,2},{1,3},{2,0},{3,1},{4,6},{5,7},{6,4},{7,5},{8,10},{9,11},{10,... | collective-permute-start | bytes 202760 | tf_op jit(solution)/shard_map/ppermute | solution.py:402
  14.8 5.8 %collective-permute-start.5 = (bf16[8,4224]{1,0:T(8,128)(2,1)S(1)}, bf16[8,4224]{1,0:T(8,128)(2,1)S(1)}, u32[]{:S(2)}, u32[]{:S(2)}) collective-permute-start(bf16[8,4224]{1,0:T(8,128)(2,1)S(1)} %collective-permute-done.4.after_ref.refs_5_.far_grad_ref), channel_id=1, source_target_pairs={{0,2},{1,3},{2,0},{3,1},{4,6},{5,7},{6,4},{7,5},{8,10},{9,11},{10,... | collective-permute-start | bytes 202760 | tf_op jit(solution)/shard_map/ppermute | solution.py:402
  15.5 5.1 %copy-start.4 = (bf16[1,1,192,4096]{3,2,1,0:T(8,128)(2,1)S(1)}, bf16[1,1,192,4096]{3,2,1,0:T(8,128)(2,1)}, u32[]{:S(2)}) copy-start(bf16[1,1,192,4096]{3,2,1,0:T(8,128)(2,1)} %param.13) | copy-start | bytes 4718596
  20.6 7.4 %copy-start.1 = (f32[1,4096]{1,0:T(1,128)S(1)}, f32[1,4096]{1,0:T(1,128)}, u32[]{:S(2)}) copy-start(f32[1,4096]{1,0:T(1,128)} %gain_ref.1) | copy-start | bytes 49156
  23.0 15.5 %copy-start.2 = (s32[1,128,8]{1,2,0:T(8,128)S(1)}, s32[1,128,8]{1,2,0:T(8,128)}, u32[]{:S(2)}) copy-start(s32[1,128,8]{1,2,0:T(8,128)} %param.9) | copy-start | bytes 12292
  23.0 5.1 %collective-permute-start.7 = (bf16[16,4224]{1,0:T(8,128)(2,1)S(1)}, bf16[16,4224]{1,0:T(8,128)(2,1)S(1)}, u32[]{:S(2)}, u32[]{:S(2)}) collective-permute-start(bf16[16,4224]{1,0:T(8,128)(2,1)S(1)} %get-tuple-element.31), channel_id=1, source_target_pairs={{0,2},{1,3},{2,0},{3,1},{4,6},{5,7},{6,4},{7,5},{8,10},{9,11},{10,... | collective-permute-start | bytes 405512 | tf_op jit(solution)/shard_map/ppermute | solution.py:402
  24.0 1.2 %collective-permute-start.15 = (bf16[32,640]{1,0:T(8,128)(2,1)S(1)}, bf16[32,640]{1,0:T(8,128)(2,1)S(1)}, u32[]{:S(2)}, u32[]{:S(2)}) collective-permute-start(bf16[32,640]{1,0:T(8,128)(2,1)S(1)} %get-tuple-element.40), channel_id=1, source_target_pairs={{0,1},{1,0},{2,3},{3,2},{4,5},{5,4},{6,7},{7,6},{8,9},{9,8},{10,11... | collective-permute-start | bytes 122888 | tf_op jit(solution)/shard_map/ppermute | solution.py:405
  24.0 4.3 %collective-permute-start.13 = (bf16[16,4096]{1,0:T(8,128)(2,1)S(1)}, bf16[16,4096]{1,0:T(8,128)(2,1)S(1)}, u32[]{:S(2)}, u32[]{:S(2)}) collective-permute-start(bf16[16,4096]{1,0:T(8,128)(2,1)S(1)} %get-tuple-element.37.refs_4_), channel_id=1, source_target_pairs={{0,1},{1,0},{2,3},{3,2},{4,5},{5,4},{6,7},{7,6},{8,9},{9,8},{10,11... | collective-permute-start | bytes 393224 | tf_op jit(solution)/shard_map/ppermute | solution.py:405
  24.5 7.8 %collective-permute-start.14 = (bf16[16,4096]{1,0:T(8,128)(2,1)S(1)}, bf16[16,4096]{1,0:T(8,128)(2,1)S(1)}, u32[]{:S(2)}, u32[]{:S(2)}) collective-permute-start(bf16[16,4096]{1,0:T(8,128)(2,1)S(1)} %get-tuple-element.38.refs_5_), channel_id=1, source_target_pairs={{0,1},{1,0},{2,3},{3,2},{4,5},{5,4},{6,7},{7,6},{8,9},{9,8},{10,11... | collective-permute-start | bytes 393224 | tf_op jit(solution)/shard_map/ppermute | solution.py:405
  25.2 8.4 %collective-permute-start.11 = (bf16[16,4096]{1,0:T(8,128)(2,1)S(1)}, bf16[16,4096]{1,0:T(8,128)(2,1)S(1)}, u32[]{:S(2)}, u32[]{:S(2)}) collective-permute-start(bf16[16,4096]{1,0:T(8,128)(2,1)S(1)} %get-tuple-element.35.refs_0_), channel_id=1, source_target_pairs={{0,1},{1,0},{2,3},{3,2},{4,5},{5,4},{6,7},{7,6},{8,9},{9,8},{10,11... | collective-permute-start | bytes 393224 | tf_op jit(solution)/shard_map/ppermute | solution.py:405
  28.0 5.6 %collective-permute-start.12 = (bf16[16,4096]{1,0:T(8,128)(2,1)S(1)}, bf16[16,4096]{1,0:T(8,128)(2,1)S(1)}, u32[]{:S(2)}, u32[]{:S(2)}) collective-permute-start(bf16[16,4096]{1,0:T(8,128)(2,1)S(1)} %get-tuple-element.36.refs_1_), channel_id=1, source_target_pairs={{0,1},{1,0},{2,3},{3,2},{4,5},{5,4},{6,7},{7,6},{8,9},{9,8},{10,11... | collective-permute-start | bytes 393224 | tf_op jit(solution)/shard_map/ppermute | solution.py:405
  28.3 8.7 %collective-permute-start.8 = (bf16[8,4224]{1,0:T(8,128)(2,1)S(1)}, bf16[8,4224]{1,0:T(8,128)(2,1)S(1)}, u32[]{:S(2)}, u32[]{:S(2)}) collective-permute-start(bf16[8,4224]{1,0:T(8,128)(2,1)S(1)} %get-tuple-element.33), channel_id=1, source_target_pairs={{8,4},{9,5},{10,6},{11,7},{12,0},{13,1},{14,2},{15,3},{16,12},{17,... | collective-permute-start | bytes 202760 | tf_op jit(solution)/shard_map/ppermute | solution.py:413
  32.3 4.6 %collective-permute-start.9 = (bf16[8,4096]{1,0:T(8,128)(2,1)S(1)}, bf16[8,4096]{1,0:T(8,128)(2,1)S(1)}, u32[]{:S(2)}, u32[]{:S(2)}) collective-permute-start(bf16[8,4096]{1,0:T(8,128)(2,1)S(1)} %get-tuple-element.34.refs_10_), channel_id=1, source_target_pairs={{8,0},{9,1},{10,2},{11,3},{12,4},{13,5},{14,6},{15,7},{16,8},{17,9... | collective-permute-start | bytes 196616 | tf_op jit(solution)/shard_map/ppermute | solution.py:413
  33.6 4.8 %collective-permute-start.16 = (f32[8,128]{1,0:T(8,128)S(1)}, f32[8,128]{1,0:T(8,128)S(1)}, u32[]{:S(2)}, u32[]{:S(2)}) collective-permute-start(f32[8,128]{1,0:T(8,128)S(1)} %get-tuple-element.44), channel_id=1, source_target_pairs={{0,4},{1,5},{2,6},{3,7},{4,0},{5,1},{6,2},{7,3},{8,12},{9,13},{10,... | collective-permute-start | bytes 12296 | tf_op jit(solution)/shard_map/ppermute | solution.py:402

commit v10 on v8

--- a/solution.py
+++ b/solution.py
@@ -345,7 +345,7 @@
 
 
 def weight_grads(blocks, keep, got, after, hidden, width):
-    chunks = 4
+    chunks = 8
     return pl.pallas_call(
         functools.partial(weights_kernel, chunks),
         in_specs=[IN_VMEM] * (len(blocks) + 2) + [pl.BlockSpec(memory_space=pl.ANY)],

time: 38.7 us -> 38.7 us (level)
  no operation moved by 1% of the time
where the time goes in v10:
time: 38.7 us; the launch traced here: 38.5 us
  starting transfers between devices  18.5 us (48%)
  Pallas kernels  11.2 us (29%)
  waiting for transfers between devices  8.12 us (21%)
  between operations  0.74 us (2%)
    ppermute x7, starting transfers between devices, across(): lax.ppermute(block, 'expert', [(i, i ^ 2 * offset) for i in range(devices)])  9.12 us
    ppermute x3, starting transfers between devices, handed(): return lax.ppermute(block, ('pipe', 'expert'), route)  8.05 us
    ppermute x7, waiting for transfers between devices, across(): lax.ppermute(block, 'expert', [(i, i ^ 2 * offset) for i in range(devices)])  6.61 us
    pallas_call x1, Pallas kernels, weight_grads(): pl.pallas_call(functools.partial(weights_kernel, chunks), in_specs=[IN_VM...  2.62 us
    pallas_call x1, Pallas kernels, on_one(): call(hidden_kernel, [((2 * cap, wide), BF16)] * 2 + [half_rows] * 2 + [((...  2.32 us
    pallas_call x1, Pallas kernels, on_one(): call(rows_kernel, [((cap, wide), BF16)] * 2 + [((2 * cap, wide), BF16), (...  2 us
    pallas_call x1, Pallas kernels, on_one(): call(project_kernel, [((total_rows // 2, 2 * hidden), F32)] * 2 + [half_r...  1.93 us
    pallas_call x1, Pallas kernels, on_one(): call(finish_kernel, [((tokens, width), BF16)], 4 * tokens * width * cap,...  1.51 us
  transfers between devices with their start and end apart: 17, of which 5 were waited for; matrix products, arithmetic and copies ran while one was open for 0% of the time, Pallas kernels for 28%

profile of v10, /device:TPU:0, one launch (start us, length us, event | category | flops | bytes accessed | tf_op | source)
XLA Modules:
  0.0 38.5 jit_solution(6545940788008415207)
XLA Ops:
  0.6 0.5 %collective-permute-start.1 = (bf16[384,4096]{1,0:T(8,128)(2,1)}, bf16[384,4096]{1,0:T(8,128)(2,1)S(1)}, u32[]{:S(2)}, u32[]{:S(2)}) collective-permute-start(bf16[384,4096]{1,0:T(8,128)(2,1)} %bitcast.16), channel_id=1, source_target_pairs={{0,1},{1,0},{2,3},{3,2},{4,5},{5,4},{6,7},{7,6},{8,9},{9,8},{10,11... | collective-permute-start | bytes 9437192 | tf_op jit(solution)/shard_map/ppermute | solution.py:407
  1.1 0.1 collective-permute-start.6
  1.2 2.0 %shard_map.102 = (bf16[8,4224]{1,0:T(8,128)(2,1)S(1)}, bf16[8,4224]{1,0:T(8,128)(2,1)S(1)}, bf16[16,4224]{1,0:T(8,128)(2,1)S(1)}, f32[8,4096]{1,0:T(8,128)S(1)}, f32[8,128]{1,0:T(8,128)S(1)}) custom-call(s32[8,128]{1,0:T(8,128)} %bitcast.19, bf16[8,128]{1,0:T(8,128)(2,1)} %bitcast.28, f32[1,4096]{1,0:T(1,128)} %gain_ref.1, bf16[128,4096]{1,0:T(8,128)(2,1)} %bitcast.24, ...), custom_call_target="tpu_custom_call" | custom-call | flops 16777216 | bytes 2097152 | tf_op jit(solution)/shard_map/pallas_call | solution.py:418
  3.2 4.1 %collective-permute-start = (bf16[8,4224]{1,0:T(8,128)(2,1)S(1)}, bf16[8,4224]{1,0:T(8,128)(2,1)S(1)}, u32[]{:S(2)}, u32[]{:S(2)}) collective-permute-start(bf16[8,4224]{1,0:T(8,128)(2,1)S(1)} %get-tuple-element.25.refs_0_.in_ref), channel_id=1, source_target_pairs={{0,4},{1,5},{2,6},{3,7},{4,0},{5,1},{6,2},{7,3},{8,12},{9,13},{10,... | collective-permute-start | bytes 202760 | tf_op jit(solution)/shard_map/ppermute | solution.py:404
  7.3 0.1 collective-permute-start.4
  7.4 2.7 %collective-permute-start.10 = (bf16[128,4096]{1,0:T(8,128)(2,1)}, bf16[128,4096]{1,0:T(8,128)(2,1)S(1)}, u32[]{:S(2)}, u32[]{:S(2)}) collective-permute-start(bf16[128,4096]{1,0:T(8,128)(2,1)} %bitcast.26), channel_id=1, source_target_pairs={{8,0},{9,1},{10,2},{11,3},{12,4},{13,5},{14,6},{15,7},{16,8},{17,9... | collective-permute-start | bytes 3145736 | tf_op jit(solution)/shard_map/ppermute | solution.py:415
  10.1 1.6 %collective-permute-start.2 = (bf16[16,4224]{1,0:T(8,128)(2,1)S(1)}, bf16[16,4224]{1,0:T(8,128)(2,1)S(1)}, u32[]{:S(2)}, u32[]{:S(2)}) collective-permute-start(bf16[16,4224]{1,0:T(8,128)(2,1)S(1)} %shard_map.103), channel_id=1, source_target_pairs={{0,2},{1,3},{2,0},{3,1},{4,6},{5,7},{6,4},{7,5},{8,10},{9,11},{10,... | collective-permute-start | bytes 405512 | tf_op jit(solution)/shard_map/ppermute | solution.py:404
  11.8 1.6 %collective-permute-start.3 = (bf16[8,4224]{1,0:T(8,128)(2,1)S(1)}, bf16[8,4224]{1,0:T(8,128)(2,1)S(1)}, u32[]{:S(2)}, u32[]{:S(2)}) collective-permute-start(bf16[8,4224]{1,0:T(8,128)(2,1)S(1)} %collective-permute-done.refs_1_.far_in_ref), channel_id=1, source_target_pairs={{0,2},{1,3},{2,0},{3,1},{4,6},{5,7},{6,4},{7,5},{8,10},{9,11},{10,... | collective-permute-start | bytes 202760 | tf_op jit(solution)/shard_map/ppermute | solution.py:404
  13.4 0.7 %collective-permute-done.4.after_ref.refs_5_.far_grad_ref = bf16[8,4224]{1,0:T(8,128)(2,1)S(1)} collective-permute-done((bf16[8,4224]{1,0:T(8,128)(2,1)S(1)}, bf16[8,4224]{1,0:T(8,128)(2,1)S(1)}, u32[]{:S(2)}, u32[]{:S(2)}) %collective-permute-start.4) | collective-permute-done | bytes 67616 | tf_op jit(solution)/shard_map/ppermute | solution.py:404
  14.1 0.7 %collective-permute-start.5 = (bf16[8,4224]{1,0:T(8,128)(2,1)S(1)}, bf16[8,4224]{1,0:T(8,128)(2,1)S(1)}, u32[]{:S(2)}, u32[]{:S(2)}) collective-permute-start(bf16[8,4224]{1,0:T(8,128)(2,1)S(1)} %collective-permute-done.4.after_ref.refs_5_.far_grad_ref), channel_id=1, source_target_pairs={{0,2},{1,3},{2,0},{3,1},{4,6},{5,7},{6,4},{7,5},{8,10},{9,11},{10,... | collective-permute-start | bytes 202760 | tf_op jit(solution)/shard_map/ppermute | solution.py:404
  14.8 3.2 %collective-permute-done.3.refs_3_ = bf16[8,4224]{1,0:T(8,128)(2,1)S(1)} collective-permute-done((bf16[8,4224]{1,0:T(8,128)(2,1)S(1)}, bf16[8,4224]{1,0:T(8,128)(2,1)S(1)}, u32[]{:S(2)}, u32[]{:S(2)}) %collective-permute-start.3) | collective-permute-done | bytes 67616 | tf_op jit(solution)/shard_map/ppermute | solution.py:404
  18.0 0.0 collective-permute-done.2.refs_2_.refs_6_
  18.0 1.9 %shard_map.105 = (f32[32,384]{1,0:T(8,128)S(1)}, f32[32,384]{1,0:T(8,128)S(1)}, bf16[16,4096]{1,0:T(8,128)(2,1)S(1)}, bf16[16,4096]{1,0:T(8,128)(2,1)S(1)}) custom-call(bf16[8,4224]{1,0:T(8,128)(2,1)S(1)} %get-tuple-element.25.refs_0_.in_ref, bf16[8,4224]{1,0:T(8,128)(2,1)S(1)} %collective-permute-done.refs_1_.far_in_ref, ...), custom_call_target="tpu_custom_call" | custom-call | bytes 3145728 | tf_op jit(solution)/shard_map/pallas_call | solution.py:457
  19.9 0.0 collective-permute-done.5.refs_7_
  19.9 0.0 collective-permute-done.6.refs_13_
  20.0 0.0 copy-start.1
  20.0 2.3 %shard_map.106 = (bf16[16,4224]{1,0:T(8,128)(2,1)S(1)}, bf16[16,4224]{1,0:T(8,128)(2,1)S(1)}, bf16[16,4096]{1,0:T(8,128)(2,1)S(1)}, bf16[16,4096]{1,0:T(8,128)(2...) custom-call(bf16[8,4224]{1,0:T(8,128)(2,1)S(1)} %get-tuple-element.25.refs_0_.in_ref, ...), custom_call_target="tpu_custom_call" | custom-call | flops 6400000000 | bytes 4718592 | tf_op jit(solution)/shard_map/pallas_call | solution.py:464
  22.3 0.0 copy-start.2
  22.3 1.0 %collective-permute-start.7 = (bf16[16,4224]{1,0:T(8,128)(2,1)S(1)}, bf16[16,4224]{1,0:T(8,128)(2,1)S(1)}, u32[]{:S(2)}, u32[]{:S(2)}) collective-permute-start(bf16[16,4224]{1,0:T(8,128)(2,1)S(1)} %get-tuple-element.31), channel_id=1, source_target_pairs={{0,2},{1,3},{2,0},{3,1},{4,6},{5,7},{6,4},{7,5},{8,10},{9,11},{10,... | collective-permute-start | bytes 405512 | tf_op jit(solution)/shard_map/ppermute | solution.py:404
  23.3 0.0 collective-permute-start.15
  23.3 0.5 %collective-permute-start.13 = (bf16[16,4096]{1,0:T(8,128)(2,1)S(1)}, bf16[16,4096]{1,0:T(8,128)(2,1)S(1)}, u32[]{:S(2)}, u32[]{:S(2)}) collective-permute-start(bf16[16,4096]{1,0:T(8,128)(2,1)S(1)} %get-tuple-element.37.refs_4_), channel_id=1, source_target_pairs={{0,1},{1,0},{2,3},{3,2},{4,5},{5,4},{6,7},{7,6},{8,9},{9,8},{10,11... | collective-permute-start | bytes 393224 | tf_op jit(solution)/shard_map/ppermute | solution.py:407
  23.8 0.7 %collective-permute-done.15.refs_9_ = bf16[32,640]{1,0:T(8,128)(2,1)S(1)} collective-permute-done((bf16[32,640]{1,0:T(8,128)(2,1)S(1)}, bf16[32,640]{1,0:T(8,128)(2,1)S(1)}, u32[]{:S(2)}, u32[]{:S(2)}) %collective-permute-start.15) | collective-permute-done | bytes 40992 | tf_op jit(solution)/shard_map/ppermute | solution.py:407
  24.6 0.2 collective-permute-start.11
  24.7 2.7 %collective-permute-done.7.got_ref = bf16[16,4224]{1,0:T(8,128)(2,1)S(1)} collective-permute-done((bf16[16,4224]{1,0:T(8,128)(2,1)S(1)}, bf16[16,4224]{1,0:T(8,128)(2,1)S(1)}, u32[]{:S(2)}, u32[]{:S(2)}) %collective-permute-start.7) | collective-permute-done | bytes 135200 | tf_op jit(solution)/shard_map/ppermute | solution.py:404
  27.4 0.0 collective-permute-start.12
  27.4 0.2 shard_map.107
  27.6 4.5 %collective-permute-start.8 = (bf16[8,4224]{1,0:T(8,128)(2,1)S(1)}, bf16[8,4224]{1,0:T(8,128)(2,1)S(1)}, u32[]{:S(2)}, u32[]{:S(2)}) collective-permute-start(bf16[8,4224]{1,0:T(8,128)(2,1)S(1)} %get-tuple-element.33), channel_id=1, source_target_pairs={{8,4},{9,5},{10,6},{11,7},{12,0},{13,1},{14,2},{15,3},{16,12},{17,... | collective-permute-start | bytes 202760 | tf_op jit(solution)/shard_map/ppermute | solution.py:415
  32.1 0.8 %collective-permute-start.9 = (bf16[8,4096]{1,0:T(8,128)(2,1)S(1)}, bf16[8,4096]{1,0:T(8,128)(2,1)S(1)}, u32[]{:S(2)}, u32[]{:S(2)}) collective-permute-start(bf16[8,4096]{1,0:T(8,128)(2,1)S(1)} %get-tuple-element.34.refs_10_), channel_id=1, source_target_pairs={{8,0},{9,1},{10,2},{11,3},{12,4},{13,5},{14,6},{15,7},{16,8},{17,9... | collective-permute-start | bytes 196616 | tf_op jit(solution)/shard_map/ppermute | solution.py:415
  33.0 2.6 %shard_map.109 = (bf16[384,4096]{1,0:T(8,128)(2,1)}, bf16[192,4096]{1,0:T(8,128)(2,1)}) custom-call(bf16[16,4096]{1,0:T(8,128)(2,1)S(1)} %get-tuple-element.35.refs_0_, bf16[16,4096]{1,0:T(8,128)(2,1)S(1)} %get-tuple-element.36.refs_1_, bf16[16,4096]{1,0:T(8,128)(2,1)S(1)} %collective-permute-done.11.refs_2_, ...), custom_call_target="tpu_custom_call" | custom-call | flops 301989888 | bytes 4718592 | tf_op jit(solution)/shard_map/pallas_call | solution.py:349
  35.6 0.8 %collective-permute-done.9.own_ref = bf16[8,4096]{1,0:T(8,128)(2,1)S(1)} collective-permute-done((bf16[8,4096]{1,0:T(8,128)(2,1)S(1)}, bf16[8,4096]{1,0:T(8,128)(2,1)S(1)}, u32[]{:S(2)}, u32[]{:S(2)}) %collective-permute-start.9) | collective-permute-done | bytes 65568 | tf_op jit(solution)/shard_map/ppermute | solution.py:415
  36.4 1.5 %shard_map.108.after_ref = bf16[128,4096]{1,0:T(8,128)(2,1)} custom-call(bf16[8,4224]{1,0:T(8,128)(2,1)S(1)} %collective-permute-done.8.other_ref, bf16[8,4096]{1,0:T(8,128)(2,1)S(1)} %collective-permute-done.9.own_ref, bf16[128,4096]{1,0:T(8,128)(2,1)S(1)} %collective-permute-done.10.grad_ref), custom_call_target="tpu_custom_call" | custom-call | flops 16777216 | bytes 2097152 | tf_op jit(solution)/shard_map/pallas_call | solution.py:482
  37.9 0.6 %shard_map.110 = f32[8,128]{1,0:T(8,128)} custom-call(f32[8,128]{1,0:T(8,128)S(1)} %get-tuple-element.43.own_comb_ref, f32[8,128]{1,0:T(8,128)S(1)} %collective-permute-done.16.other_comb_ref, s32[8,128]{1,0:T(8,128)S(1)} %bitcast.20, f32[8,128]{1,0:T(8,128)S(1)} %get-tuple-element.45.place_ref, bf16[128,4096]{1,0:T(8,128)(2,1)} %shard_map.108.after_ref), custom_call_target="tpu_custom_call" | custom-call | bytes 4096 | tf_op jit(solution)/shard_map/pallas_call | solution.py:485
  (19 shorter events, 0.1 us)
Async XLA Ops:
  0.6 9.5 %collective-permute-start.1 = (bf16[384,4096]{1,0:T(8,128)(2,1)}, bf16[384,4096]{1,0:T(8,128)(2,1)S(1)}, u32[]{:S(2)}, u32[]{:S(2)}) collective-permute-start(bf16[384,4096]{1,0:T(8,128)(2,1)} %bitcast.16), channel_id=1, source_target_pairs={{0,1},{1,0},{2,3},{3,2},{4,5},{5,4},{6,7},{7,6},{8,9},{9,8},{10,11... | collective-permute-start | bytes 9437192 | tf_op jit(solution)/shard_map/ppermute | solution.py:407
  1.1 18.8 %collective-permute-start.6 = (bf16[192,4096]{1,0:T(8,128)(2,1)}, bf16[192,4096]{1,0:T(8,128)(2,1)S(1)}, u32[]{:S(2)}, u32[]{:S(2)}) collective-permute-start(bf16[192,4096]{1,0:T(8,128)(2,1)} %bitcast.21), channel_id=1, source_target_pairs={{0,1},{1,0},{2,3},{3,2},{4,5},{5,4},{6,7},{7,6},{8,9},{9,8},{10,11... | collective-permute-start | bytes 4718600 | tf_op jit(solution)/shard_map/ppermute | solution.py:407
  3.2 8.5 %collective-permute-start = (bf16[8,4224]{1,0:T(8,128)(2,1)S(1)}, bf16[8,4224]{1,0:T(8,128)(2,1)S(1)}, u32[]{:S(2)}, u32[]{:S(2)}) collective-permute-start(bf16[8,4224]{1,0:T(8,128)(2,1)S(1)} %get-tuple-element.25.refs_0_.in_ref), channel_id=1, source_target_pairs={{0,4},{1,5},{2,6},{3,7},{4,0},{5,1},{6,2},{7,3},{8,12},{9,13},{10,... | collective-permute-start | bytes 202760 | tf_op jit(solution)/shard_map/ppermute | solution.py:404
  7.3 6.8 %collective-permute-start.4 = (bf16[8,4224]{1,0:T(8,128)(2,1)S(1)}, bf16[8,4224]{1,0:T(8,128)(2,1)S(1)}, u32[]{:S(2)}, u32[]{:S(2)}) collective-permute-start(bf16[8,4224]{1,0:T(8,128)(2,1)S(1)} %get-tuple-element.27.refs_4_), channel_id=1, source_target_pairs={{0,4},{1,5},{2,6},{3,7},{4,0},{5,1},{6,2},{7,3},{8,12},{9,13},{10,... | collective-permute-start | bytes 202760 | tf_op jit(solution)/shard_map/ppermute | solution.py:404
  7.4 28.2 %collective-permute-start.10 = (bf16[128,4096]{1,0:T(8,128)(2,1)}, bf16[128,4096]{1,0:T(8,128)(2,1)S(1)}, u32[]{:S(2)}, u32[]{:S(2)}) collective-permute-start(bf16[128,4096]{1,0:T(8,128)(2,1)} %bitcast.26), channel_id=1, source_target_pairs={{8,0},{9,1},{10,2},{11,3},{12,4},{13,5},{14,6},{15,7},{16,8},{17,9... | collective-permute-start | bytes 3145736 | tf_op jit(solution)/shard_map/ppermute | solution.py:415
  10.1 7.9 %copy-start = (bf16[1,1,2,192,4096]{4,3,2,1,0:T(8,128)(2,1)S(1)}, bf16[1,1,2,192,4096]{4,3,2,1,0:T(8,128)(2,1)}, u32[]{:S(2)}) copy-start(bf16[1,1,2,192,4096]{4,3,2,1,0:T(8,128)(2,1)} %param.12) | copy-start | bytes 9437188
  10.1 7.9 %collective-permute-start.2 = (bf16[16,4224]{1,0:T(8,128)(2,1)S(1)}, bf16[16,4224]{1,0:T(8,128)(2,1)S(1)}, u32[]{:S(2)}, u32[]{:S(2)}) collective-permute-start(bf16[16,4224]{1,0:T(8,128)(2,1)S(1)} %shard_map.103), channel_id=1, source_target_pairs={{0,2},{1,3},{2,0},{3,1},{4,6},{5,7},{6,4},{7,5},{8,10},{9,11},{10,... | collective-permute-start | bytes 405512 | tf_op jit(solution)/shard_map/ppermute | solution.py:404
  11.8 6.2 %collective-permute-start.3 = (bf16[8,4224]{1,0:T(8,128)(2,1)S(1)}, bf16[8,4224]{1,0:T(8,128)(2,1)S(1)}, u32[]{:S(2)}, u32[]{:S(2)}) collective-permute-start(bf16[8,4224]{1,0:T(8,128)(2,1)S(1)} %collective-permute-done.refs_1_.far_in_ref), channel_id=1, source_target_pairs={{0,2},{1,3},{2,0},{3,1},{4,6},{5,7},{6,4},{7,5},{8,10},{9,11},{10,... | collective-permute-start | bytes 202760 | tf_op jit(solution)/shard_map/ppermute | solution.py:404
  14.1 5.8 %collective-permute-start.5 = (bf16[8,4224]{1,0:T(8,128)(2,1)S(1)}, bf16[8,4224]{1,0:T(8,128)(2,1)S(1)}, u32[]{:S(2)}, u32[]{:S(2)}) collective-permute-start(bf16[8,4224]{1,0:T(8,128)(2,1)S(1)} %collective-permute-done.4.after_ref.refs_5_.far_grad_ref), channel_id=1, source_target_pairs={{0,2},{1,3},{2,0},{3,1},{4,6},{5,7},{6,4},{7,5},{8,10},{9,11},{10,... | collective-permute-start | bytes 202760 | tf_op jit(solution)/shard_map/ppermute | solution.py:404
  14.8 5.1 %copy-start.3 = (bf16[1,1,192,4096]{3,2,1,0:T(8,128)(2,1)S(1)}, bf16[1,1,192,4096]{3,2,1,0:T(8,128)(2,1)}, u32[]{:S(2)}) copy-start(bf16[1,1,192,4096]{3,2,1,0:T(8,128)(2,1)} %param.13) | copy-start | bytes 4718596
  20.0 7.4 %copy-start.1 = (f32[1,4096]{1,0:T(1,128)S(1)}, f32[1,4096]{1,0:T(1,128)}, u32[]{:S(2)}) copy-start(f32[1,4096]{1,0:T(1,128)} %gain_ref.1) | copy-start | bytes 49156
  22.3 15.6 %copy-start.2 = (s32[1,128,8]{1,2,0:T(8,128)S(1)}, s32[1,128,8]{1,2,0:T(8,128)}, u32[]{:S(2)}) copy-start(s32[1,128,8]{1,2,0:T(8,128)} %param.9) | copy-start | bytes 12292
  22.3 5.1 %collective-permute-start.7 = (bf16[16,4224]{1,0:T(8,128)(2,1)S(1)}, bf16[16,4224]{1,0:T(8,128)(2,1)S(1)}, u32[]{:S(2)}, u32[]{:S(2)}) collective-permute-start(bf16[16,4224]{1,0:T(8,128)(2,1)S(1)} %get-tuple-element.31), channel_id=1, source_target_pairs={{0,2},{1,3},{2,0},{3,1},{4,6},{5,7},{6,4},{7,5},{8,10},{9,11},{10,... | collective-permute-start | bytes 405512 | tf_op jit(solution)/shard_map/ppermute | solution.py:404
  23.3 1.2 %collective-permute-start.15 = (bf16[32,640]{1,0:T(8,128)(2,1)S(1)}, bf16[32,640]{1,0:T(8,128)(2,1)S(1)}, u32[]{:S(2)}, u32[]{:S(2)}) collective-permute-start(bf16[32,640]{1,0:T(8,128)(2,1)S(1)} %get-tuple-element.40), channel_id=1, source_target_pairs={{0,1},{1,0},{2,3},{3,2},{4,5},{5,4},{6,7},{7,6},{8,9},{9,8},{10,11... | collective-permute-start | bytes 122888 | tf_op jit(solution)/shard_map/ppermute | solution.py:407
  23.3 4.3 %collective-permute-start.13 = (bf16[16,4096]{1,0:T(8,128)(2,1)S(1)}, bf16[16,4096]{1,0:T(8,128)(2,1)S(1)}, u32[]{:S(2)}, u32[]{:S(2)}) collective-permute-start(bf16[16,4096]{1,0:T(8,128)(2,1)S(1)} %get-tuple-element.37.refs_4_), channel_id=1, source_target_pairs={{0,1},{1,0},{2,3},{3,2},{4,5},{5,4},{6,7},{7,6},{8,9},{9,8},{10,11... | collective-permute-start | bytes 393224 | tf_op jit(solution)/shard_map/ppermute | solution.py:407
  23.8 8.3 %collective-permute-start.14 = (bf16[16,4096]{1,0:T(8,128)(2,1)S(1)}, bf16[16,4096]{1,0:T(8,128)(2,1)S(1)}, u32[]{:S(2)}, u32[]{:S(2)}) collective-permute-start(bf16[16,4096]{1,0:T(8,128)(2,1)S(1)} %get-tuple-element.38.refs_5_), channel_id=1, source_target_pairs={{0,1},{1,0},{2,3},{3,2},{4,5},{5,4},{6,7},{7,6},{8,9},{9,8},{10,11... | collective-permute-start | bytes 393224 | tf_op jit(solution)/shard_map/ppermute | solution.py:407
  24.6 8.4 %collective-permute-start.11 = (bf16[16,4096]{1,0:T(8,128)(2,1)S(1)}, bf16[16,4096]{1,0:T(8,128)(2,1)S(1)}, u32[]{:S(2)}, u32[]{:S(2)}) collective-permute-start(bf16[16,4096]{1,0:T(8,128)(2,1)S(1)} %get-tuple-element.35.refs_0_), channel_id=1, source_target_pairs={{0,1},{1,0},{2,3},{3,2},{4,5},{5,4},{6,7},{7,6},{8,9},{9,8},{10,11... | collective-permute-start | bytes 393224 | tf_op jit(solution)/shard_map/ppermute | solution.py:407
  27.4 5.6 %collective-permute-start.12 = (bf16[16,4096]{1,0:T(8,128)(2,1)S(1)}, bf16[16,4096]{1,0:T(8,128)(2,1)S(1)}, u32[]{:S(2)}, u32[]{:S(2)}) collective-permute-start(bf16[16,4096]{1,0:T(8,128)(2,1)S(1)} %get-tuple-element.36.refs_1_), channel_id=1, source_target_pairs={{0,1},{1,0},{2,3},{3,2},{4,5},{5,4},{6,7},{7,6},{8,9},{9,8},{10,11... | collective-permute-start | bytes 393224 | tf_op jit(solution)/shard_map/ppermute | solution.py:407
  27.6 8.8 %collective-permute-start.8 = (bf16[8,4224]{1,0:T(8,128)(2,1)S(1)}, bf16[8,4224]{1,0:T(8,128)(2,1)S(1)}, u32[]{:S(2)}, u32[]{:S(2)}) collective-permute-start(bf16[8,4224]{1,0:T(8,128)(2,1)S(1)} %get-tuple-element.33), channel_id=1, source_target_pairs={{8,4},{9,5},{10,6},{11,7},{12,0},{13,1},{14,2},{15,3},{16,12},{17,... | collective-permute-start | bytes 202760 | tf_op jit(solution)/shard_map/ppermute | solution.py:415
  32.1 4.3 %collective-permute-start.9 = (bf16[8,4096]{1,0:T(8,128)(2,1)S(1)}, bf16[8,4096]{1,0:T(8,128)(2,1)S(1)}, u32[]{:S(2)}, u32[]{:S(2)}) collective-permute-start(bf16[8,4096]{1,0:T(8,128)(2,1)S(1)} %get-tuple-element.34.refs_10_), channel_id=1, source_target_pairs={{8,0},{9,1},{10,2},{11,3},{12,4},{13,5},{14,6},{15,7},{16,8},{17,9... | collective-permute-start | bytes 196616 | tf_op jit(solution)/shard_map/ppermute | solution.py:415
  33.0 5.0 %collective-permute-start.16 = (f32[8,128]{1,0:T(8,128)S(1)}, f32[8,128]{1,0:T(8,128)S(1)}, u32[]{:S(2)}, u32[]{:S(2)}) collective-permute-start(f32[8,128]{1,0:T(8,128)S(1)} %get-tuple-element.44), channel_id=1, source_target_pairs={{0,4},{1,5},{2,6},{3,7},{4,0},{5,1},{6,2},{7,3},{8,12},{9,13},{10,... | collective-permute-start | bytes 12296 | tf_op jit(solution)/shard_map/ppermute | solution.py:404
